TPU v7x, 256 devices: a whole 4x4x8 slice. The times are simulated.
256 devices in a mesh: seq: 32 (over x, z), fsdp: 8 (over y, core).
Axes of the slice: x: 4, y: 4, z: 8, core: 2. Of those that a mesh axis runs over, the one named last changes fastest.
Arguments:
- byte_states: bfloat16 [8, 16384, 1024], P('fsdp', 'seq'), may hold values from -6 to 6
- group_states: bfloat16 [8, 4096, 1024], P('fsdp', 'seq'), may hold values from -6 to 6
- boundaries: int32 [8, 4096], P('fsdp'), may hold values from 0 to 16383, as said below
- w_query: bfloat16 [1024, 1024], P('fsdp'), may hold values from -0.1875 to 0.1875
- w_key: bfloat16 [1024, 1024], P('fsdp'), may hold values from -0.1875 to 0.1875
- w_value: bfloat16 [1024, 1024], P('fsdp'), may hold values from -0.1875 to 0.1875
- w_out: bfloat16 [1024, 1024], P('fsdp'), may hold values from -0.75 to 0.75
Outputs:
- dechunked: bfloat16 [8, 16384, 1024], P('fsdp', 'seq')
- attended: bfloat16 [8, 16384, 1024], P('fsdp', 'seq')
Inputs may be any that keep to these rules, and one draw needn't show every extreme that they name: Each boundaries[i] rises strictly and starts at 0. Device j along seq holds bytes j * 512 to (j + 1) * 512 - 1 and groups j * 128 to (j + 1) * 128 - 1; the bytes of device j lie in groups j * 128 - 64 to (j + 1) * 128 - 1, for j > 0 the first of them is below j * 128, and in every document some device's first is exactly j * 128 - 64.
All inputs are finite; a program needn't handle non-finite values.
Results may differ from a plain program's by a relative error of at most 0.022.
Values may be sent and summed in bfloat16 or wider, within the bound.
No kernel may reach another device: no remote copies, remote signals or barrier semaphores. Data moves between devices by JAX's collectives and lax.ppermute only.
A program may use at most 128 MiB of HBM per device.

v0:
```python
import jax
import jax.numpy as jnp
from jax import lax
from jax.sharding import PartitionSpec as P

HEAD_DIM = 64
W = 2048
TAIL = 64
DEPTH = 4
QB = 512


score_scale = 16.0
norm_eps = 1e-06


def shortened(x):
    return jax.tree.map(lambda a: a.astype(jnp.bfloat16) if a.dtype == jnp.float32 else a, x)


def shifted(block, axis, distance):
    devices = range(lax.axis_size(axis))
    route = [(i - distance, i) for i in devices if i - distance in devices]
    return lax.ppermute(block, axis, route)


def head_norm(matrix, factor):
    row_count = matrix.shape[0]
    per_head = matrix.reshape(row_count, matrix.shape[1] // HEAD_DIM, HEAD_DIM)
    mean_square = jnp.mean(per_head * per_head, axis=-1, keepdims=True)
    return (per_head * lax.rsqrt(mean_square + norm_eps) * factor).reshape(matrix.shape)


def contract(source, piece_rows):
    return jnp.dot(source, piece_rows, preferred_element_type=jnp.float32)


def reach_back(payload):
    tail_rows = tuple((member for member in payload))
    received = []
    for hop_index in range(DEPTH):
        received.append(
            jax.tree.map(
                lambda part, own: part.astype(own.dtype),
                shifted(shortened(tail_rows), "seq", hop_index + 1),
                tail_rows,
            )
        )
    return tuple(
        (
            jnp.concatenate(
                [received[DEPTH - 1 - hop_index][member] for hop_index in range(DEPTH)], axis=0
            )
            for member in range(len(payload))
        )
    )


def attend(query_hat, key_hat, value_all, base_position):
    row_count, width = query_hat.shape
    pair_width = 2 * HEAD_DIM
    pair_count = width // pair_width

    def one_block(block_start):
        offset = jnp.arange(QB, dtype=jnp.int32)[:, None]
        key_index = jnp.arange(W + QB, dtype=jnp.int32)[None, :]
        allowed = (
            (key_index >= offset)
            & (key_index <= offset + W)
            & (base_position + block_start + key_index >= 0)
        )

        def one_pair(pair_index, output):
            column = pair_index * pair_width
            query_part = lax.dynamic_slice_in_dim(query_hat, column, pair_width, 1).reshape(
                QB, 2, HEAD_DIM
            )
            key_part = lax.dynamic_slice_in_dim(key_hat, column, pair_width, 1).reshape(
                W + QB, 2, HEAD_DIM
            )
            value_part = lax.dynamic_slice_in_dim(value_all, column, pair_width, 1).reshape(
                W + QB, 2, HEAD_DIM
            )
            scores = jnp.einsum(
                "qhd,khd->hqk", query_part, key_part, preferred_element_type=jnp.float32
            )
            exponent = jnp.where(allowed[None], jnp.exp(scores), 0.0)
            weights = (exponent / jnp.sum(exponent, axis=-1, keepdims=True)).astype(jnp.bfloat16)
            context = jnp.einsum(
                "hqk,khd->qhd", weights, value_part, preferred_element_type=jnp.float32
            )
            return lax.dynamic_update_slice_in_dim(
                output, context.reshape(QB, pair_width).astype(jnp.bfloat16), column, 1
            )

        return lax.fori_loop(0, pair_count, one_pair, jnp.zeros((QB, width), jnp.bfloat16))

    contexts = lax.map(one_block, jnp.arange(row_count // QB, dtype=jnp.int32) * QB)
    return contexts.reshape(row_count, width)


def local(byte_states, group_states, boundaries, w_query, w_key, w_value, w_out):
    own_bytes = byte_states[0]
    own_groups = group_states[0]
    start_list = boundaries[0]
    row_count, width = own_bytes.shape
    owned_count = own_groups.shape[0]
    device_pos = lax.axis_index("seq")
    carried = shifted(own_groups[owned_count - TAIL :], "seq", 1)
    group_table = jnp.concatenate([carried, own_groups], axis=0)
    first_group = device_pos * owned_count - TAIL
    lowest = jnp.maximum(first_group, 0)
    window_starts = lax.dynamic_slice_in_dim(start_list, lowest, owned_count + TAIL, 0)
    positions = device_pos * row_count + jnp.arange(row_count, dtype=jnp.int32)
    counted = jnp.sum((window_starts[None, :] <= positions[:, None]).astype(jnp.int32), axis=1)
    slot_index = lowest + counted - 1 - first_group
    lifted = jnp.take(group_table, slot_index, axis=0)
    dechunked = (own_bytes.astype(jnp.float32) + lifted.astype(jnp.float32)).astype(jnp.bfloat16)
    widened = dechunked.astype(jnp.float32)
    normed = (
        widened * lax.rsqrt(jnp.mean(widened * widened, axis=-1, keepdims=True) + norm_eps)
    ).astype(jnp.bfloat16)
    queries = contract(normed, lax.all_gather(w_query, "fsdp", axis=0, tiled=True))
    keys_raw = contract(normed, lax.all_gather(w_key, "fsdp", axis=0, tiled=True))
    values_raw = contract(normed, lax.all_gather(w_value, "fsdp", axis=0, tiled=True))
    own_keys = head_norm(keys_raw, 1.0).astype(jnp.bfloat16)
    own_values = values_raw.astype(jnp.bfloat16)
    past_keys, past_values = reach_back((own_keys, own_values))
    key_hat = jnp.concatenate([past_keys, own_keys], axis=0)
    value_all = jnp.concatenate([past_values, own_values], axis=0)
    query_hat = head_norm(queries, score_scale / HEAD_DIM).astype(jnp.bfloat16)
    context = attend(query_hat, key_hat, value_all, device_pos * row_count - W)
    attended = contract(context, lax.all_gather(w_out, "fsdp", axis=0, tiled=True)).astype(
        jnp.bfloat16
    )
    return (dechunked[None], attended[None])


def solution(mesh):
    placed = (
        P("fsdp", "seq", None),
        P("fsdp", "seq", None),
        P("fsdp", None),
        P("fsdp", None),
        P("fsdp", None),
        P("fsdp", None),
        P("fsdp", None),
    )
    return jax.shard_map(
        local,
        mesh=mesh,
        in_specs=placed,
        out_specs=(P("fsdp", "seq", None), P("fsdp", "seq", None)),
        check_vma=False,
    )
```

profile of v0, /device:TPU:24, one launch (start us, length us, event | category | flops | bytes accessed | tf_op | source)
XLA Modules:
  0.0 559.4 jit_solution(16077799660658742794)
XLA Ops:
  21.0 18.3 %all-gather.9.cloned.1.call-done = bf16[1024,1024]{1,0:T(8,128)(2,1)} async-done(((bf16[128,1024]{1,0:T(8,128)(2,1)}), bf16[1024,1024]{1,0:T(8,128)(2,1)}) %all-gather.9.cloned.1.call-update) | async-done | bytes 2097168 | tf_op jit(solution)/shard_map/all_gather | solution.py:124
  46.6 8.6 %collective-permute-start.5 = (bf16[512,1024]{0,1:T(8,128)(2,1)S(1)}, bf16[512,1024]{0,1:T(8,128)(2,1)}, u32[]{:S(2)}, u32[]{:S(2)}) collective-permute-start(bf16[512,1024]{0,1:T(8,128)(2,1)S(1)} %bitcast.68), channel_id=1, source_target_pairs={{0,32},{8,40},{16,48},{24,56},{32,64},{40,72},{48,80},{56,88},{64,... | collective-permute-start | bytes 3145736 | tf_op jit(solution)/shard_map/ppermute | solution.py:24
  73.1 8.3 %collective-permute-start.1 = (bf16[512,1024]{1,0:T(8,128)(2,1)}, bf16[512,1024]{1,0:T(8,128)(2,1)}, u32[]{:S(2)}, u32[]{:S(2)}) collective-permute-start(bf16[512,1024]{1,0:T(8,128)(2,1)} %convolution_convert_fusion.1), channel_id=1, source_target_pairs={{0,32},{8,40},{16,48},{24,56},{32,64},{40,72},{48,80},{56,88},{64,... | collective-permute-start | bytes 3145736 | tf_op jit(solution)/shard_map/ppermute | solution.py:24
  81.4 17.8 %all-gather.7.cloned.1.call-done = bf16[1024,1024]{1,0:T(8,128)(2,1)} async-done(((bf16[128,1024]{1,0:T(8,128)(2,1)}), bf16[1024,1024]{1,0:T(8,128)(2,1)}) %all-gather.7.cloned.1.call-update) | async-done | bytes 2097168 | tf_op jit(solution)/shard_map/all_gather | solution.py:123
  104.7 5.5 collective-permute-start.2
  110.2 55.8 %collective-permute-done.6 = bf16[512,1024]{0,1:T(8,128)(2,1)} collective-permute-done((bf16[512,1024]{0,1:T(8,128)(2,1)S(1)}, bf16[512,1024]{0,1:T(8,128)(2,1)}, u32[]{:S(2)}, u32[]{:S(2)}) %collective-permute-start.6) | collective-permute-done | bytes 1048608 | tf_op jit(solution)/shard_map/ppermute | solution.py:24
  169.6 20.5 %collective-permute-done.7 = bf16[512,1024]{0,1:T(8,128)(2,1)} collective-permute-done((bf16[512,1024]{0,1:T(8,128)(2,1)S(1)}, bf16[512,1024]{0,1:T(8,128)(2,1)}, u32[]{:S(2)}, u32[]{:S(2)}) %collective-permute-start.7) | collective-permute-done | bytes 1048608 | tf_op jit(solution)/shard_map/ppermute | solution.py:24
  190.2 25.8 %collective-permute-start.4 = (bf16[512,1024]{1,0:T(8,128)(2,1)}, bf16[512,1024]{1,0:T(8,128)(2,1)S(1)}, u32[]{:S(2)}, u32[]{:S(2)}) collective-permute-start(bf16[512,1024]{1,0:T(8,128)(2,1)} %convolution_convert_fusion.1), channel_id=1, source_target_pairs={{0,8},{8,16},{16,24},{24,32},{32,40},{40,48},{48,56},{56,64},{64,7... | collective-permute-start | bytes 3145736 | tf_op jit(solution)/shard_map/ppermute | solution.py:24
  219.8 15.6 %collective-permute-done.8 = bf16[512,1024]{0,1:T(8,128)(2,1)} collective-permute-done((bf16[512,1024]{0,1:T(8,128)(2,1)S(1)}, bf16[512,1024]{0,1:T(8,128)(2,1)}, u32[]{:S(2)}, u32[]{:S(2)}) %collective-permute-start.8) | collective-permute-done | bytes 1048608 | tf_op jit(solution)/shard_map/ppermute | solution.py:24
  239.2 38.0 %collective-permute-done.1 = bf16[512,1024]{1,0:T(8,128)(2,1)} collective-permute-done((bf16[512,1024]{1,0:T(8,128)(2,1)}, bf16[512,1024]{1,0:T(8,128)(2,1)}, u32[]{:S(2)}, u32[]{:S(2)}) %collective-permute-start.1) | collective-permute-done | bytes 1048608 | tf_op jit(solution)/shard_map/ppermute | solution.py:24
  278.4 67.1 %collective-permute-done.2 = bf16[512,1024]{1,0:T(8,128)(2,1)S(1)} collective-permute-done((bf16[512,1024]{1,0:T(8,128)(2,1)}, bf16[512,1024]{1,0:T(8,128)(2,1)S(1)}, u32[]{:S(2)}, u32[]{:S(2)}) %collective-permute-start.2) | collective-permute-done | bytes 1048608 | tf_op jit(solution)/shard_map/ppermute | solution.py:24
  345.6 24.4 %collective-permute-done.3 = bf16[512,1024]{1,0:T(8,128)(2,1)S(1)} collective-permute-done((bf16[512,1024]{1,0:T(8,128)(2,1)}, bf16[512,1024]{1,0:T(8,128)(2,1)S(1)}, u32[]{:S(2)}, u32[]{:S(2)}) %collective-permute-start.3) | collective-permute-done | bytes 1048608 | tf_op jit(solution)/shard_map/ppermute | solution.py:24
  370.1 44.6 %collective-permute-done.4 = bf16[512,1024]{1,0:T(8,128)(2,1)S(1)} collective-permute-done((bf16[512,1024]{1,0:T(8,128)(2,1)}, bf16[512,1024]{1,0:T(8,128)(2,1)S(1)}, u32[]{:S(2)}, u32[]{:S(2)}) %collective-permute-start.4) | collective-permute-done | bytes 1048608 | tf_op jit(solution)/shard_map/ppermute | solution.py:24
  418.6 130.2 %while.21 = (s32[]{:T(128)}, bf16[512,1024]{0,1:T(8,128)(2,1)}, bf16[2560,1024]{1,0:T(8,128)(2,1)}, bf16[512,1024]{0,1:T(8,128)(2,1)}, bf16[2560,1024]{0,1:T(8,1...) while((s32[]{:T(128)}, bf16[512,1024]{0,1:T(8,128)(2,1)}, ...), condition=%wide.region_6.7_spmd.clone, body=%wide.region_4.6_spmd.clone.sunk | while | flops 689503232 | bytes 30945964 | solution.py:96
  428.6 5.6 fusion.41
  444.9 5.6 fusion.41
  454.4 5.3 fusion.40
  461.1 5.6 fusion.41
  477.4 5.6 fusion.41
  486.9 5.3 fusion.40
  493.6 5.6 fusion.41
  509.9 5.6 fusion.41
  526.2 5.6 fusion.41
  542.5 5.6 fusion.41
  (116 shorter events, 139.7 us)
Async XLA Ops:
  7.2 7.1 %copy-start = (s32[1,4096]{1,0:T(1,128)S(1)}, s32[1,4096]{1,0:T(1,128)}, u32[]{:S(2)}) copy-start(s32[1,4096]{1,0:T(1,128)} %param.11) | copy-start | bytes 49156
  7.2 32.2 %all-gather.9.cloned.1.call-start = ((), (), s32[]{:S(2)}) async-start(), calls=%async_computation.2 | async-start | bytes 2359296 | tf_op jit(solution)/shard_map/all_gather | solution.py:124
  7.9 61.4 %all-gather.5.cloned.1.call-start = ((), (), s32[]{:S(2)}) async-start(), calls=%async_computation | async-start | bytes 2359296 | tf_op jit(solution)/shard_map/all_gather | solution.py:125
  8.7 90.6 %all-gather.7.cloned.1.call-start = ((), (), s32[]{:S(2)}) async-start(), calls=%async_computation.1 | async-start | bytes 2359296 | tf_op jit(solution)/shard_map/all_gather | solution.py:123
  9.4 539.3 %all-gather.11.cloned.1.call-start = ((), (), s32[]{:S(2)}) async-start(), calls=%async_computation.3 | async-start | bytes 2359296 | tf_op jit(solution)/shard_map/all_gather | solution.py:133
  10.4 6.6 %collective-permute-start = (bf16[64,1024]{1,0:T(8,128)(2,1)S(1)}, bf16[64,1024]{1,0:T(8,128)(2,1)S(1)}, u32[]{:S(2)}, u32[]{:S(2)}) collective-permute-start(bf16[64,1024]{1,0:T(8,128)(2,1)S(1)} %slice_bitcast_fusion), channel_id=1, source_target_pairs={{0,8},{8,16},{16,24},{24,32},{32,40},{40,48},{48,56},{56,64},{64,7... | collective-permute-start | bytes 393224 | tf_op jit(solution)/shard_map/ppermute | solution.py:24
  17.9 2.1 copy-start.1
  20.4 22.9 %copy-start.4 = (bf16[1,512,1024]{2,1,0:T(8,128)(2,1)}, bf16[1,512,1024]{2,1,0:T(8,128)(2,1)S(1)}, u32[]{:S(2)}) copy-start(bf16[1,512,1024]{2,1,0:T(8,128)(2,1)S(1)} %fusion.8) | copy-start | bytes 3145732
  46.6 58.1 %collective-permute-start.5 = (bf16[512,1024]{0,1:T(8,128)(2,1)S(1)}, bf16[512,1024]{0,1:T(8,128)(2,1)}, u32[]{:S(2)}, u32[]{:S(2)}) collective-permute-start(bf16[512,1024]{0,1:T(8,128)(2,1)S(1)} %bitcast.68), channel_id=1, source_target_pairs={{0,32},{8,40},{16,48},{24,56},{32,64},{40,72},{48,80},{56,88},{64,... | collective-permute-start | bytes 3145736 | tf_op jit(solution)/shard_map/ppermute | solution.py:24
  55.3 110.8 %collective-permute-start.6 = (bf16[512,1024]{0,1:T(8,128)(2,1)S(1)}, bf16[512,1024]{0,1:T(8,128)(2,1)}, u32[]{:S(2)}, u32[]{:S(2)}) collective-permute-start(bf16[512,1024]{0,1:T(8,128)(2,1)S(1)} %bitcast.69), channel_id=1, source_target_pairs={{0,24},{8,32},{16,40},{24,48},{32,56},{40,64},{48,72},{56,80},{64,... | collective-permute-start | bytes 3145736 | tf_op jit(solution)/shard_map/ppermute | solution.py:24
  59.0 131.2 %collective-permute-start.7 = (bf16[512,1024]{0,1:T(8,128)(2,1)S(1)}, bf16[512,1024]{0,1:T(8,128)(2,1)}, u32[]{:S(2)}, u32[]{:S(2)}) collective-permute-start(bf16[512,1024]{0,1:T(8,128)(2,1)S(1)} %bitcast.70), channel_id=1, source_target_pairs={{0,16},{8,24},{16,32},{24,40},{32,48},{40,56},{48,64},{56,72},{64,... | collective-permute-start | bytes 3145736 | tf_op jit(solution)/shard_map/ppermute | solution.py:24
  62.8 172.7 %collective-permute-start.8 = (bf16[512,1024]{0,1:T(8,128)(2,1)S(1)}, bf16[512,1024]{0,1:T(8,128)(2,1)}, u32[]{:S(2)}, u32[]{:S(2)}) collective-permute-start(bf16[512,1024]{0,1:T(8,128)(2,1)S(1)} %bitcast.71), channel_id=1, source_target_pairs={{0,8},{8,16},{16,24},{24,32},{32,40},{40,48},{48,56},{56,64},{64,7... | collective-permute-start | bytes 3145736 | tf_op jit(solution)/shard_map/ppermute | solution.py:24
  73.1 204.0 %collective-permute-start.1 = (bf16[512,1024]{1,0:T(8,128)(2,1)}, bf16[512,1024]{1,0:T(8,128)(2,1)}, u32[]{:S(2)}, u32[]{:S(2)}) collective-permute-start(bf16[512,1024]{1,0:T(8,128)(2,1)} %convolution_convert_fusion.1), channel_id=1, source_target_pairs={{0,32},{8,40},{16,48},{24,56},{32,64},{40,72},{48,80},{56,88},{64,... | collective-permute-start | bytes 3145736 | tf_op jit(solution)/shard_map/ppermute | solution.py:24
  104.7 240.8 %collective-permute-start.2 = (bf16[512,1024]{1,0:T(8,128)(2,1)}, bf16[512,1024]{1,0:T(8,128)(2,1)S(1)}, u32[]{:S(2)}, u32[]{:S(2)}) collective-permute-start(bf16[512,1024]{1,0:T(8,128)(2,1)} %convolution_convert_fusion.1), channel_id=1, source_target_pairs={{0,24},{8,32},{16,40},{24,48},{32,56},{40,64},{48,72},{56,80},{64,... | collective-permute-start | bytes 3145736 | tf_op jit(solution)/shard_map/ppermute | solution.py:24
  166.0 204.0 %collective-permute-start.3 = (bf16[512,1024]{1,0:T(8,128)(2,1)}, bf16[512,1024]{1,0:T(8,128)(2,1)S(1)}, u32[]{:S(2)}, u32[]{:S(2)}) collective-permute-start(bf16[512,1024]{1,0:T(8,128)(2,1)} %convolution_convert_fusion.1), channel_id=1, source_target_pairs={{0,16},{8,24},{16,32},{24,40},{32,48},{40,56},{48,64},{56,72},{64,... | collective-permute-start | bytes 3145736 | tf_op jit(solution)/shard_map/ppermute | solution.py:24
  190.2 224.4 %collective-permute-start.4 = (bf16[512,1024]{1,0:T(8,128)(2,1)}, bf16[512,1024]{1,0:T(8,128)(2,1)S(1)}, u32[]{:S(2)}, u32[]{:S(2)}) collective-permute-start(bf16[512,1024]{1,0:T(8,128)(2,1)} %convolution_convert_fusion.1), channel_id=1, source_target_pairs={{0,8},{8,16},{16,24},{24,32},{32,40},{40,48},{48,56},{56,64},{64,7... | collective-permute-start | bytes 3145736 | tf_op jit(solution)/shard_map/ppermute | solution.py:24
  236.8 2.4 copy-start.3
  416.0 2.6 copy-start.2
Sparse Core Ops, SparseCore 0:
  9.9 29.4 all-gather.8
  41.2 28.0 all-gather.4
  71.1 28.0 all-gather.6
  100.9 28.0 all-gather.10
where the time goes:
time: 565 us; the launch traced here: 559 us
  waiting for transfers between devices  310 us (55%)
  matrix products  101 us (18%)
  starting transfers between devices  65.4 us (12%)
  local copies, waits for them, and re-layouts  55.7 us (10%)
  between operations  14 us (2%)
  other arithmetic  13.9 us (2%)
    ppermute x9, waiting for transfers between devices, shifted(): return lax.ppermute(block, axis, route)  268 us
    ppermute x9, starting transfers between devices, shifted(): return lax.ppermute(block, axis, route)  65.3 us
    dot_general x8, matrix products, one_pair(): jnp.einsum('hqk,khd->qhd', weights, value_part, preferred_element_type=jn...  44.5 us
    dot_general x8, matrix products, one_pair(): jnp.einsum('qhd,khd->hqk', query_part, key_part, preferred_element_type=j...  42.5 us
    all_gather x1, waiting for transfers between devices, local(): lax.all_gather(w_key, 'fsdp', axis=0, tiled=True)  18.3 us
    all_gather x1, waiting for transfers between devices, local(): lax.all_gather(w_query, 'fsdp', axis=0, tiled=True)  17.8 us
    dot_general x4, matrix products, contract(): return jnp.dot(source, piece_rows, preferred_element_type=jnp.float32)  13.6 us
  transfers between devices with their start and end apart: 13, of which 11 were waited for; matrix products, arithmetic and copies ran while one was open for 29% of the time, Pallas kernels for 0%

commit v1 on v0

v1 whole, which is shorter than its diff:
```python
import functools

import jax
import jax.numpy as jnp
from jax import lax
from jax.experimental import pallas as pl
from jax.experimental.pallas import tpu as pltpu
from jax.sharding import PartitionSpec as P

HEAD_DIM = 64
TAIL = 64
PAIR = 2 * HEAD_DIM
QUAD = 2 * PAIR
HALF = 256
EPS = 1e-6
QUERY_FACTOR = 16.0 / HEAD_DIM * 1.4426950408889634
BF = jnp.bfloat16
F32 = jnp.float32
NT = (((1,), (1,)), ((), ()))
VMEM_LIMIT = 40 * 2**20


def params():
    return pltpu.CompilerParams(vmem_limit_bytes=VMEM_LIMIT)


def prep_kernel(row0, order_ref, win_ref, bytes_ref, carried_ref, groups_ref, out_ref, normed_ref, hold):
    rows, width = bytes_ref.shape
    position = row0 + lax.broadcasted_iota(jnp.int32, (rows, TAIL), 0)
    position_own = row0 + lax.broadcasted_iota(jnp.int32, (rows, PAIR), 0)
    start, following = win_ref[0:1, :], win_ref[1:2, :]

    def one_hot(lo, hi, where):
        return ((start[:, lo:hi] <= where) & (following[:, lo:hi] > where)).astype(F32).astype(BF)

    own = groups_ref.shape[0]
    lifted = jnp.dot(one_hot(PAIR, PAIR + own, position_own), groups_ref[...], preferred_element_type=F32)
    lifted += jnp.dot(one_hot(0, TAIL, position), carried_ref[...], preferred_element_type=F32)
    dechunked = (bytes_ref[...].astype(F32) + lifted).astype(BF)
    out_ref[...] = dechunked
    wide = dechunked.astype(F32)
    mean = jnp.sum(wide * wide, axis=-1, keepdims=True) * (1.0 / width)
    hold[...] = (wide * lax.rsqrt(mean + EPS)).astype(BF)
    for r in range(width // PAIR):
        at = pl.multiple_of(order_ref[r] * PAIR, PAIR)
        normed_ref[:, r * PAIR : (r + 1) * PAIR] = hold[:, pl.ds(at, PAIR)]


def prep(row0, order, window, own_bytes, carried, own_groups):
    width = own_bytes.shape[1]
    vmem = pl.BlockSpec(memory_space=pltpu.VMEM)
    shape = jax.ShapeDtypeStruct((HALF, width), BF)
    return pl.pallas_call(
        functools.partial(prep_kernel, row0),
        grid=(1,),
        in_specs=[
            pl.BlockSpec(memory_space=pltpu.SMEM),
            pl.BlockSpec(window.shape, lambda i: (0, 0)),
            pl.BlockSpec((HALF, width), lambda i: (row0 // HALF, 0)),
            pl.BlockSpec(carried.shape, lambda i: (0, 0)),
            pl.BlockSpec(own_groups.shape, lambda i: (0, 0)),
        ],
        out_specs=[pl.BlockSpec((HALF, width), lambda i: (0, 0))] * 2,
        out_shape=[shape, shape],
        scratch_shapes=[pltpu.VMEM((HALF, width), BF)],
        compiler_params=params(),
        cost_estimate=pl.CostEstimate(flops=2 * HALF * 192 * width, bytes_accessed=2**21, transcendentals=HALF),
        name="prep",
    )(order, window, own_bytes, carried, own_groups)


def head_norm(raw, factor):
    n = raw.shape[1]
    row = lax.broadcasted_iota(jnp.int32, (n, n), 0) // HEAD_DIM
    column = lax.broadcasted_iota(jnp.int32, (n, n), 1) // HEAD_DIM
    mean_of_head = jnp.where(row == column, 1.0 / HEAD_DIM, 0.0).astype(BF)
    mean_square = jnp.dot((raw * raw).astype(BF), mean_of_head, preferred_element_type=F32)
    return (raw * (lax.rsqrt(mean_square + EPS) * factor)).astype(BF)


def project(x, parts):
    return jnp.dot(x, jnp.concatenate([p[...] for p in parts], axis=0), preferred_element_type=F32)


def masked(scores, mode):
    weights = jnp.exp2(scores)
    if mode != "full":
        query = lax.broadcasted_iota(jnp.int32, scores.shape, 0)
        key = lax.broadcasted_iota(jnp.int32, scores.shape, 1)
        keep = key <= query if mode == "until" else key >= query
        weights = jnp.where(keep, weights, 0.0)
    return weights.astype(BF)


def attend_quad(query, pieces, add_to, put):
    low_q = lax.broadcasted_iota(jnp.int32, (HALF, PAIR), 1) < HEAD_DIM
    zero = jnp.zeros((HALF, PAIR), BF)
    for pair in range(2):
        lanes = slice(pair * PAIR, (pair + 1) * PAIR)
        rights = []
        for keys, values, ones, _ in pieces:
            v = values[:, lanes]
            rights.append(
                (
                    jnp.concatenate([jnp.where(low_q, v, zero), jnp.where(low_q, ones, zero)], axis=1),
                    jnp.concatenate([jnp.where(low_q, zero, v), jnp.where(low_q, zero, ones)], axis=1),
                )
            )
        for part in range(2):
            rows = slice(part * HALF, (part + 1) * HALF)
            q = query[rows, lanes]
            q_a, q_b = jnp.where(low_q, q, zero), jnp.where(low_q, zero, q)
            left, right = [], []
            for (keys, _, _, modes), (right_a, right_b) in zip(pieces, rights):
                if modes[part] == "none":
                    continue
                k = keys[:, lanes]
                left.append(masked(lax.dot_general(q_a, k, NT, preferred_element_type=F32), modes[part]))
                left.append(masked(lax.dot_general(q_b, k, NT, preferred_element_type=F32), modes[part]))
                right += [right_a, right_b]
            total = jnp.dot(
                jnp.concatenate(left, axis=1), jnp.concatenate(right, axis=0), preferred_element_type=F32
            )
            put(pair, rows, total if add_to is None else add_to[pair, rows, :] + total)


def own_kernel(*refs):
    top_ref, bottom_ref = refs[0:2]
    w_q, w_k, w_v = refs[2:10], refs[10:18], refs[18:26]
    query_ref, total_ref = refs[26:]
    x = jnp.concatenate([top_ref[...], bottom_ref[...]], axis=0)
    query = head_norm(project(x, w_q), QUERY_FACTOR)
    query_ref[...] = query
    key = head_norm(project(x, w_k), 1.0)
    value = project(x, w_v).astype(BF)
    ones = jnp.ones((HALF, PAIR), BF)
    pieces = [
        (key[:HALF], value[:HALF], ones, ("until", "full")),
        (key[HALF:], value[HALF:], ones, ("none", "until")),
    ]

    def put(pair, rows, total):
        total_ref[pair, rows, :] = total

    attend_quad(query, pieces, None, put)


def step_body(modes, valid_ref, a_ref, b_ref, w_k, w_v, query_ref, total_ref, put):
    pieces = []
    for i, x_ref in enumerate((a_ref, b_ref)):
        x = x_ref[...]
        valid = valid_ref[i] > 0
        key = head_norm(project(x, w_k), 1.0)
        value = jnp.where(valid, project(x, w_v), 0.0).astype(BF)
        ones = jnp.where(valid, jnp.ones((HALF, PAIR), F32), 0.0).astype(BF)
        pieces.append((key, value, ones, modes[i]))
    attend_quad(query_ref[...], pieces, total_ref, put)


def step_kernel(modes, *refs):
    valid_ref, a_ref, b_ref = refs[0:3]
    query_ref, total_ref, out_ref = refs[19:]

    def put(pair, rows, total):
        out_ref[pair, rows, :] = total

    step_body(modes, valid_ref, a_ref, b_ref, refs[3:11], refs[11:19], query_ref, total_ref, put)


def last_kernel(modes, *refs):
    valid_ref, order_ref, a_ref, b_ref = refs[0:4]
    w_k, w_v, w_o = refs[4:12], refs[12:20], refs[20:28]
    query_ref, total_ref, out_ref, context = refs[28:]
    g = pl.program_id(0)

    def put(pair, rows, total):
        context[2 * g + pair, rows, :] = (total[:, :PAIR] / total[:, PAIR:]).astype(BF)

    step_body(modes, valid_ref, a_ref, b_ref, w_k, w_v, query_ref, total_ref, put)

    @pl.when(g == pl.num_programs(0) - 1)
    def _():
        x = jnp.concatenate([context[order_ref[r]] for r in range(8)], axis=1)
        out_ref[...] = project(x, w_o).astype(BF)


def weight_specs(weights, kind):
    arrays = [part[kind][0] for part in weights]
    specs = [
        pl.BlockSpec((PAIR, QUAD), functools.partial(lambda row, g: (row, g), part[kind][1])) for part in weights
    ]
    return arrays, specs


def fixed(shape):
    return pl.BlockSpec(shape, lambda g: (0,) * len(shape))


def attention_cost(keys, projections):
    flops = 2 * 512 * keys * 1024 * 2 + 2 * 1024 * 1024 * projections
    return pl.CostEstimate(flops=2 * flops, bytes_accessed=14 * 2**20, transcendentals=512 * keys * 16)


def attend_own(top, bottom, weights):
    width = top.shape[1]
    q, q_specs = weight_specs(weights, 0)
    k, k_specs = weight_specs(weights, 1)
    v, v_specs = weight_specs(weights, 2)
    return pl.pallas_call(
        own_kernel,
        grid=(width // QUAD,),
        in_specs=[fixed(top.shape), fixed(bottom.shape)] + q_specs + k_specs + v_specs,
        out_specs=[
            pl.BlockSpec((2 * HALF, QUAD), lambda g: (0, g)),
            pl.BlockSpec((2, 2 * HALF, QUAD), lambda g: (g, 0, 0)),
        ],
        out_shape=[
            jax.ShapeDtypeStruct((2 * HALF, width), BF),
            jax.ShapeDtypeStruct((width // PAIR, 2 * HALF, QUAD), F32),
        ],
        compiler_params=params(),
        cost_estimate=attention_cost(384, 3 * 512),
        name="own",
    )(top, bottom, *q, *k, *v)


def attend_step(modes, valid, a, b, weights, query, total):
    width = a.shape[1]
    k, k_specs = weight_specs(weights, 1)
    v, v_specs = weight_specs(weights, 2)
    return pl.pallas_call(
        functools.partial(step_kernel, modes),
        grid=(width // QUAD,),
        in_specs=[pl.BlockSpec(memory_space=pltpu.SMEM), fixed(a.shape), fixed(b.shape)]
        + k_specs
        + v_specs
        + [
            pl.BlockSpec((2 * HALF, QUAD), lambda g: (0, g)),
            pl.BlockSpec((2, 2 * HALF, QUAD), lambda g: (g, 0, 0)),
        ],
        out_specs=pl.BlockSpec((2, 2 * HALF, QUAD), lambda g: (g, 0, 0)),
        out_shape=jax.ShapeDtypeStruct(total.shape, F32),
        compiler_params=params(),
        cost_estimate=attention_cost(512, 2 * 512),
        name="step",
    )(valid, a, b, *k, *v, query, total)


def attend_last(modes, valid, order, a, b, weights, query, total):
    width = a.shape[1]
    k, k_specs = weight_specs(weights, 1)
    v, v_specs = weight_specs(weights, 2)
    o = [part[3][0] for part in weights]
    o_specs = [
        pl.BlockSpec((PAIR, width), functools.partial(lambda row, g: (row, 0), part[3][1])) for part in weights
    ]
    return pl.pallas_call(
        functools.partial(last_kernel, modes),
        grid=(width // QUAD,),
        in_specs=[pl.BlockSpec(memory_space=pltpu.SMEM)] * 2
        + [fixed(a.shape), fixed(b.shape)]
        + k_specs
        + v_specs
        + o_specs
        + [
            pl.BlockSpec((2 * HALF, QUAD), lambda g: (0, g)),
            pl.BlockSpec((2, 2 * HALF, QUAD), lambda g: (g, 0, 0)),
        ],
        out_specs=fixed((2 * HALF, width)),
        out_shape=jax.ShapeDtypeStruct((2 * HALF, width), BF),
        scratch_shapes=[pltpu.VMEM((width // PAIR, 2 * HALF, PAIR), BF)],
        compiler_params=params(),
        cost_estimate=attention_cost(512, 3 * 512),
        name="last",
    )(valid, order, a, b, *k, *v, *o, query, total)


def along_seq(block, distance):
    count = lax.axis_size("seq")
    return lax.ppermute(block, "seq", [(i, (i + distance) % count) for i in range(count)])


def along_y(block, distance):
    count = lax.axis_size("fsdp")
    return lax.ppermute(block, "fsdp", [(i, (i + 2 * distance) % count) for i in range(count)])


def other_core(block):
    return lax.ppermute(block, "fsdp", [(i, i ^ 1) for i in range(lax.axis_size("fsdp"))])


def gather_weights(w_query, w_key, w_value, w_out):
    own = jnp.concatenate([w_query, w_key, w_value, w_out], axis=0)
    rows = w_query.shape[0]
    below, above = along_y(own, 1), along_y(own, -1)
    other = other_core(own)
    far_qk = along_y(below[: 2 * rows], 1)
    far_vo = along_y(above[2 * rows :], -1)
    other_below, other_above = other_core(below), other_core(above)
    other_far_qk, other_far_vo = other_core(far_qk), other_core(far_vo)
    parts = [tuple((part, i) for i in range(4)) for part in (own, other, below, other_below, above, other_above)]
    for qk, vo in ((far_qk, far_vo), (other_far_qk, other_far_vo)):
        parts.append(((qk, 0), (qk, 1), (vo, 0), (vo, 1)))
    return parts


def weight_order():
    me = lax.axis_index("fsdp")
    y, core = me // 2, me % 2
    return jnp.stack(
        [2 * ((y + dy) % 4) + (core + other) % 2 for dy in (0, 3, 1, 2) for other in (0, 1)]
    ).astype(jnp.int32)


def local(byte_states, group_states, boundaries, w_query, w_key, w_value, w_out):
    own_bytes, own_groups, starts = byte_states[0], group_states[0], boundaries[0]
    rows, width = own_bytes.shape
    owned = own_groups.shape[0]
    position = lax.axis_index("seq")
    order = weight_order()

    carried = along_seq(own_groups[owned - TAIL :], 1)
    weights = gather_weights(w_query, w_key, w_value, w_out)

    far = jnp.int32(2**30)
    padded = jnp.concatenate([jnp.zeros((TAIL,), jnp.int32), starts, jnp.full((1,), far, jnp.int32)])
    window = lax.dynamic_slice_in_dim(padded, position * owned, owned + TAIL + 1, 0) - position * rows
    begin, end = window[:-1], window[1:]
    gap = jnp.full((PAIR - TAIL,), far, jnp.int32)
    window = jnp.stack([jnp.concatenate([w[:TAIL], gap, w[TAIL:]]) for w in (begin, end)])

    out_bottom, bottom = prep(HALF, order, window, own_bytes, carried, own_groups)
    down = along_seq(bottom, 4)
    out_top, top = prep(0, order, window, own_bytes, carried, own_groups)
    up = along_seq(top, 1)
    dechunked = jnp.concatenate([out_top, out_bottom], axis=0)

    query, total = attend_own(top, bottom, weights)

    full = ("full", "full")
    for k in range(1, 5):
        valid = jnp.stack([position >= k, position >= 5 - k]).astype(jnp.int32)
        modes = (full if k < 4 else ("from", "none"), full if k > 1 else ("full", "from"))
        if k < 4:
            total = attend_step(modes, valid, up, down, weights, query, total)
            up, down = along_seq(up, 1), along_seq(down, -1)
        else:
            attended = attend_last(modes, valid, order, up, down, weights, query, total)
    return dechunked[None], attended[None]


def solution(mesh):
    placed = (P("fsdp", "seq", None),) * 2 + (P("fsdp", None),) * 5
    return jax.shard_map(
        local,
        mesh=mesh,
        in_specs=placed,
        out_specs=(P("fsdp", "seq", None), P("fsdp", "seq", None)),
        check_vma=False,
    )
```

time: 565 us -> 169 us (0.30)
  waiting for transfers between devices: 310 us -> 59 us
  matrix products: 101 us -> 0 us
  Pallas kernels: 0 us -> 64.8 us
  local copies, waits for them, and re-layouts: 55.7 us -> 15.6 us
  starting transfers between devices: 65.4 us -> 25.6 us
  between operations: 14 us -> 0.87 us
  other arithmetic: 13.9 us -> 2.85 us
    ppermute x9 -> x18, waiting for transfers between devices: 268 us -> 59 us  [the longest x9 59 us: along_seq(): lax.ppermute(block, 'seq', [(i, (i + distance) % count) for i in range(co...]
    dot_general x20 -> x0, matrix products: 101 us -> none  [the longest x8 44.5 us: one_pair(): jnp.einsum('hqk,khd->qhd', weights, value_part, preferred_element_type=jn...]
    pallas_call x0 -> x7, Pallas kernels: none -> 64.8 us  [the longest x3 35.3 us: attend_step(): pl.pallas_call(functools.partial(step_kernel, modes), grid=(width // QUAD...]
    ppermute x9 -> x18, starting transfers between devices: 65.3 us -> 25.6 us  [the longest x9 20.9 us: along_seq(): lax.ppermute(block, 'seq', [(i, (i + distance) % count) for i in range(co...]
    all_gather x4 -> x0, waiting for transfers between devices: 39.1 us -> none  [the longest x1 18.3 us: local(): lax.all_gather(w_key, 'fsdp', axis=0, tiled=True)]
    dynamic_slice x33 -> x0, local copies, waits for them, and re-layouts: 27.5 us -> none  [the longest x16 11 us: one_pair(): lax.dynamic_slice_in_dim(value_all, column, pair_width, 1)]
    and x9 -> x0, other arithmetic: 10.1 us -> none  [the longest x8 10.1 us: one_block(): (key_index >= offset) & (key_index <= offset + W)]
    dot_general x2 -> x0, local copies, waits for them, and re-layouts: 6.85 us -> none  [contract(): return jnp.dot(source, piece_rows, preferred_element_type=jnp.float32)]
  transfers between devices with their start and end apart: 13 -> 18, of which waited for: 11 -> 5; matrix products, arithmetic and copies ran while one was open for 29% -> 4% of each run, Pallas kernels for 0% -> 31%
where the time goes in v1:
time: 169 us
  Pallas kernels  64.8 us (38%)
  waiting for transfers between devices  59 us (35%)
  starting transfers between devices  25.6 us (15%)
  local copies, waits for them, and re-layouts  15.6 us (9%)
  other arithmetic  2.85 us (2%)
    ppermute x9, waiting for transfers between devices, along_seq(): lax.ppermute(block, 'seq', [(i, (i + distance) % count) for i in range(co...  59 us
    pallas_call x3, Pallas kernels, attend_step(): pl.pallas_call(functools.partial(step_kernel, modes), grid=(width // QUAD...  35.3 us
    ppermute x9, starting transfers between devices, along_seq(): lax.ppermute(block, 'seq', [(i, (i + distance) % count) for i in range(co...  20.9 us
    pallas_call x1, Pallas kernels, attend_own(): pl.pallas_call(own_kernel, grid=(width // QUAD,), in_specs=[fixed(top.sha...  14.6 us
    pallas_call x1, Pallas kernels, attend_last(): pl.pallas_call(functools.partial(last_kernel, modes), grid=(width // QUAD...  12.3 us
    unnamed x37, local copies, waits for them, and re-layouts  11 us
    ppermute x4, starting transfers between devices, along_y(): lax.ppermute(block, 'fsdp', [(i, (i + 2 * distance) % count) for i in ran...  4.13 us
  transfers between devices with their start and end apart: 18, of which 5 were waited for; matrix products, arithmetic and copies ran while one was open for 4% of the time, Pallas kernels for 31%

profile of v1, /device:TPU:24, one launch (start us, length us, event | category | flops | bytes accessed | tf_op | source)
XLA Modules:
  0.0 168.7 jit_solution(9206247145741939744)
XLA Ops:
  4.5 2.0 %collective-permute-start.10 = (bf16[512,1024]{1,0:T(8,128)(2,1)S(1)}, bf16[512,1024]{1,0:T(8,128)(2,1)S(1)}, u32[]{:S(2)}, u32[]{:S(2)}) collective-permute-start(bf16[512,1024]{1,0:T(8,128)(2,1)S(1)} %constant_dynamic-update-slice_fusion.refs_2_.refs_10_.refs_18_.refs_3_.refs_11_.refs_4_.refs_12_.refs_20_), channel_id=1, source_target_pairs={{0,2},{1,3},{2,4},{3,5},{4,6},{5,7},{6,0},{7,1},{8,10},{9,11},{10,... | collective-permute-start | bytes 3145736 | tf_op jit(solution)/shard_map/ppermute | solution.py:285
  7.5 2.0 %collective-permute-start = (bf16[64,1024]{1,0:T(8,128)(2,1)S(1)}, bf16[64,1024]{1,0:T(8,128)(2,1)S(1)}, u32[]{:S(2)}, u32[]{:S(2)}) collective-permute-start(bf16[64,1024]{1,0:T(8,128)(2,1)S(1)} %slice_bitcast_fusion), channel_id=1, source_target_pairs={{0,8},{8,16},{16,24},{24,32},{32,40},{40,48},{48,56},{56,64},{64,7... | collective-permute-start | bytes 393224 | tf_op jit(solution)/shard_map/ppermute | solution.py:280
  10.8 7.8 %collective-permute-done.carried_ref = bf16[64,1024]{1,0:T(8,128)(2,1)S(1)} collective-permute-done((bf16[64,1024]{1,0:T(8,128)(2,1)S(1)}, bf16[64,1024]{1,0:T(8,128)(2,1)S(1)}, u32[]{:S(2)}, u32[]{:S(2)}) %collective-permute-start) | collective-permute-done | bytes 131104 | tf_op jit(solution)/shard_map/ppermute | solution.py:280
  18.6 1.2 copy-done.3
  20.8 1.3 prep.2
  22.9 1.3 prep.3
  24.2 2.4 %collective-permute-start.5 = (bf16[256,1024]{1,0:T(8,128)(2,1)S(1)}, bf16[256,1024]{1,0:T(8,128)(2,1)S(1)}, u32[]{:S(2)}, u32[]{:S(2)}) collective-permute-start(bf16[256,1024]{1,0:T(8,128)(2,1)S(1)} %get-tuple-element.11.refs_1_), channel_id=1, source_target_pairs={{0,32},{8,40},{16,48},{24,56},{32,64},{40,72},{48,80},{56,88},{64,... | collective-permute-start | bytes 1572872 | tf_op jit(solution)/shard_map/ppermute | solution.py:280
  26.6 36.1 %collective-permute-done.1.refs_1_ = bf16[256,1024]{1,0:T(8,128)(2,1)S(1)} collective-permute-done((bf16[256,1024]{1,0:T(8,128)(2,1)S(1)}, bf16[256,1024]{1,0:T(8,128)(2,1)S(1)}, u32[]{:S(2)}, u32[]{:S(2)}) %collective-permute-start.1) | collective-permute-done | bytes 524320 | tf_op jit(solution)/shard_map/ppermute | solution.py:280
  62.7 5.3 %collective-permute-start.6 = (bf16[256,1024]{1,0:T(8,128)(2,1)S(1)}, bf16[256,1024]{1,0:T(8,128)(2,1)S(1)}, u32[]{:S(2)}, u32[]{:S(2)}) collective-permute-start(bf16[256,1024]{1,0:T(8,128)(2,1)S(1)} %collective-permute-done.5.refs_2_), channel_id=1, source_target_pairs={{0,248},{8,0},{16,8},{24,16},{32,24},{40,32},{48,40},{56,48},{64,5... | collective-permute-start | bytes 1572872 | tf_op jit(solution)/shard_map/ppermute | solution.py:280
  70.5 1.2 collective-permute-start.16
  71.7 6.1 %collective-permute-done.2.refs_1_ = bf16[256,1024]{1,0:T(8,128)(2,1)} collective-permute-done((bf16[256,1024]{1,0:T(8,128)(2,1)S(1)}, bf16[256,1024]{1,0:T(8,128)(2,1)}, u32[]{:S(2)}, u32[]{:S(2)}) %collective-permute-start.2) | collective-permute-done | bytes 524320 | tf_op jit(solution)/shard_map/ppermute | solution.py:280
  80.2 5.3 %collective-permute-start.7 = (bf16[256,1024]{1,0:T(8,128)(2,1)}, bf16[256,1024]{1,0:T(8,128)(2,1)}, u32[]{:S(2)}, u32[]{:S(2)}) collective-permute-start(bf16[256,1024]{1,0:T(8,128)(2,1)} %copy-done.9), channel_id=1, source_target_pairs={{0,248},{8,0},{16,8},{24,16},{32,24},{40,32},{48,40},{56,48},{64,5... | collective-permute-start | bytes 1572872 | tf_op jit(solution)/shard_map/ppermute | solution.py:280
  85.5 5.1 %collective-permute-done.3.refs_1_ = bf16[256,1024]{1,0:T(8,128)(2,1)} collective-permute-done((bf16[256,1024]{1,0:T(8,128)(2,1)}, bf16[256,1024]{1,0:T(8,128)(2,1)}, u32[]{:S(2)}, u32[]{:S(2)}) %collective-permute-start.3) | collective-permute-done | bytes 524320 | tf_op jit(solution)/shard_map/ppermute | solution.py:280
  90.9 2.4 %maximum_bitcast_fusion = bf16[1,512,1024]{2,1,0:T(8,128)(2,1)} fusion(bf16[256,1024]{1,0:T(8,128)(2,1)} %copy-done.12, bf16[256,1024]{1,0:T(8,128)(2,1)} %copy-done.11), kind=kLoop, calls=%fused_computation | loop fusion | flops 2097152 | bytes 2097152 | tf_op jit(solution)/shard_map/broadcast_in_dim | solution.py:349
  93.3 3.8 %collective-permute-done.7.refs_2_ = bf16[256,1024]{1,0:T(8,128)(2,1)} collective-permute-done((bf16[256,1024]{1,0:T(8,128)(2,1)}, bf16[256,1024]{1,0:T(8,128)(2,1)}, u32[]{:S(2)}, u32[]{:S(2)}) %collective-permute-start.7) | collective-permute-done | bytes 524320 | tf_op jit(solution)/shard_map/ppermute | solution.py:280
  97.2 5.8 %collective-permute-start.8 = (bf16[256,1024]{1,0:T(8,128)(2,1)}, bf16[256,1024]{1,0:T(8,128)(2,1)S(1)}, u32[]{:S(2)}, u32[]{:S(2)}) collective-permute-start(bf16[256,1024]{1,0:T(8,128)(2,1)} %collective-permute-done.7.refs_2_), channel_id=1, source_target_pairs={{0,248},{8,0},{16,8},{24,16},{32,24},{40,32},{48,40},{56,48},{64,5... | collective-permute-start | bytes 1572872 | tf_op jit(solution)/shard_map/ppermute | solution.py:280
  103.0 1.2 copy-done.1
  104.2 1.0 copy-done.14
  105.3 1.0 copy-done.16
  106.3 14.6 %own.1 = (bf16[512,1024]{1,0:T(8,128)(2,1)S(1)}, f32[8,512,256]{2,1,0:T(8,128)}) custom-call(bf16[256,1024]{1,0:T(8,128)(2,1)S(1)} %copy-done.14, bf16[256,1024]{1,0:T(8,128)(2,1)S(1)} %copy-done.16, bf16[512,1024]{1,0:T(8,128)(2,1)S(1)} %constant_dynamic-update-slice_fusion.refs_2_.refs_10_.refs_18_.refs_3_.refs_11_.refs_4_.refs_12_.refs_20_, ...), custom_call_target="tpu_custom_call" | custom-call | flops 8053063680 | bytes 14680064 | tf_op jit(solution)/shard_map/own/pallas_call | solution.py:209
  121.0 11.6 %step.3.refs_20_ = f32[8,512,256]{2,1,0:T(8,128)} custom-call(s32[2]{0:T(128)S(1)} %add_convert_fusion.3.refs_0_, bf16[256,1024]{1,0:T(8,128)(2,1)S(1)} %copy-done.6, bf16[256,1024]{1,0:T(8,128)(2,1)S(1)} %copy-done.8, bf16[512,1024]{1,0:T(8,128)(2,1)S(1)} %constant_dynamic-update-slice_fusion.refs_2_.refs_10_.refs_18_.refs_3_.refs_11_.refs_4_.refs_12_.refs_20_, ...), custom_call_target="tpu_custom_call" | custom-call | flops 6442450944 | bytes 14680064 | tf_op jit(solution)/shard_map/step/pallas_call | solution.py:231
  132.6 11.8 %step.4.refs_20_ = f32[8,512,256]{2,1,0:T(8,128)} custom-call(s32[2]{0:T(128)S(1)} %add_convert_fusion.2.refs_0_, bf16[256,1024]{1,0:T(8,128)(2,1)} %collective-permute-done.2.refs_1_, bf16[256,1024]{1,0:T(8,128)(2,1)S(1)} %copy-done.10, ...), custom_call_target="tpu_custom_call" | custom-call | flops 6442450944 | bytes 14680064 | tf_op jit(solution)/shard_map/step/pallas_call | solution.py:231
  144.5 11.9 %step.5.refs_29_ = f32[8,512,256]{2,1,0:T(8,128)} custom-call(s32[2]{0:T(128)S(1)} %add_convert_fusion.1.refs_0_, bf16[256,1024]{1,0:T(8,128)(2,1)} %collective-permute-done.3.refs_1_, bf16[256,1024]{1,0:T(8,128)(2,1)} %collective-permute-done.7.refs_2_, ...), custom_call_target="tpu_custom_call" | custom-call | flops 6442450944 | bytes 14680064 | tf_op jit(solution)/shard_map/step/pallas_call | solution.py:231
  156.4 12.3 %last.1 = bf16[512,1024]{1,0:T(8,128)(2,1)} custom-call(s32[2]{0:T(128)S(1)} %add_convert_fusion.refs_0_, s32[8]{0:T(128)S(1)} %stack.72.order_ref.refs_1_, bf16[256,1024]{1,0:T(8,128)(2,1)S(1)} %collective-permute-done.4.refs_2_, bf16[256,1024]{1,0:T(8,128)(2,1)S(1)} %collective-permute-done.8.refs_3_, ...), custom_call_target="tpu_custom_call" | custom-call | flops 8589934592 | bytes 14680064 | tf_op jit(solution)/shard_map/last/pallas_call | solution.py:257
  (74 shorter events, 13.0 us)
Async XLA Ops:
  4.5 63.5 %collective-permute-start.10 = (bf16[512,1024]{1,0:T(8,128)(2,1)S(1)}, bf16[512,1024]{1,0:T(8,128)(2,1)S(1)}, u32[]{:S(2)}, u32[]{:S(2)}) collective-permute-start(bf16[512,1024]{1,0:T(8,128)(2,1)S(1)} %constant_dynamic-update-slice_fusion.refs_2_.refs_10_.refs_18_.refs_3_.refs_11_.refs_4_.refs_12_.refs_20_), channel_id=1, source_target_pairs={{0,2},{1,3},{2,4},{3,5},{4,6},{5,7},{6,0},{7,1},{8,10},{9,11},{10,... | collective-permute-start | bytes 3145736 | tf_op jit(solution)/shard_map/ppermute | solution.py:285
  6.6 63.1 %collective-permute-start.12 = (bf16[512,1024]{1,0:T(8,128)(2,1)S(1)}, bf16[512,1024]{1,0:T(8,128)(2,1)S(1)}, u32[]{:S(2)}, u32[]{:S(2)}) collective-permute-start(bf16[512,1024]{1,0:T(8,128)(2,1)S(1)} %constant_dynamic-update-slice_fusion.refs_2_.refs_10_.refs_18_.refs_3_.refs_11_.refs_4_.refs_12_.refs_20_), channel_id=1, source_target_pairs={{0,6},{1,7},{2,0},{3,1},{4,2},{5,3},{6,4},{7,5},{8,14},{9,15},{10,... | collective-permute-start | bytes 3145736 | tf_op jit(solution)/shard_map/ppermute | solution.py:285
  7.5 11.1 %collective-permute-start = (bf16[64,1024]{1,0:T(8,128)(2,1)S(1)}, bf16[64,1024]{1,0:T(8,128)(2,1)S(1)}, u32[]{:S(2)}, u32[]{:S(2)}) collective-permute-start(bf16[64,1024]{1,0:T(8,128)(2,1)S(1)} %slice_bitcast_fusion), channel_id=1, source_target_pairs={{0,8},{8,16},{16,24},{24,32},{32,40},{40,48},{48,56},{56,64},{64,7... | collective-permute-start | bytes 393224 | tf_op jit(solution)/shard_map/ppermute | solution.py:280
  22.9 56.0 %copy-start.13 = (bf16[256,1024]{1,0:T(8,128)(2,1)}, bf16[256,1024]{1,0:T(8,128)(2,1)S(1)}, u32[]{:S(2)}) copy-start(bf16[256,1024]{1,0:T(8,128)(2,1)S(1)} %get-tuple-element.10.refs_0_) | copy-start | bytes 1572868
  22.9 39.8 %collective-permute-start.1 = (bf16[256,1024]{1,0:T(8,128)(2,1)S(1)}, bf16[256,1024]{1,0:T(8,128)(2,1)S(1)}, u32[]{:S(2)}, u32[]{:S(2)}) collective-permute-start(bf16[256,1024]{1,0:T(8,128)(2,1)S(1)} %get-tuple-element.10.refs_0_), channel_id=1, source_target_pairs={{0,8},{8,16},{16,24},{24,32},{32,40},{40,48},{48,56},{56,64},{64,7... | collective-permute-start | bytes 1572872 | tf_op jit(solution)/shard_map/ppermute | solution.py:280
  22.9 55.0 %collective-permute-start.9 = (bf16[512,1024]{1,0:T(8,128)(2,1)S(1)}, bf16[512,1024]{1,0:T(8,128)(2,1)S(1)}, u32[]{:S(2)}, u32[]{:S(2)}) collective-permute-start(bf16[512,1024]{1,0:T(8,128)(2,1)S(1)} %constant_dynamic-update-slice_fusion.refs_2_.refs_10_.refs_18_.refs_3_.refs_11_.refs_4_.refs_12_.refs_20_), channel_id=1, source_target_pairs={{0,1},{1,0},{2,3},{3,2},{4,5},{5,4},{6,7},{7,6},{8,9},{9,8},{10,11... | collective-permute-start | bytes 3145736 | tf_op jit(solution)/shard_map/ppermute | solution.py:289
  24.1 54.7 %copy-start.12 = (bf16[256,1024]{1,0:T(8,128)(2,1)}, bf16[256,1024]{1,0:T(8,128)(2,1)S(1)}, u32[]{:S(2)}) copy-start(bf16[256,1024]{1,0:T(8,128)(2,1)S(1)} %get-tuple-element.9) | copy-start | bytes 1572868
  24.1 54.7 %copy-start.15 = (bf16[256,1024]{1,0:T(8,128)(2,1)}, bf16[256,1024]{1,0:T(8,128)(2,1)S(1)}, u32[]{:S(2)}) copy-start(bf16[256,1024]{1,0:T(8,128)(2,1)S(1)} %get-tuple-element.11.refs_1_) | copy-start | bytes 1572868
  24.2 38.5 %collective-permute-start.5 = (bf16[256,1024]{1,0:T(8,128)(2,1)S(1)}, bf16[256,1024]{1,0:T(8,128)(2,1)S(1)}, u32[]{:S(2)}, u32[]{:S(2)}) collective-permute-start(bf16[256,1024]{1,0:T(8,128)(2,1)S(1)} %get-tuple-element.11.refs_1_), channel_id=1, source_target_pairs={{0,32},{8,40},{16,48},{24,56},{32,64},{40,72},{48,80},{56,88},{64,... | collective-permute-start | bytes 1572872 | tf_op jit(solution)/shard_map/ppermute | solution.py:280
  62.7 15.2 %collective-permute-start.2 = (bf16[256,1024]{1,0:T(8,128)(2,1)S(1)}, bf16[256,1024]{1,0:T(8,128)(2,1)}, u32[]{:S(2)}, u32[]{:S(2)}) collective-permute-start(bf16[256,1024]{1,0:T(8,128)(2,1)S(1)} %collective-permute-done.1.refs_1_), channel_id=1, source_target_pairs={{0,8},{8,16},{16,24},{24,32},{32,40},{40,48},{48,56},{56,64},{64,7... | collective-permute-start | bytes 1572872 | tf_op jit(solution)/shard_map/ppermute | solution.py:280
  62.7 16.1 %collective-permute-start.6 = (bf16[256,1024]{1,0:T(8,128)(2,1)S(1)}, bf16[256,1024]{1,0:T(8,128)(2,1)S(1)}, u32[]{:S(2)}, u32[]{:S(2)}) collective-permute-start(bf16[256,1024]{1,0:T(8,128)(2,1)S(1)} %collective-permute-done.5.refs_2_), channel_id=1, source_target_pairs={{0,248},{8,0},{16,8},{24,16},{32,24},{40,32},{48,40},{56,48},{64,5... | collective-permute-start | bytes 1572872 | tf_op jit(solution)/shard_map/ppermute | solution.py:280
  68.8 11.3 %collective-permute-start.14 = (bf16[256,1024]{1,0:T(8,128)(2,1)}, bf16[256,1024]{1,0:T(8,128)(2,1)}, u32[]{:S(2)}, u32[]{:S(2)}) collective-permute-start(bf16[256,1024]{1,0:T(8,128)(2,1)} %slice.38), channel_id=1, source_target_pairs={{0,2},{1,3},{2,4},{3,5},{4,6},{5,7},{6,0},{7,1},{8,10},{9,11},{10,... | collective-permute-start | bytes 1572872 | tf_op jit(solution)/shard_map/ppermute | solution.py:285
  70.5 15.0 %collective-permute-start.16 = (bf16[256,1024]{1,0:T(8,128)(2,1)}, bf16[256,1024]{1,0:T(8,128)(2,1)}, u32[]{:S(2)}, u32[]{:S(2)}) collective-permute-start(bf16[256,1024]{1,0:T(8,128)(2,1)} %slice.39), channel_id=1, source_target_pairs={{0,6},{1,7},{2,0},{3,1},{4,2},{5,3},{6,4},{7,5},{8,14},{9,15},{10,... | collective-permute-start | bytes 1572872 | tf_op jit(solution)/shard_map/ppermute | solution.py:285
  77.8 12.8 %collective-permute-start.3 = (bf16[256,1024]{1,0:T(8,128)(2,1)}, bf16[256,1024]{1,0:T(8,128)(2,1)}, u32[]{:S(2)}, u32[]{:S(2)}) collective-permute-start(bf16[256,1024]{1,0:T(8,128)(2,1)} %collective-permute-done.2.refs_1_), channel_id=1, source_target_pairs={{0,8},{8,16},{16,24},{24,32},{32,40},{40,48},{48,56},{56,64},{64,7... | collective-permute-start | bytes 1572872 | tf_op jit(solution)/shard_map/ppermute | solution.py:280
  78.8 24.2 %collective-permute-start.11 = (bf16[512,1024]{1,0:T(8,128)(2,1)S(1)}, bf16[512,1024]{1,0:T(8,128)(2,1)}, u32[]{:S(2)}, u32[]{:S(2)}) collective-permute-start(bf16[512,1024]{1,0:T(8,128)(2,1)S(1)} %collective-permute-done.10.refs_4_.refs_12_.refs_20_.refs_5_.refs_13_.refs_6_.refs_14_.refs_22_), channel_id=1, source_target_pairs={{0,1},{1,0},{2,3},{3,2},{4,5},{5,4},{6,7},{7,6},{8,9},{9,8},{10,11... | collective-permute-start | bytes 3145736 | tf_op jit(solution)/shard_map/ppermute | solution.py:289
  79.7 23.3 %collective-permute-start.13 = (bf16[512,1024]{1,0:T(8,128)(2,1)S(1)}, bf16[512,1024]{1,0:T(8,128)(2,1)}, u32[]{:S(2)}, u32[]{:S(2)}) collective-permute-start(bf16[512,1024]{1,0:T(8,128)(2,1)S(1)} %collective-permute-done.12.refs_6_.refs_14_.refs_22_.refs_7_.refs_15_.refs_8_.refs_16_.refs_24_), channel_id=1, source_target_pairs={{0,1},{1,0},{2,3},{3,2},{4,5},{5,4},{6,7},{7,6},{8,9},{9,8},{10,11... | collective-permute-start | bytes 3145736 | tf_op jit(solution)/shard_map/ppermute | solution.py:289
  80.2 17.0 %collective-permute-start.7 = (bf16[256,1024]{1,0:T(8,128)(2,1)}, bf16[256,1024]{1,0:T(8,128)(2,1)}, u32[]{:S(2)}, u32[]{:S(2)}) collective-permute-start(bf16[256,1024]{1,0:T(8,128)(2,1)} %copy-done.9), channel_id=1, source_target_pairs={{0,248},{8,0},{16,8},{24,16},{32,24},{40,32},{48,40},{56,48},{64,5... | collective-permute-start | bytes 1572872 | tf_op jit(solution)/shard_map/ppermute | solution.py:280
  85.5 11.7 %collective-permute-start.15 = (bf16[256,1024]{1,0:T(8,128)(2,1)}, bf16[256,1024]{1,0:T(8,128)(2,1)}, u32[]{:S(2)}, u32[]{:S(2)}) collective-permute-start(bf16[256,1024]{1,0:T(8,128)(2,1)} %collective-permute-done.14.refs_8_.refs_16_.refs_9_.refs_10_), channel_id=1, source_target_pairs={{0,1},{1,0},{2,3},{3,2},{4,5},{5,4},{6,7},{7,6},{8,9},{9,8},{10,11... | collective-permute-start | bytes 1572872 | tf_op jit(solution)/shard_map/ppermute | solution.py:289
  90.6 12.4 %collective-permute-start.17 = (bf16[256,1024]{1,0:T(8,128)(2,1)}, bf16[256,1024]{1,0:T(8,128)(2,1)}, u32[]{:S(2)}, u32[]{:S(2)}) collective-permute-start(bf16[256,1024]{1,0:T(8,128)(2,1)} %collective-permute-done.16.refs_24_.refs_17_.refs_18_.refs_26_), channel_id=1, source_target_pairs={{0,1},{1,0},{2,3},{3,2},{4,5},{5,4},{6,7},{7,6},{8,9},{9,8},{10,11... | collective-permute-start | bytes 1572872 | tf_op jit(solution)/shard_map/ppermute | solution.py:289
  90.9 30.0 %copy-start.2 = (bf16[512,1024]{1,0:T(8,128)(2,1)S(1)}, bf16[512,1024]{1,0:T(8,128)(2,1)}, u32[]{:S(2)}) copy-start(bf16[512,1024]{1,0:T(8,128)(2,1)} %copy-done) | copy-start | bytes 3145732
  90.9 30.0 %copy-start.6 = (bf16[256,1024]{1,0:T(8,128)(2,1)S(1)}, bf16[256,1024]{1,0:T(8,128)(2,1)}, u32[]{:S(2)}) copy-start(bf16[256,1024]{1,0:T(8,128)(2,1)} %copy-done.5) | copy-start | bytes 1572868
  90.9 30.0 %copy-start.8 = (bf16[256,1024]{1,0:T(8,128)(2,1)S(1)}, bf16[256,1024]{1,0:T(8,128)(2,1)}, u32[]{:S(2)}) copy-start(bf16[256,1024]{1,0:T(8,128)(2,1)} %copy-done.7) | copy-start | bytes 1572868
  97.2 59.2 %collective-permute-start.4 = (bf16[256,1024]{1,0:T(8,128)(2,1)}, bf16[256,1024]{1,0:T(8,128)(2,1)S(1)}, u32[]{:S(2)}, u32[]{:S(2)}) collective-permute-start(bf16[256,1024]{1,0:T(8,128)(2,1)} %collective-permute-done.3.refs_1_), channel_id=1, source_target_pairs={{0,8},{8,16},{16,24},{24,32},{32,40},{40,48},{48,56},{56,64},{64,7... | collective-permute-start | bytes 1572872 | tf_op jit(solution)/shard_map/ppermute | solution.py:280
  97.2 59.2 %collective-permute-start.8 = (bf16[256,1024]{1,0:T(8,128)(2,1)}, bf16[256,1024]{1,0:T(8,128)(2,1)S(1)}, u32[]{:S(2)}, u32[]{:S(2)}) collective-permute-start(bf16[256,1024]{1,0:T(8,128)(2,1)} %collective-permute-done.7.refs_2_), channel_id=1, source_target_pairs={{0,248},{8,0},{16,8},{24,16},{32,24},{40,32},{48,40},{56,48},{64,5... | collective-permute-start | bytes 1572872 | tf_op jit(solution)/shard_map/ppermute | solution.py:280
  (11 other events, 52.0 us)

commit v2 on v1

v2 whole, which is shorter than its diff:
```python
import functools

import jax
import jax.numpy as jnp
from jax import lax
from jax.experimental import pallas as pl
from jax.experimental.pallas import tpu as pltpu
from jax.sharding import PartitionSpec as P

HEAD_DIM = 64
TAIL = 64
PAIR = 2 * HEAD_DIM
QUAD = 2 * PAIR
HALF = 256
UPPER = 256
BLOCK = 512
EPS = 1e-6
QUERY_FACTOR = 16.0 / HEAD_DIM * 1.4426950408889634
BF = jnp.bfloat16
F32 = jnp.float32
VMEM_WHOLE = pl.BlockSpec(memory_space=pltpu.VMEM)
SMEM_WHOLE = pl.BlockSpec(memory_space=pltpu.SMEM)
SMALL = pl.CostEstimate(flops=1, bytes_accessed=1, transcendentals=0)
TOKEN = jax.ShapeDtypeStruct((8, 128), F32)
NT = (((1,), (1,)), ((), ()))
VMEM_LIMIT = 60 * 2**20


def params():
    return pltpu.CompilerParams(vmem_limit_bytes=VMEM_LIMIT)


def prep_kernel(order_ref, win_ref, bytes_ref, carried_ref, groups_ref, out_ref, upper_ref, lower_ref, hold):
    rows, width = bytes_ref.shape
    start, following = win_ref[0:1, :], win_ref[1:2, :]

    def one_hot(lo, hi):
        position = lax.broadcasted_iota(jnp.int32, (rows, hi - lo), 0)
        return ((start[:, lo:hi] <= position) & (following[:, lo:hi] > position)).astype(F32).astype(BF)

    own = groups_ref.shape[0]
    lifted = jnp.dot(one_hot(PAIR, PAIR + own), groups_ref[...], preferred_element_type=F32)
    lifted += jnp.dot(one_hot(0, TAIL), carried_ref[...], preferred_element_type=F32)
    dechunked = (bytes_ref[...].astype(F32) + lifted).astype(BF)
    out_ref[...] = dechunked
    wide = dechunked.astype(F32)
    mean = jnp.sum(wide * wide, axis=-1, keepdims=True) * (1.0 / width)
    hold[...] = (wide * lax.rsqrt(mean + EPS)).astype(BF)
    for r in range(width // PAIR):
        at = pl.multiple_of(order_ref[r] * PAIR, PAIR)
        upper_ref[:, r * PAIR : (r + 1) * PAIR] = hold[:UPPER, pl.ds(at, PAIR)]
        lower_ref[:, r * PAIR : (r + 1) * PAIR] = hold[UPPER:, pl.ds(at, PAIR)]


def whole(shape):
    return pl.BlockSpec(shape, lambda *_: (0,) * len(shape))


def prep(order, window, own_bytes, carried, own_groups):
    rows, width = own_bytes.shape
    shapes = [(rows, width), (UPPER, width), (rows - UPPER, width)]
    return pl.pallas_call(
        prep_kernel,
        grid=(1,),
        in_specs=[SMEM_WHOLE] + [whole(x.shape) for x in (window, own_bytes, carried, own_groups)],
        out_specs=[whole(shape) for shape in shapes],
        out_shape=[jax.ShapeDtypeStruct(shape, BF) for shape in shapes],
        scratch_shapes=[pltpu.VMEM((rows, width), BF)],
        compiler_params=params(),
        cost_estimate=SMALL,
        name="prep",
    )(order, window, own_bytes, carried, own_groups)


def stack_kernel(*refs):
    out_ref = refs[-1]
    rows = refs[0].shape[0]
    for i, ref in enumerate(refs[:-1]):
        out_ref[i * rows : (i + 1) * rows] = ref[...]


def stack(*arrays):
    rows, width = arrays[0].shape
    shape = (len(arrays) * rows, width)
    return pl.pallas_call(
        stack_kernel,
        grid=(1,),
        in_specs=[whole((rows, width))] * len(arrays),
        out_specs=whole(shape),
        out_shape=jax.ShapeDtypeStruct(shape, BF),
        compiler_params=params(),
        cost_estimate=SMALL,
        name="stack",
    )(*arrays)


def head_norm(raw, factor):
    n = raw.shape[1]
    row = lax.broadcasted_iota(jnp.int32, (n, n), 0) // HEAD_DIM
    column = lax.broadcasted_iota(jnp.int32, (n, n), 1) // HEAD_DIM
    mean_of_head = jnp.where(row == column, 1.0 / HEAD_DIM, 0.0).astype(BF)
    mean_square = jnp.dot((raw * raw).astype(BF), mean_of_head, preferred_element_type=F32)
    return (raw * (lax.rsqrt(mean_square + EPS) * factor)).astype(BF)


def project(x, weight):
    return jnp.dot(x, weight, preferred_element_type=F32)


def joined(refs):
    return jnp.concatenate([r[...] for r in refs], axis=0)


def weights_of(scores, keep):
    weights = jnp.exp2(scores)
    if keep is not None:
        weights = jnp.where(keep, weights, 0.0)
    return weights.astype(BF)


def attend_quad(query, key, value, ones, plan, put):
    low = lax.broadcasted_iota(jnp.int32, ones.shape, 1) < HEAD_DIM
    low_q = low[:HALF]
    zero = jnp.zeros(ones.shape, BF)
    zero_q = zero[:HALF]
    for pair in range(2):
        lanes = slice(pair * PAIR, (pair + 1) * PAIR)
        k, v = key[:, lanes], value[:, lanes]
        right_a = jnp.concatenate([jnp.where(low, v, zero), jnp.where(low, ones, zero)], axis=1)
        right_b = jnp.concatenate([jnp.where(low, zero, v), jnp.where(low, zero, ones)], axis=1)
        for part in range(2):
            rows = slice(part * HALF, (part + 1) * HALF)
            q = query[rows, lanes]
            left, right = [], []
            for begin, end, rule in plan[part]:
                keep = None
                if rule is not None:
                    shape = (HALF, end - begin)
                    i = part * HALF + lax.broadcasted_iota(jnp.int32, shape, 0)
                    keep = rule(i, begin + lax.broadcasted_iota(jnp.int32, shape, 1))
                for q_head, v_head in (
                    (jnp.where(low_q, q, zero_q), right_a),
                    (jnp.where(low_q, zero_q, q), right_b),
                ):
                    scores = lax.dot_general(q_head, k[begin:end], NT, preferred_element_type=F32)
                    left.append(weights_of(scores, keep))
                    right.append(v_head[begin:end])
            total = jnp.dot(
                jnp.concatenate(left, axis=1), jnp.concatenate(right, axis=0), preferred_element_type=F32
            )
            put(pair, rows, total)


def until(i, j):
    return j <= i


def since(i, j):
    return j >= i


FIRST_PLAN = (
    ((0, HALF, until), (BLOCK, BLOCK + UPPER, None)),
    ((0, HALF, None), (HALF, BLOCK, until), (BLOCK, BLOCK + UPPER, None)),
)
SECOND_PLAN = (
    ((0, BLOCK, None),),
    ((0, UPPER, None), (UPPER, BLOCK, since)),
)
FULL_PLAN = (((0, BLOCK, None),),) * 2
LAST_PLAN = (
    ((0, UPPER, since), (UPPER, 3 * HALF, None)),
    ((UPPER, 3 * HALF, None),),
)


def keys_of(x, w_k, w_v, valid_ref, valid):
    key = head_norm(project(x, joined(w_k)), 1.0)
    value = project(x, joined(w_v))
    values, ones = [], []
    for n, place in enumerate(valid):
        part, one = value[n * HALF : (n + 1) * HALF], jnp.ones((HALF, PAIR), F32)
        if place is not None:
            counts = valid_ref[place] > 0
            part, one = jnp.where(counts, part, 0.0), jnp.where(counts, one, 0.0)
        values.append(part.astype(BF))
        ones.append(one.astype(BF))
    return key, jnp.concatenate(values, axis=0), jnp.concatenate(ones, axis=0)


def first_kernel(*refs):
    valid_ref = refs[0]
    w_q, w_k, w_v = refs[4:12], refs[12:20], refs[20:28]
    query_ref, total_ref, token_ref = refs[28:]
    token_ref[...] = jnp.zeros_like(token_ref)
    x = joined(refs[1:4])
    query = head_norm(project(x[:BLOCK], joined(w_q)), QUERY_FACTOR)
    query_ref[...] = query

    def put(pair, rows, total):
        total_ref[pair, rows, :] = total

    attend_quad(query, *keys_of(x, w_k, w_v, valid_ref, (None, None, 0)), FIRST_PLAN, put)


def step_kernel(plan, valid, *refs):
    n = len(valid)
    valid_ref, rows = refs[0], refs[1 : 1 + n]
    w_k, w_v = refs[1 + n : 9 + n], refs[9 + n : 17 + n]
    query_ref, total_ref, _, out_ref, token_ref = refs[17 + n :]
    token_ref[...] = jnp.zeros_like(token_ref)

    def put(pair, rows, total):
        out_ref[pair, rows, :] = total_ref[pair, rows, :] + total

    attend_quad(query_ref[...], *keys_of(joined(rows), w_k, w_v, valid_ref, valid), plan, put)


def last_kernel(plan, valid, *refs):
    n = len(valid)
    valid_ref, order_ref, rows = refs[0], refs[1], refs[2 : 2 + n]
    w_k, w_v, w_out = refs[2 + n : 10 + n], refs[10 + n : 18 + n], refs[18 + n : 20 + n]
    query_ref, total_ref, _, out_ref, context = refs[20 + n :]
    g = pl.program_id(0)

    def put(pair, rows, total):
        total = total_ref[pair, rows, :] + total
        context[2 * g + pair, rows, :] = (total[:, :PAIR] / total[:, PAIR:]).astype(BF)

    attend_quad(query_ref[...], *keys_of(joined(rows), w_k, w_v, valid_ref, valid), plan, put)

    @pl.when(g == pl.num_programs(0) - 1)
    def _():
        x = jnp.concatenate([context[order_ref[r]] for r in (0, 2, 4, 6, 1, 3, 5, 7)], axis=1)
        out_ref[...] = project(x, joined(w_out)).astype(BF)


def weight_specs(parts, kind):
    return [pl.BlockSpec((PAIR, QUAD), lambda g: (kind, g))] * len(parts)


QUERY_SPEC = pl.BlockSpec((BLOCK, QUAD), lambda g: (0, g))
TOTAL_SPEC = pl.BlockSpec((2, BLOCK, QUAD), lambda g: (g, 0, 0))


def attend_first(valid, rows, parts):
    width = rows[0].shape[1]
    return pl.pallas_call(
        first_kernel,
        grid=(width // QUAD,),
        in_specs=[SMEM_WHOLE]
        + [whole(x.shape) for x in rows]
        + weight_specs(parts, 0)
        + weight_specs(parts, 1)
        + weight_specs(parts, 2),
        out_specs=[QUERY_SPEC, TOTAL_SPEC, whole(TOKEN.shape)],
        out_shape=[
            jax.ShapeDtypeStruct((BLOCK, width), BF),
            jax.ShapeDtypeStruct((width // PAIR, BLOCK, QUAD), F32),
            TOKEN,
        ],
        compiler_params=params(),
        cost_estimate=SMALL,
        name="first",
    )(valid, *rows, *parts, *parts, *parts)


def attend_step(plan, places, valid, rows, parts, query, total, token):
    width = rows[0].shape[1]
    return pl.pallas_call(
        functools.partial(step_kernel, plan, places),
        grid=(width // QUAD,),
        in_specs=[SMEM_WHOLE]
        + [whole(x.shape) for x in rows]
        + weight_specs(parts, 1)
        + weight_specs(parts, 2)
        + [QUERY_SPEC, TOTAL_SPEC, pl.BlockSpec(memory_space=pl.ANY)],
        out_specs=[TOTAL_SPEC, whole(TOKEN.shape)],
        out_shape=[jax.ShapeDtypeStruct(total.shape, F32), TOKEN],
        compiler_params=params(),
        cost_estimate=SMALL,
        name="step",
    )(valid, *rows, *parts, *parts, query, total, token)


def attend_last(plan, places, valid, order, rows, parts, w_out, query, total, token):
    width = rows[0].shape[1]
    return pl.pallas_call(
        functools.partial(last_kernel, plan, places),
        grid=(width // QUAD,),
        in_specs=[SMEM_WHOLE] * 2
        + [whole(x.shape) for x in rows]
        + weight_specs(parts, 1)
        + weight_specs(parts, 2)
        + [whole(w.shape) for w in w_out]
        + [QUERY_SPEC, TOTAL_SPEC, pl.BlockSpec(memory_space=pl.ANY)],
        out_specs=whole((BLOCK, width)),
        out_shape=jax.ShapeDtypeStruct((BLOCK, width), BF),
        scratch_shapes=[pltpu.VMEM((width // PAIR, BLOCK, PAIR), BF)],
        compiler_params=params(),
        cost_estimate=SMALL,
        name="last",
    )(valid, order, *rows, *parts, *parts, *w_out, query, total, token)


def along_seq(block, distance):
    count = lax.axis_size("seq")
    return lax.ppermute(block, "seq", [(i, (i + distance) % count) for i in range(count)])


def over_fsdp(block, dy, other):
    count = lax.axis_size("fsdp")
    return lax.ppermute(block, "fsdp", [(i, (i // 2 * 2 + 2 * dy) % count + (i + other) % 2) for i in range(count)])


def together(*arrays):
    return lax.optimization_barrier(arrays)


def gather_parts(rows):
    return [rows] + [over_fsdp(rows, dy, 0) for dy in (1, -1, 2)]


def weight_order():
    me = lax.axis_index("fsdp")
    y, core = me // 2, me % 2
    return jnp.stack(
        [2 * ((y + dy) % 4) + (core + other) % 2 for dy in (0, 3, 1, 2) for other in (0, 1)]
    ).astype(jnp.int32)


def local(byte_states, group_states, boundaries, w_query, w_key, w_value, w_out):
    own_bytes, own_groups, starts = byte_states[0], group_states[0], boundaries[0]
    rows, width = own_bytes.shape
    owned = own_groups.shape[0]
    position = lax.axis_index("seq")
    order = weight_order()
    valid = jnp.stack([position >= k for k in range(1, 5)]).astype(jnp.int32)

    tail, w_query, w_key, w_value = together(own_groups[owned - TAIL :], w_query, w_key, w_value)
    carried = along_seq(tail, 1)
    packed = stack(w_query, w_key, w_value)
    own_core = gather_parts(packed)

    far = jnp.int32(2**30)
    padded = jnp.concatenate([jnp.zeros((TAIL,), jnp.int32), starts, jnp.full((1,), far, jnp.int32)])
    window = lax.dynamic_slice_in_dim(padded, position * owned, owned + TAIL + 1, 0) - position * rows
    begin, end = window[:-1], window[1:]
    gap = jnp.full((PAIR - TAIL,), far, jnp.int32)
    window = jnp.stack([jnp.concatenate([w[:TAIL], gap, w[TAIL:]]) for w in (begin, end)])

    dechunked, upper, lower = prep(order, window, own_bytes, carried, own_groups)

    up, down = {1: along_seq(upper, 1)}, {4: along_seq(lower, 4)}
    other = [over_fsdp(part, 0, 1) for part in own_core[:3]]
    own_core[3], up[1], down[4] = together(own_core[3], up[1], down[4])
    other.append(over_fsdp(own_core[3], 0, 1))

    other[3], w_out = together(other[3], w_out)
    w_out_core = gather_parts(w_out)
    up[2], down[3] = along_seq(up[1], 1), along_seq(down[4], -1)
    parts = [part for pair in zip(own_core, other) for part in pair]
    query, total, token = attend_first(valid, (upper, lower, up[1]), parts)

    up[2], down[3], token, *w_out_core = together(up[2], down[3], token, *w_out_core)
    up[3], down[2] = along_seq(up[2], 1), along_seq(down[3], -1)
    token, w_out_core = together(token, stack(*w_out_core))
    w_out = w_out_core, over_fsdp(w_out_core, 0, 1)
    rows = (up[2], down[4])
    total, token = attend_step(SECOND_PLAN, (1, 3), valid, rows, parts, query, total, token)

    up[3], down[2], token = together(up[3], down[2], token)
    up[4], down[1] = along_seq(up[3], 1), along_seq(down[2], -1)
    rows = (up[3], down[3])
    total, token = attend_step(FULL_PLAN, (2, 2), valid, rows, parts, query, total, token)

    rows = (up[4], down[2], down[1])
    attended = attend_last(LAST_PLAN, (3, 1, 0), valid, order, rows, parts, w_out, query, total, token)
    return dechunked[None], attended[None]


def solution(mesh):
    placed = (P("fsdp", "seq", None),) * 2 + (P("fsdp", None),) * 5
    return jax.shard_map(
        local,
        mesh=mesh,
        in_specs=placed,
        out_specs=(P("fsdp", "seq", None), P("fsdp", "seq", None)),
        check_vma=False,
    )
```

time: 169 us -> 148 us (0.88); the launches traced: 169 us -> 145 us
  waiting for transfers between devices: 59 us -> 38 us
  local copies, waits for them, and re-layouts: 15.6 us -> 5.37 us
  Pallas kernels: 64.8 us -> 69.8 us
  starting transfers between devices: 25.6 us -> 29.4 us
    ppermute x9, waiting for transfers between devices: 59 us -> 36.6 us  [along_seq(): lax.ppermute(block, 'seq', [(i, (i + distance) % count) for i in range(co...]
    unnamed x37 -> x28, local copies, waits for them, and re-layouts: 11 us -> 2.87 us
    pallas_call x7, Pallas kernels: 64.8 us -> 69.8 us  [the longest x2 25.7 us: attend_step(): pl.pallas_call(functools.partial(step_kernel, plan, places), grid=(width...]
    ppermute x9 -> x11, starting transfers between devices: 4.64 us -> 9.25 us  [over_fsdp(): lax.ppermute(block, 'fsdp', [(i, (i // 2 * 2 + 2 * dy) % count + (i + oth...]
    broadcast_in_dim x1 -> x0, other arithmetic: 2.39 us -> none  [local(): return (dechunked[None], attended[None])]
  transfers between devices with their start and end apart: 18 -> 20, of which waited for: 5 -> 3; matrix products, arithmetic and copies ran while one was open for 4% -> 2% of each run, Pallas kernels for 31% -> 36%
where the time goes in v2:
time: 148 us; the launch traced here: 145 us
  Pallas kernels  69.8 us (47%)
  waiting for transfers between devices  38 us (26%)
  starting transfers between devices  29.4 us (20%)
  local copies, waits for them, and re-layouts  5.37 us (4%)
    ppermute x9, waiting for transfers between devices, along_seq(): lax.ppermute(block, 'seq', [(i, (i + distance) % count) for i in range(co...  36.6 us
    pallas_call x2, Pallas kernels, attend_step(): pl.pallas_call(functools.partial(step_kernel, plan, places), grid=(width...  25.7 us
    ppermute x9, starting transfers between devices, along_seq(): lax.ppermute(block, 'seq', [(i, (i + distance) % count) for i in range(co...  20.2 us
    pallas_call x1, Pallas kernels, attend_first(): pl.pallas_call(first_kernel, grid=(width // QUAD,), in_specs=[SMEM_WHOLE]...  19.2 us
    pallas_call x1, Pallas kernels, attend_last(): pl.pallas_call(functools.partial(last_kernel, plan, places), grid=(width...  17.3 us
    ppermute x11, starting transfers between devices, over_fsdp(): lax.ppermute(block, 'fsdp', [(i, (i // 2 * 2 + 2 * dy) % count + (i + oth...  9.25 us
    pallas_call x2, Pallas kernels, stack(): pl.pallas_call(stack_kernel, grid=(1,), in_specs=[whole((rows, width))] *...  4.29 us
    pallas_call x1, Pallas kernels, prep(): pl.pallas_call(prep_kernel, grid=(1,), in_specs=[SMEM_WHOLE] + [whole(x.s...  3.38 us
  transfers between devices with their start and end apart: 20, of which 3 were waited for; matrix products, arithmetic and copies ran while one was open for 2% of the time, Pallas kernels for 36%

profile of v2, /device:TPU:24, one launch (start us, length us, event | category | flops | bytes accessed | tf_op | source)
XLA Modules:
  0.0 145.0 jit_solution(16250091497048755201)
XLA Ops:
  0.6 0.9 slice_bitcast_fusion
  1.5 2.0 %collective-permute-start = (bf16[64,1024]{1,0:T(8,128)(2,1)S(1)}, bf16[64,1024]{1,0:T(8,128)(2,1)S(1)}, u32[]{:S(2)}, u32[]{:S(2)}) collective-permute-start(bf16[64,1024]{1,0:T(8,128)(2,1)S(1)} %slice_bitcast_fusion), channel_id=1, source_target_pairs={{0,8},{8,16},{16,24},{24,32},{32,40},{40,48},{48,56},{56,64},{64,7... | collective-permute-start | bytes 393224 | tf_op jit(solution)/shard_map/ppermute | solution.py:308
  3.5 2.0 %stack.70.refs_4_.refs_12_.refs_20_.refs_3_.refs_11_.refs_5_.refs_13_ = bf16[384,1024]{1,0:T(8,128)(2,1)} custom-call(bf16[128,1024]{1,0:T(8,128)(2,1)} %refs_0_, bf16[128,1024]{1,0:T(8,128)(2,1)} %refs_1_, bf16[128,1024]{1,0:T(8,128)(2,1)} %refs_2_), custom_call_target="tpu_custom_call" | custom-call | flops 1 | bytes 1 | tf_op jit(solution)/shard_map/stack/pallas_call | solution.py:85
  5.6 1.2 collective-permute-start.1
  6.8 0.8 concatenate.9
  9.2 4.0 %collective-permute-done.carried_ref = bf16[64,1024]{1,0:T(8,128)(2,1)S(1)} collective-permute-done((bf16[64,1024]{1,0:T(8,128)(2,1)S(1)}, bf16[64,1024]{1,0:T(8,128)(2,1)S(1)}, u32[]{:S(2)}, u32[]{:S(2)}) %collective-permute-start) | collective-permute-done | bytes 131104 | tf_op jit(solution)/shard_map/ppermute | solution.py:308
  13.2 0.7 copy-done.13
  13.8 3.4 %prep.1 = (bf16[512,1024]{1,0:T(8,128)(2,1)}, bf16[256,1024]{1,0:T(8,128)(2,1)}, bf16[256,1024]{1,0:T(8,128)(2,1)}) custom-call(s32[8]{0:T(128)} %stack.61.order_ref.refs_1_, s32[2,256]{1,0:T(2,128)} %pad_add_fusion.win_ref, bf16[512,1024]{1,0:T(8,128)(2,1)} %bitcast.22, bf16[64,1024]{1,0:T(8,128)(2,1)} %copy-done.13, bf16[128,1024]{1,0:T(8,128)(2,1)} %bitcast.23), custom_call_target="tpu_custom_call" | custom-call | flops 1 | bytes 1 | tf_op jit(solution)/shard_map/prep/pallas_call | solution.py:62
  17.2 3.3 %collective-permute-start.3 = (bf16[256,1024]{1,0:T(8,128)(2,1)}, bf16[256,1024]{1,0:T(8,128)(2,1)}, u32[]{:S(2)}, u32[]{:S(2)}) collective-permute-start(bf16[256,1024]{1,0:T(8,128)(2,1)} %get-tuple-element.39.refs_2_), channel_id=1, source_target_pairs={{0,32},{8,40},{16,48},{24,56},{32,64},{40,72},{48,80},{56,88},{64,... | collective-permute-start | bytes 1572872 | tf_op jit(solution)/shard_map/ppermute | solution.py:308
  20.6 3.2 %collective-permute-start.7 = (bf16[384,1024]{1,0:T(8,128)(2,1)}, bf16[384,1024]{1,0:T(8,128)(2,1)S(1)}, u32[]{:S(2)}, u32[]{:S(2)}) collective-permute-start(bf16[384,1024]{1,0:T(8,128)(2,1)} %stack.70.refs_4_.refs_12_.refs_20_.refs_3_.refs_11_.refs_5_.refs_13_), channel_id=1, source_target_pairs={{0,2},{1,3},{2,4},{3,5},{4,6},{5,7},{6,0},{7,1},{8,10},{9,11},{10,... | collective-permute-start | bytes 2359304 | tf_op jit(solution)/shard_map/ppermute | solution.py:313
  23.8 32.6 %collective-permute-done.2.refs_3_ = bf16[256,1024]{1,0:T(8,128)(2,1)} collective-permute-done((bf16[256,1024]{1,0:T(8,128)(2,1)}, bf16[256,1024]{1,0:T(8,128)(2,1)}, u32[]{:S(2)}, u32[]{:S(2)}) %collective-permute-start.2) | collective-permute-done | bytes 524320 | tf_op jit(solution)/shard_map/ppermute | solution.py:308
  57.6 1.4 collective-permute-done.11.refs_11_.refs_19_.refs_27_.refs_10_.refs_18_.refs_12_.refs_20_
  58.9 4.0 %collective-permute-start.5 = (bf16[256,1024]{1,0:T(8,128)(2,1)}, bf16[256,1024]{1,0:T(8,128)(2,1)}, u32[]{:S(2)}, u32[]{:S(2)}) collective-permute-start(bf16[256,1024]{1,0:T(8,128)(2,1)} %collective-permute-done.3.refs_2_), channel_id=1, source_target_pairs={{0,248},{8,0},{16,8},{24,16},{32,24},{40,32},{48,40},{56,48},{64,5... | collective-permute-start | bytes 1572872 | tf_op jit(solution)/shard_map/ppermute | solution.py:308
  62.9 2.0 %collective-permute-start.13 = (bf16[128,1024]{1,0:T(8,128)(2,1)}, bf16[128,1024]{1,0:T(8,128)(2,1)}, u32[]{:S(2)}, u32[]{:S(2)}) collective-permute-start(bf16[128,1024]{1,0:T(8,128)(2,1)} %refs_0_.1), channel_id=1, source_target_pairs={{0,6},{1,7},{2,0},{3,1},{4,2},{5,3},{6,4},{7,5},{8,14},{9,15},{10,... | collective-permute-start | bytes 786440 | tf_op jit(solution)/shard_map/ppermute | solution.py:313
  65.0 0.9 copy-done.6
  65.9 1.7 %collective-permute-start.14 = (bf16[128,1024]{1,0:T(8,128)(2,1)}, bf16[128,1024]{1,0:T(8,128)(2,1)}, u32[]{:S(2)}, u32[]{:S(2)}) collective-permute-start(bf16[128,1024]{1,0:T(8,128)(2,1)} %refs_0_.1), channel_id=1, source_target_pairs={{0,4},{1,5},{2,6},{3,7},{4,0},{5,1},{6,2},{7,3},{8,12},{9,13},{10,... | collective-permute-start | bytes 786440 | tf_op jit(solution)/shard_map/ppermute | solution.py:313
  68.1 19.2 %first.1 = (bf16[512,1024]{1,0:T(8,128)(2,1)}, f32[8,512,256]{2,1,0:T(8,128)}, f32[8,128]{1,0:T(8,128)}) custom-call(s32[4]{0:T(128)} %add_convert_fusion.refs_0_, bf16[256,1024]{1,0:T(8,128)(2,1)} %get-tuple-element.38.refs_1_, bf16[256,1024]{1,0:T(8,128)(2,1)} %get-tuple-element.39.refs_2_, bf16[256,1024]{1,0:T(8,128)(2,1)} %collective-permute-done.2.refs_3_, ...), custom_call_target="tpu_custom_call" | custom-call | flops 1 | bytes 1 | tf_op jit(solution)/shard_map/first/pallas_call | solution.py:248
  87.5 5.3 %collective-permute-start.16 = (bf16[256,1024]{1,0:T(8,128)(2,1)}, bf16[256,1024]{1,0:T(8,128)(2,1)S(1)}, u32[]{:S(2)}, u32[]{:S(2)}) collective-permute-start(bf16[256,1024]{1,0:T(8,128)(2,1)} %collective-permute-done.5.refs_2_), channel_id=1, source_target_pairs={{0,248},{8,0},{16,8},{24,16},{32,24},{40,32},{48,40},{56,48},{64,5... | collective-permute-start | bytes 1572872 | tf_op jit(solution)/shard_map/ppermute | solution.py:308
  92.8 2.2 %stack.71.refs_21_ = bf16[512,1024]{1,0:T(8,128)(2,1)} custom-call(bf16[128,1024]{1,0:T(8,128)(2,1)} %refs_0_.1, bf16[128,1024]{1,0:T(8,128)(2,1)} %copy-done.12, bf16[128,1024]{1,0:T(8,128)(2,1)} %collective-permute-done.13.refs_2_, bf16[128,1024]{1,0:T(8,128)(2,1)} %collective-permute-done.14.refs_3_), custom_call_target="tpu_custom_call" | custom-call | flops 1 | bytes 1 | tf_op jit(solution)/shard_map/stack/pallas_call | solution.py:85
  95.1 12.9 %step.2 = (f32[8,512,256]{2,1,0:T(8,128)}, f32[8,128]{1,0:T(8,128)}) custom-call(s32[4]{0:T(128)} %add_convert_fusion.refs_0_, bf16[256,1024]{1,0:T(8,128)(2,1)} %collective-permute-done.4.refs_1_, bf16[256,1024]{1,0:T(8,128)(2,1)} %collective-permute-done.3.refs_2_, bf16[384,1024]{1,0:T(8,128)(2,1)} %stack.70.refs_4_.refs_12_.refs_20_.refs_3_.refs_11_.refs_5_.refs_13_, ...), custom_call_target="tpu_custom_call" | custom-call | flops 1 | bytes 1 | tf_op jit(solution)/shard_map/step/pallas_call | solution.py:270
  108.1 5.3 %collective-permute-start.18 = (bf16[256,1024]{1,0:T(8,128)(2,1)S(1)}, bf16[256,1024]{1,0:T(8,128)(2,1)S(1)}, u32[]{:S(2)}, u32[]{:S(2)}) collective-permute-start(bf16[256,1024]{1,0:T(8,128)(2,1)S(1)} %collective-permute-done.16.refs_3_), channel_id=1, source_target_pairs={{0,248},{8,0},{16,8},{24,16},{32,24},{40,32},{48,40},{56,48},{64,5... | collective-permute-start | bytes 1572872 | tf_op jit(solution)/shard_map/ppermute | solution.py:308
  113.4 12.8 %step.3 = (f32[8,512,256]{2,1,0:T(8,128)}, f32[8,128]{1,0:T(8,128)}) custom-call(s32[4]{0:T(128)} %add_convert_fusion.refs_0_, bf16[256,1024]{1,0:T(8,128)(2,1)} %copy-done.9, bf16[256,1024]{1,0:T(8,128)(2,1)} %collective-permute-done.5.refs_2_, bf16[384,1024]{1,0:T(8,128)(2,1)} %stack.70.refs_4_.refs_12_.refs_20_.refs_3_.refs_11_.refs_5_.refs_13_, ...), custom_call_target="tpu_custom_call" | custom-call | flops 1 | bytes 1 | tf_op jit(solution)/shard_map/step/pallas_call | solution.py:270
  126.3 0.7 copy-done.10
  127.6 17.3 %last.1 = bf16[512,1024]{1,0:T(8,128)(2,1)} custom-call(s32[4]{0:T(128)} %add_convert_fusion.refs_0_, s32[8]{0:T(128)} %stack.61.order_ref.refs_1_, bf16[256,1024]{1,0:T(8,128)(2,1)} %copy-done.10, bf16[256,1024]{1,0:T(8,128)(2,1)} %copy-done.8, bf16[256,1024]{1,0:T(8,128)(2,1)} %copy-done.11, ...), custom_call_target="tpu_custom_call" | custom-call | flops 1 | bytes 1 | tf_op jit(solution)/shard_map/last/pallas_call | solution.py:288
  (62 shorter events, 4.0 us)
Async XLA Ops:
  1.5 11.6 %collective-permute-start = (bf16[64,1024]{1,0:T(8,128)(2,1)S(1)}, bf16[64,1024]{1,0:T(8,128)(2,1)S(1)}, u32[]{:S(2)}, u32[]{:S(2)}) collective-permute-start(bf16[64,1024]{1,0:T(8,128)(2,1)S(1)} %slice_bitcast_fusion), channel_id=1, source_target_pairs={{0,8},{8,16},{16,24},{24,32},{32,40},{40,48},{48,56},{56,64},{64,7... | collective-permute-start | bytes 393224 | tf_op jit(solution)/shard_map/ppermute | solution.py:308
  5.6 50.8 %collective-permute-start.1 = (bf16[384,1024]{1,0:T(8,128)(2,1)}, bf16[384,1024]{1,0:T(8,128)(2,1)S(1)}, u32[]{:S(2)}, u32[]{:S(2)}) collective-permute-start(bf16[384,1024]{1,0:T(8,128)(2,1)} %stack.70.refs_4_.refs_12_.refs_20_.refs_3_.refs_11_.refs_5_.refs_13_), channel_id=1, source_target_pairs={{0,4},{1,5},{2,6},{3,7},{4,0},{5,1},{6,2},{7,3},{8,12},{9,13},{10,... | collective-permute-start | bytes 2359304 | tf_op jit(solution)/shard_map/ppermute | solution.py:313
  17.2 39.2 %collective-permute-start.2 = (bf16[256,1024]{1,0:T(8,128)(2,1)}, bf16[256,1024]{1,0:T(8,128)(2,1)}, u32[]{:S(2)}, u32[]{:S(2)}) collective-permute-start(bf16[256,1024]{1,0:T(8,128)(2,1)} %get-tuple-element.38.refs_1_), channel_id=1, source_target_pairs={{0,8},{8,16},{16,24},{24,32},{32,40},{40,48},{48,56},{56,64},{64,7... | collective-permute-start | bytes 1572872 | tf_op jit(solution)/shard_map/ppermute | solution.py:308
  17.2 39.2 %collective-permute-start.3 = (bf16[256,1024]{1,0:T(8,128)(2,1)}, bf16[256,1024]{1,0:T(8,128)(2,1)}, u32[]{:S(2)}, u32[]{:S(2)}) collective-permute-start(bf16[256,1024]{1,0:T(8,128)(2,1)} %get-tuple-element.39.refs_2_), channel_id=1, source_target_pairs={{0,32},{8,40},{16,48},{24,56},{32,64},{40,72},{48,80},{56,88},{64,... | collective-permute-start | bytes 1572872 | tf_op jit(solution)/shard_map/ppermute | solution.py:308
  20.6 36.5 %collective-permute-start.9 = (bf16[384,1024]{1,0:T(8,128)(2,1)}, bf16[384,1024]{1,0:T(8,128)(2,1)S(1)}, u32[]{:S(2)}, u32[]{:S(2)}) collective-permute-start(bf16[384,1024]{1,0:T(8,128)(2,1)} %stack.70.refs_4_.refs_12_.refs_20_.refs_3_.refs_11_.refs_5_.refs_13_), channel_id=1, source_target_pairs={{0,6},{1,7},{2,0},{3,1},{4,2},{5,3},{6,4},{7,5},{8,14},{9,15},{10,... | collective-permute-start | bytes 2359304 | tf_op jit(solution)/shard_map/ppermute | solution.py:313
  20.6 36.6 %collective-permute-start.7 = (bf16[384,1024]{1,0:T(8,128)(2,1)}, bf16[384,1024]{1,0:T(8,128)(2,1)S(1)}, u32[]{:S(2)}, u32[]{:S(2)}) collective-permute-start(bf16[384,1024]{1,0:T(8,128)(2,1)} %stack.70.refs_4_.refs_12_.refs_20_.refs_3_.refs_11_.refs_5_.refs_13_), channel_id=1, source_target_pairs={{0,2},{1,3},{2,4},{3,5},{4,6},{5,7},{6,0},{7,1},{8,10},{9,11},{10,... | collective-permute-start | bytes 2359304 | tf_op jit(solution)/shard_map/ppermute | solution.py:313
  56.4 11.7 %copy-start = (bf16[384,1024]{1,0:T(8,128)(2,1)}, bf16[384,1024]{1,0:T(8,128)(2,1)S(1)}, u32[]{:S(2)}) copy-start(bf16[384,1024]{1,0:T(8,128)(2,1)S(1)} %collective-permute-done.1.refs_10_.refs_18_.refs_26_.refs_9_.refs_17_.refs_11_.refs_19_) | copy-start | bytes 2359300
  56.4 2.5 %collective-permute-start.11 = (bf16[384,1024]{1,0:T(8,128)(2,1)S(1)}, bf16[384,1024]{1,0:T(8,128)(2,1)S(1)}, u32[]{:S(2)}, u32[]{:S(2)}) collective-permute-start(bf16[384,1024]{1,0:T(8,128)(2,1)S(1)} %collective-permute-done.1.refs_10_.refs_18_.refs_26_.refs_9_.refs_17_.refs_11_.refs_19_), channel_id=1, source_target_pairs={{0,1},{1,0},{2,3},{3,2},{4,5},{5,4},{6,7},{7,6},{8,9},{9,8},{10,11... | collective-permute-start | bytes 2359304 | tf_op jit(solution)/shard_map/ppermute | solution.py:313
  56.5 6.4 %collective-permute-start.6 = (bf16[384,1024]{1,0:T(8,128)(2,1)}, bf16[384,1024]{1,0:T(8,128)(2,1)S(1)}, u32[]{:S(2)}, u32[]{:S(2)}) collective-permute-start(bf16[384,1024]{1,0:T(8,128)(2,1)} %stack.70.refs_4_.refs_12_.refs_20_.refs_3_.refs_11_.refs_5_.refs_13_), channel_id=1, source_target_pairs={{0,1},{1,0},{2,3},{3,2},{4,5},{5,4},{6,7},{7,6},{8,9},{9,8},{10,11... | collective-permute-start | bytes 2359304 | tf_op jit(solution)/shard_map/ppermute | solution.py:313
  57.0 11.1 %copy-start.1 = (bf16[384,1024]{1,0:T(8,128)(2,1)}, bf16[384,1024]{1,0:T(8,128)(2,1)S(1)}, u32[]{:S(2)}) copy-start(bf16[384,1024]{1,0:T(8,128)(2,1)S(1)} %collective-permute-done.9.refs_8_.refs_16_.refs_24_.refs_7_.refs_15_.refs_9_.refs_17_) | copy-start | bytes 2359300
  57.0 5.9 %collective-permute-start.10 = (bf16[384,1024]{1,0:T(8,128)(2,1)S(1)}, bf16[384,1024]{1,0:T(8,128)(2,1)S(1)}, u32[]{:S(2)}, u32[]{:S(2)}) collective-permute-start(bf16[384,1024]{1,0:T(8,128)(2,1)S(1)} %collective-permute-done.9.refs_8_.refs_16_.refs_24_.refs_7_.refs_15_.refs_9_.refs_17_), channel_id=1, source_target_pairs={{0,1},{1,0},{2,3},{3,2},{4,5},{5,4},{6,7},{7,6},{8,9},{9,8},{10,11... | collective-permute-start | bytes 2359304 | tf_op jit(solution)/shard_map/ppermute | solution.py:313
  57.1 11.0 %copy-start.2 = (bf16[384,1024]{1,0:T(8,128)(2,1)}, bf16[384,1024]{1,0:T(8,128)(2,1)S(1)}, u32[]{:S(2)}) copy-start(bf16[384,1024]{1,0:T(8,128)(2,1)S(1)} %collective-permute-done.7.refs_6_.refs_14_.refs_22_.refs_5_.refs_13_.refs_7_.refs_15_) | copy-start | bytes 2359300
  57.2 7.8 %collective-permute-start.8 = (bf16[384,1024]{1,0:T(8,128)(2,1)S(1)}, bf16[384,1024]{1,0:T(8,128)(2,1)S(1)}, u32[]{:S(2)}, u32[]{:S(2)}) collective-permute-start(bf16[384,1024]{1,0:T(8,128)(2,1)S(1)} %collective-permute-done.7.refs_6_.refs_14_.refs_22_.refs_5_.refs_13_.refs_7_.refs_15_), channel_id=1, source_target_pairs={{0,1},{1,0},{2,3},{3,2},{4,5},{5,4},{6,7},{7,6},{8,9},{9,8},{10,11... | collective-permute-start | bytes 2359304 | tf_op jit(solution)/shard_map/ppermute | solution.py:313
  57.6 29.8 %collective-permute-start.4 = (bf16[256,1024]{1,0:T(8,128)(2,1)}, bf16[256,1024]{1,0:T(8,128)(2,1)}, u32[]{:S(2)}, u32[]{:S(2)}) collective-permute-start(bf16[256,1024]{1,0:T(8,128)(2,1)} %collective-permute-done.2.refs_3_), channel_id=1, source_target_pairs={{0,8},{8,16},{16,24},{24,32},{32,40},{40,48},{48,56},{56,64},{64,7... | collective-permute-start | bytes 1572872 | tf_op jit(solution)/shard_map/ppermute | solution.py:308
  58.9 28.4 %collective-permute-start.5 = (bf16[256,1024]{1,0:T(8,128)(2,1)}, bf16[256,1024]{1,0:T(8,128)(2,1)}, u32[]{:S(2)}, u32[]{:S(2)}) collective-permute-start(bf16[256,1024]{1,0:T(8,128)(2,1)} %collective-permute-done.3.refs_2_), channel_id=1, source_target_pairs={{0,248},{8,0},{16,8},{24,16},{32,24},{40,32},{48,40},{56,48},{64,5... | collective-permute-start | bytes 1572872 | tf_op jit(solution)/shard_map/ppermute | solution.py:308
  62.9 24.4 %collective-permute-start.12 = (bf16[128,1024]{1,0:T(8,128)(2,1)}, bf16[128,1024]{1,0:T(8,128)(2,1)S(1)}, u32[]{:S(2)}, u32[]{:S(2)}) collective-permute-start(bf16[128,1024]{1,0:T(8,128)(2,1)} %refs_0_.1), channel_id=1, source_target_pairs={{0,2},{1,3},{2,4},{3,5},{4,6},{5,7},{6,0},{7,1},{8,10},{9,11},{10,... | collective-permute-start | bytes 786440 | tf_op jit(solution)/shard_map/ppermute | solution.py:313
  62.9 24.4 %collective-permute-start.13 = (bf16[128,1024]{1,0:T(8,128)(2,1)}, bf16[128,1024]{1,0:T(8,128)(2,1)}, u32[]{:S(2)}, u32[]{:S(2)}) collective-permute-start(bf16[128,1024]{1,0:T(8,128)(2,1)} %refs_0_.1), channel_id=1, source_target_pairs={{0,6},{1,7},{2,0},{3,1},{4,2},{5,3},{6,4},{7,5},{8,14},{9,15},{10,... | collective-permute-start | bytes 786440 | tf_op jit(solution)/shard_map/ppermute | solution.py:313
  65.9 21.5 %collective-permute-start.14 = (bf16[128,1024]{1,0:T(8,128)(2,1)}, bf16[128,1024]{1,0:T(8,128)(2,1)}, u32[]{:S(2)}, u32[]{:S(2)}) collective-permute-start(bf16[128,1024]{1,0:T(8,128)(2,1)} %refs_0_.1), channel_id=1, source_target_pairs={{0,4},{1,5},{2,6},{3,7},{4,0},{5,1},{6,2},{7,3},{8,12},{9,13},{10,... | collective-permute-start | bytes 786440 | tf_op jit(solution)/shard_map/ppermute | solution.py:313
  87.4 20.6 %collective-permute-start.15 = (bf16[256,1024]{1,0:T(8,128)(2,1)}, bf16[256,1024]{1,0:T(8,128)(2,1)S(1)}, u32[]{:S(2)}, u32[]{:S(2)}) collective-permute-start(bf16[256,1024]{1,0:T(8,128)(2,1)} %collective-permute-done.4.refs_1_), channel_id=1, source_target_pairs={{0,8},{8,16},{16,24},{24,32},{32,40},{40,48},{48,56},{56,64},{64,7... | collective-permute-start | bytes 1572872 | tf_op jit(solution)/shard_map/ppermute | solution.py:308
  87.5 20.5 %collective-permute-start.16 = (bf16[256,1024]{1,0:T(8,128)(2,1)}, bf16[256,1024]{1,0:T(8,128)(2,1)S(1)}, u32[]{:S(2)}, u32[]{:S(2)}) collective-permute-start(bf16[256,1024]{1,0:T(8,128)(2,1)} %collective-permute-done.5.refs_2_), channel_id=1, source_target_pairs={{0,248},{8,0},{16,8},{24,16},{32,24},{40,32},{48,40},{56,48},{64,5... | collective-permute-start | bytes 1572872 | tf_op jit(solution)/shard_map/ppermute | solution.py:308
  95.0 31.3 %collective-permute-start.19 = (bf16[512,1024]{1,0:T(8,128)(2,1)}, bf16[512,1024]{1,0:T(8,128)(2,1)S(1)}, u32[]{:S(2)}, u32[]{:S(2)}) collective-permute-start(bf16[512,1024]{1,0:T(8,128)(2,1)} %stack.71.refs_21_), channel_id=1, source_target_pairs={{0,1},{1,0},{2,3},{3,2},{4,5},{5,4},{6,7},{7,6},{8,9},{9,8},{10,11... | collective-permute-start | bytes 3145736 | tf_op jit(solution)/shard_map/ppermute | solution.py:313
  108.0 18.3 %copy-start.8 = (bf16[256,1024]{1,0:T(8,128)(2,1)}, bf16[256,1024]{1,0:T(8,128)(2,1)S(1)}, u32[]{:S(2)}) copy-start(bf16[256,1024]{1,0:T(8,128)(2,1)S(1)} %collective-permute-done.16.refs_3_) | copy-start | bytes 1572868
  108.0 18.3 %collective-permute-start.17 = (bf16[256,1024]{1,0:T(8,128)(2,1)S(1)}, bf16[256,1024]{1,0:T(8,128)(2,1)S(1)}, u32[]{:S(2)}, u32[]{:S(2)}) collective-permute-start(bf16[256,1024]{1,0:T(8,128)(2,1)S(1)} %collective-permute-done.15.refs_1_), channel_id=1, source_target_pairs={{0,8},{8,16},{16,24},{24,32},{32,40},{40,48},{48,56},{56,64},{64,7... | collective-permute-start | bytes 1572872 | tf_op jit(solution)/shard_map/ppermute | solution.py:308
  108.1 18.2 %collective-permute-start.18 = (bf16[256,1024]{1,0:T(8,128)(2,1)S(1)}, bf16[256,1024]{1,0:T(8,128)(2,1)S(1)}, u32[]{:S(2)}, u32[]{:S(2)}) collective-permute-start(bf16[256,1024]{1,0:T(8,128)(2,1)S(1)} %collective-permute-done.16.refs_3_), channel_id=1, source_target_pairs={{0,248},{8,0},{16,8},{24,16},{32,24},{40,32},{48,40},{56,48},{64,5... | collective-permute-start | bytes 1572872 | tf_op jit(solution)/shard_map/ppermute | solution.py:308
  (10 other events, 28.8 us)

commit v3 on v2

--- a/solution.py
+++ b/solution.py
@@ -12,7 +12,7 @@
 PAIR = 2 * HEAD_DIM
 QUAD = 2 * PAIR
 HALF = 256
-UPPER = 256
+UPPER = 384
 BLOCK = 512
 EPS = 1e-6
 QUERY_FACTOR = 16.0 / HEAD_DIM * 1.4426950408889634
@@ -155,52 +155,53 @@
     return j <= i
 
 
-def since(i, j):
-    return j >= i
+def upper_since(i, j):
+    return (j >= UPPER) | (j >= i)
+
+
+def first_lower_since(i, j):
+    return (j < BLOCK + UPPER) | (j - BLOCK >= i)
 
 
 FIRST_PLAN = (
-    ((0, HALF, until), (BLOCK, BLOCK + UPPER, None)),
-    ((0, HALF, None), (HALF, BLOCK, until), (BLOCK, BLOCK + UPPER, None)),
+    ((0, HALF, until), (BLOCK, 2 * BLOCK, None)),
+    ((0, HALF, None), (HALF, BLOCK, until), (BLOCK, 2 * BLOCK, first_lower_since)),
 )
-SECOND_PLAN = (
-    ((0, BLOCK, None),),
-    ((0, UPPER, None), (UPPER, BLOCK, since)),
-)
+FIRST_PLACES = (None, None, 0, 3)
 FULL_PLAN = (((0, BLOCK, None),),) * 2
-LAST_PLAN = (
-    ((0, UPPER, since), (UPPER, 3 * HALF, None)),
-    ((UPPER, 3 * HALF, None),),
-)
-
-
-def keys_of(x, w_k, w_v, valid_ref, valid):
+LAST_PLAN = (((0, BLOCK, upper_since),), ((HALF, BLOCK, upper_since),))
+
+
+def keys_of(refs, w_k, w_v, valid_ref, valid):
+    x = joined(refs)
     key = head_norm(project(x, joined(w_k)), 1.0)
     value = project(x, joined(w_v))
-    values, ones = [], []
-    for n, place in enumerate(valid):
-        part, one = value[n * HALF : (n + 1) * HALF], jnp.ones((HALF, PAIR), F32)
+    values, ones, row = [], [], 0
+    for ref, place in zip(refs, valid):
+        rows = ref.shape[0]
+        part, one = value[row : row + rows], jnp.ones((rows, PAIR), F32)
         if place is not None:
             counts = valid_ref[place] > 0
             part, one = jnp.where(counts, part, 0.0), jnp.where(counts, one, 0.0)
         values.append(part.astype(BF))
         ones.append(one.astype(BF))
+        row += rows
     return key, jnp.concatenate(values, axis=0), jnp.concatenate(ones, axis=0)
 
 
 def first_kernel(*refs):
-    valid_ref = refs[0]
-    w_q, w_k, w_v = refs[4:12], refs[12:20], refs[20:28]
-    query_ref, total_ref, token_ref = refs[28:]
+    n = len(FIRST_PLACES)
+    valid_ref, rows = refs[0], refs[1 : 1 + n]
+    w_q, w_k, w_v = refs[1 + n : 9 + n], refs[9 + n : 17 + n], refs[17 + n : 25 + n]
+    query_ref, total_ref, token_ref = refs[25 + n :]
     token_ref[...] = jnp.zeros_like(token_ref)
-    x = joined(refs[1:4])
-    query = head_norm(project(x[:BLOCK], joined(w_q)), QUERY_FACTOR)
+    query = head_norm(project(joined(rows[:2]), joined(w_q)), QUERY_FACTOR)
     query_ref[...] = query
 
     def put(pair, rows, total):
         total_ref[pair, rows, :] = total
 
-    attend_quad(query, *keys_of(x, w_k, w_v, valid_ref, (None, None, 0)), FIRST_PLAN, put)
+    attend_quad(query, *keys_of(rows, w_k, w_v, valid_ref, FIRST_PLACES), FIRST_PLAN, put)
 
 
 def step_kernel(plan, valid, *refs):
@@ -213,30 +214,34 @@
     def put(pair, rows, total):
         out_ref[pair, rows, :] = total_ref[pair, rows, :] + total
 
-    attend_quad(query_ref[...], *keys_of(joined(rows), w_k, w_v, valid_ref, valid), plan, put)
+    attend_quad(query_ref[...], *keys_of(rows, w_k, w_v, valid_ref, valid), plan, put)
 
 
 def last_kernel(plan, valid, *refs):
     n = len(valid)
     valid_ref, order_ref, rows = refs[0], refs[1], refs[2 : 2 + n]
-    w_k, w_v, w_out = refs[2 + n : 10 + n], refs[10 + n : 18 + n], refs[18 + n : 20 + n]
-    query_ref, total_ref, _, out_ref, context = refs[20 + n :]
+    w_k, w_v, w_out = refs[2 + n : 10 + n], refs[10 + n : 18 + n], refs[18 + n : 26 + n]
+    query_ref, total_ref, _, out_ref, context = refs[26 + n :]
     g = pl.program_id(0)
 
     def put(pair, rows, total):
         total = total_ref[pair, rows, :] + total
         context[2 * g + pair, rows, :] = (total[:, :PAIR] / total[:, PAIR:]).astype(BF)
 
-    attend_quad(query_ref[...], *keys_of(joined(rows), w_k, w_v, valid_ref, valid), plan, put)
+    attend_quad(query_ref[...], *keys_of(rows, w_k, w_v, valid_ref, valid), plan, put)
 
     @pl.when(g == pl.num_programs(0) - 1)
     def _():
-        x = jnp.concatenate([context[order_ref[r]] for r in (0, 2, 4, 6, 1, 3, 5, 7)], axis=1)
+        x = jnp.concatenate([context[order_ref[r]] for r in range(8)], axis=1)
         out_ref[...] = project(x, joined(w_out)).astype(BF)
 
 
+def weight_arrays(parts, kind):
+    return [part[kind][0] for part in parts]
+
+
 def weight_specs(parts, kind):
-    return [pl.BlockSpec((PAIR, QUAD), lambda g: (kind, g))] * len(parts)
+    return [pl.BlockSpec((PAIR, QUAD), functools.partial(lambda row, g: (row, g), part[kind][1])) for part in parts]
 
 
 QUERY_SPEC = pl.BlockSpec((BLOCK, QUAD), lambda g: (0, g))
@@ -262,7 +267,7 @@
         compiler_params=params(),
         cost_estimate=SMALL,
         name="first",
-    )(valid, *rows, *parts, *parts, *parts)
+    )(valid, *rows, *(w for kind in range(3) for w in weight_arrays(parts, kind)))
 
 
 def attend_step(plan, places, valid, rows, parts, query, total, token):
@@ -280,10 +285,10 @@
         compiler_params=params(),
         cost_estimate=SMALL,
         name="step",
-    )(valid, *rows, *parts, *parts, query, total, token)
-
-
-def attend_last(plan, places, valid, order, rows, parts, w_out, query, total, token):
+    )(valid, *rows, *weight_arrays(parts, 1), *weight_arrays(parts, 2), query, total, token)
+
+
+def attend_last(plan, places, valid, order, rows, parts, query, total, token):
     width = rows[0].shape[1]
     return pl.pallas_call(
         functools.partial(last_kernel, plan, places),
@@ -292,7 +297,9 @@
         + [whole(x.shape) for x in rows]
         + weight_specs(parts, 1)
         + weight_specs(parts, 2)
-        + [whole(w.shape) for w in w_out]
+        + [
+            pl.BlockSpec((PAIR, width), functools.partial(lambda row, g: (row, 0), part[3][1])) for part in parts
+        ]
         + [QUERY_SPEC, TOTAL_SPEC, pl.BlockSpec(memory_space=pl.ANY)],
         out_specs=whole((BLOCK, width)),
         out_shape=jax.ShapeDtypeStruct((BLOCK, width), BF),
@@ -300,7 +307,7 @@
         compiler_params=params(),
         cost_estimate=SMALL,
         name="last",
-    )(valid, order, *rows, *parts, *parts, *w_out, query, total, token)
+    )(valid, order, *rows, *(w for kind in (1, 2, 3) for w in weight_arrays(parts, kind)), query, total, token)
 
 
 def along_seq(block, distance):
@@ -315,10 +322,6 @@
 
 def together(*arrays):
     return lax.optimization_barrier(arrays)
-
-
-def gather_parts(rows):
-    return [rows] + [over_fsdp(rows, dy, 0) for dy in (1, -1, 2)]
 
 
 def weight_order():
@@ -337,45 +340,41 @@
     order = weight_order()
     valid = jnp.stack([position >= k for k in range(1, 5)]).astype(jnp.int32)
 
-    tail, w_query, w_key, w_value = together(own_groups[owned - TAIL :], w_query, w_key, w_value)
+    tail, *own_weights = together(own_groups[owned - TAIL :], w_query, w_key, w_value, w_out)
     carried = along_seq(tail, 1)
-    packed = stack(w_query, w_key, w_value)
-    own_core = gather_parts(packed)
-
-    far = jnp.int32(2**30)
-    padded = jnp.concatenate([jnp.zeros((TAIL,), jnp.int32), starts, jnp.full((1,), far, jnp.int32)])
+    packed = stack(*own_weights)
+    half = packed.shape[0] // 2
+    below, above = over_fsdp(packed, 1, 0), over_fsdp(packed, -1, 0)
+    far = over_fsdp(below[:half], 1, 0), over_fsdp(above[half:], -1, 0)
+
+    never = jnp.int32(2**30)
+    padded = jnp.concatenate([jnp.zeros((TAIL,), jnp.int32), starts, jnp.full((1,), never, jnp.int32)])
     window = lax.dynamic_slice_in_dim(padded, position * owned, owned + TAIL + 1, 0) - position * rows
     begin, end = window[:-1], window[1:]
-    gap = jnp.full((PAIR - TAIL,), far, jnp.int32)
+    gap = jnp.full((PAIR - TAIL,), never, jnp.int32)
     window = jnp.stack([jnp.concatenate([w[:TAIL], gap, w[TAIL:]]) for w in (begin, end)])
 
     dechunked, upper, lower = prep(order, window, own_bytes, carried, own_groups)
 
     up, down = {1: along_seq(upper, 1)}, {4: along_seq(lower, 4)}
-    other = [over_fsdp(part, 0, 1) for part in own_core[:3]]
-    own_core[3], up[1], down[4] = together(own_core[3], up[1], down[4])
-    other.append(over_fsdp(own_core[3], 0, 1))
-
-    other[3], w_out = together(other[3], w_out)
-    w_out_core = gather_parts(w_out)
+    *far, up[1], down[4] = together(*far, up[1], down[4])
+    parts = []
+    for part in (packed, below, above):
+        parts += [tuple((x, kind) for kind in range(4)) for x in (part, over_fsdp(part, 0, 1))]
+    for a, b in (far, [over_fsdp(x, 0, 1) for x in far]):
+        parts.append(((a, 0), (a, 1), (b, 0), (b, 1)))
+
     up[2], down[3] = along_seq(up[1], 1), along_seq(down[4], -1)
-    parts = [part for pair in zip(own_core, other) for part in pair]
-    query, total, token = attend_first(valid, (upper, lower, up[1]), parts)
-
-    up[2], down[3], token, *w_out_core = together(up[2], down[3], token, *w_out_core)
+    query, total, token = attend_first(valid, (upper, lower, up[1], down[4]), parts)
+
+    up[2], down[3], token = together(up[2], down[3], token)
     up[3], down[2] = along_seq(up[2], 1), along_seq(down[3], -1)
-    token, w_out_core = together(token, stack(*w_out_core))
-    w_out = w_out_core, over_fsdp(w_out_core, 0, 1)
-    rows = (up[2], down[4])
-    total, token = attend_step(SECOND_PLAN, (1, 3), valid, rows, parts, query, total, token)
+    total, token = attend_step(FULL_PLAN, (1, 2), valid, (up[2], down[3]), parts, query, total, token)
 
     up[3], down[2], token = together(up[3], down[2], token)
     up[4], down[1] = along_seq(up[3], 1), along_seq(down[2], -1)
-    rows = (up[3], down[3])
-    total, token = attend_step(FULL_PLAN, (2, 2), valid, rows, parts, query, total, token)
-
-    rows = (up[4], down[2], down[1])
-    attended = attend_last(LAST_PLAN, (3, 1, 0), valid, order, rows, parts, w_out, query, total, token)
+    total, token = attend_step(FULL_PLAN, (2, 1), valid, (up[3], down[2]), parts, query, total, token)
+    attended = attend_last(LAST_PLAN, (3, 0), valid, order, (up[4], down[1]), parts, query, total, token)
     return dechunked[None], attended[None]
 
 

time: 148 us -> 144 us (0.973); the launches traced: 145 us -> 144 us
  waiting for transfers between devices: 38 us -> 42 us
  Pallas kernels: 69.8 us -> 66.3 us
  starting transfers between devices: 29.4 us -> 27.6 us
    ppermute x11 -> x9, waiting for transfers between devices: 1.39 us -> 5.5 us  [over_fsdp(): lax.ppermute(block, 'fsdp', [(i, (i // 2 * 2 + 2 * dy) % count + (i + oth...]
    pallas_call x1, Pallas kernels: 17.3 us -> 13.7 us  [attend_last(): pl.pallas_call(functools.partial(last_kernel, plan, places), grid=(width...]
    ppermute x11 -> x9, starting transfers between devices: 9.25 us -> 7.23 us  [over_fsdp(): lax.ppermute(block, 'fsdp', [(i, (i // 2 * 2 + 2 * dy) % count + (i + oth...]
    pallas_call x1, Pallas kernels: 19.2 us -> 21.2 us  [attend_first(): pl.pallas_call(first_kernel, grid=(width // QUAD,), in_specs=[SMEM_WHOLE]...]
    pallas_call x2 -> x1, Pallas kernels: 4.29 us -> 2.29 us  [stack(): pl.pallas_call(stack_kernel, grid=(1,), in_specs=[whole((rows, width))] *...]
  transfers between devices with their start and end apart: 20 -> 18, of which waited for: 3 -> 6; matrix products, arithmetic and copies ran while one was open for 2% -> 2% of each run, Pallas kernels for 36% -> 35%
where the time goes in v3:
time: 144 us
  Pallas kernels  66.3 us (46%)
  waiting for transfers between devices  42 us (29%)
  starting transfers between devices  27.6 us (19%)
  local copies, waits for them, and re-layouts  5.27 us (4%)
    ppermute x9, waiting for transfers between devices, along_seq(): lax.ppermute(block, 'seq', [(i, (i + distance) % count) for i in range(co...  36.5 us
    pallas_call x2, Pallas kernels, attend_step(): pl.pallas_call(functools.partial(step_kernel, plan, places), grid=(width...  25.7 us
    pallas_call x1, Pallas kernels, attend_first(): pl.pallas_call(first_kernel, grid=(width // QUAD,), in_specs=[SMEM_WHOLE]...  21.2 us
    ppermute x9, starting transfers between devices, along_seq(): lax.ppermute(block, 'seq', [(i, (i + distance) % count) for i in range(co...  20.3 us
    pallas_call x1, Pallas kernels, attend_last(): pl.pallas_call(functools.partial(last_kernel, plan, places), grid=(width...  13.7 us
    ppermute x9, starting transfers between devices, over_fsdp(): lax.ppermute(block, 'fsdp', [(i, (i // 2 * 2 + 2 * dy) % count + (i + oth...  7.23 us
    ppermute x9, waiting for transfers between devices, over_fsdp(): lax.ppermute(block, 'fsdp', [(i, (i // 2 * 2 + 2 * dy) % count + (i + oth...  5.5 us
    pallas_call x1, Pallas kernels, prep(): pl.pallas_call(prep_kernel, grid=(1,), in_specs=[SMEM_WHOLE] + [whole(x.s...  3.48 us
  transfers between devices with their start and end apart: 18, of which 6 were waited for; matrix products, arithmetic and copies ran while one was open for 2% of the time, Pallas kernels for 35%

profile of v3, /device:TPU:24, one launch (start us, length us, event | category | flops | bytes accessed | tf_op | source)
XLA Modules:
  0.0 143.6 jit_solution(6579426683594687077)
XLA Ops:
  0.6 0.9 slice_bitcast_fusion
  1.5 2.3 %stack.69.refs_5_.refs_13_.refs_21_.refs_3_.refs_11_.refs_4_.refs_12_.refs_20_ = bf16[512,1024]{1,0:T(8,128)(2,1)} custom-call(bf16[128,1024]{1,0:T(8,128)(2,1)} %refs_0_, bf16[128,1024]{1,0:T(8,128)(2,1)} %refs_1_, bf16[128,1024]{1,0:T(8,128)(2,1)} %refs_2_, bf16[128,1024]{1,0:T(8,128)(2,1)} %refs_3_), custom_call_target="tpu_custom_call" | custom-call | flops 1 | bytes 1 | tf_op jit(solution)/shard_map/stack/pallas_call | solution.py:85
  3.8 0.7 collective-permute-start.3
  4.6 2.5 %collective-permute-start.1 = (bf16[512,1024]{1,0:T(8,128)(2,1)}, bf16[512,1024]{1,0:T(8,128)(2,1)S(1)}, u32[]{:S(2)}, u32[]{:S(2)}) collective-permute-start(bf16[512,1024]{1,0:T(8,128)(2,1)} %stack.69.refs_5_.refs_13_.refs_21_.refs_3_.refs_11_.refs_4_.refs_12_.refs_20_), channel_id=1, source_target_pairs={{0,2},{1,3},{2,4},{3,5},{4,6},{5,7},{6,0},{7,1},{8,10},{9,11},{10,... | collective-permute-start | bytes 3145736 | tf_op jit(solution)/shard_map/ppermute | solution.py:320
  7.1 1.9 %collective-permute-start = (bf16[64,1024]{1,0:T(8,128)(2,1)S(1)}, bf16[64,1024]{1,0:T(8,128)(2,1)S(1)}, u32[]{:S(2)}, u32[]{:S(2)}) collective-permute-start(bf16[64,1024]{1,0:T(8,128)(2,1)S(1)} %slice_bitcast_fusion), channel_id=1, source_target_pairs={{0,8},{8,16},{16,24},{24,32},{32,40},{40,48},{48,56},{56,64},{64,7... | collective-permute-start | bytes 393224 | tf_op jit(solution)/shard_map/ppermute | solution.py:315
  9.0 0.8 concatenate.9
  11.4 6.7 %collective-permute-done.carried_ref = bf16[64,1024]{1,0:T(8,128)(2,1)S(1)} collective-permute-done((bf16[64,1024]{1,0:T(8,128)(2,1)S(1)}, bf16[64,1024]{1,0:T(8,128)(2,1)S(1)}, u32[]{:S(2)}, u32[]{:S(2)}) %collective-permute-start) | collective-permute-done | bytes 131104 | tf_op jit(solution)/shard_map/ppermute | solution.py:315
  18.7 3.5 %prep.1 = (bf16[512,1024]{1,0:T(8,128)(2,1)}, bf16[384,1024]{1,0:T(8,128)(2,1)}, bf16[128,1024]{1,0:T(8,128)(2,1)}) custom-call(s32[8]{0:T(128)} %stack.60.order_ref.refs_1_, s32[2,256]{1,0:T(2,128)} %pad_add_fusion.win_ref, bf16[512,1024]{1,0:T(8,128)(2,1)} %bitcast.22, bf16[64,1024]{1,0:T(8,128)(2,1)} %copy-done.9, bf16[128,1024]{1,0:T(8,128)(2,1)} %bitcast.23), custom_call_target="tpu_custom_call" | custom-call | flops 1 | bytes 1 | tf_op jit(solution)/shard_map/prep/pallas_call | solution.py:62
  22.2 2.4 %collective-permute-start.6 = (bf16[128,1024]{1,0:T(8,128)(2,1)}, bf16[128,1024]{1,0:T(8,128)(2,1)}, u32[]{:S(2)}, u32[]{:S(2)}) collective-permute-start(bf16[128,1024]{1,0:T(8,128)(2,1)} %get-tuple-element.34.refs_2_), channel_id=1, source_target_pairs={{0,32},{8,40},{16,48},{24,56},{32,64},{40,72},{48,80},{56,88},{64,... | collective-permute-start | bytes 786440 | tf_op jit(solution)/shard_map/ppermute | solution.py:315
  24.7 5.5 %collective-permute-done.3.refs_9_.refs_17_.refs_25_.refs_7_.refs_15_.refs_8_.refs_16_.refs_24_ = bf16[512,1024]{1,0:T(8,128)(2,1)S(1)} collective-permute-done((bf16[512,1024]{1,0:T(8,128)(2,1)}, bf16[512,1024]{1,0:T(8,128)(2,1)S(1)}, u32[]{:S(2)}, u32[]{:S(2)}) %collective-permute-start.3) | collective-permute-done | bytes 1048608 | tf_op jit(solution)/shard_map/ppermute | solution.py:320
  30.4 3.3 %collective-permute-start.2 = (bf16[256,1024]{1,0:T(8,128)(2,1)S(1)}, bf16[256,1024]{1,0:T(8,128)(2,1)}, u32[]{:S(2)}, u32[]{:S(2)}) collective-permute-start(bf16[256,1024]{1,0:T(8,128)(2,1)S(1)} %slice.38), channel_id=1, source_target_pairs={{0,2},{1,3},{2,4},{3,5},{4,6},{5,7},{6,0},{7,1},{8,10},{9,11},{10,... | collective-permute-start | bytes 1572872 | tf_op jit(solution)/shard_map/ppermute | solution.py:320
  33.6 18.9 %collective-permute-done.6.refs_4_ = bf16[128,1024]{1,0:T(8,128)(2,1)} collective-permute-done((bf16[128,1024]{1,0:T(8,128)(2,1)}, bf16[128,1024]{1,0:T(8,128)(2,1)}, u32[]{:S(2)}, u32[]{:S(2)}) %collective-permute-start.6) | collective-permute-done | bytes 262176 | tf_op jit(solution)/shard_map/ppermute | solution.py:315
  52.6 2.4 %collective-permute-done.5.refs_3_ = bf16[384,1024]{1,0:T(8,128)(2,1)} collective-permute-done((bf16[384,1024]{1,0:T(8,128)(2,1)}, bf16[384,1024]{1,0:T(8,128)(2,1)}, u32[]{:S(2)}, u32[]{:S(2)}) %collective-permute-start.5) | collective-permute-done | bytes 786464 | tf_op jit(solution)/shard_map/ppermute | solution.py:315
  55.7 1.1 copy-done.3
  56.8 5.1 %collective-permute-start.8 = (bf16[128,1024]{1,0:T(8,128)(2,1)}, bf16[128,1024]{1,0:T(8,128)(2,1)S(1)}, u32[]{:S(2)}, u32[]{:S(2)}) collective-permute-start(bf16[128,1024]{1,0:T(8,128)(2,1)} %collective-permute-done.6.refs_4_), channel_id=1, source_target_pairs={{0,248},{8,0},{16,8},{24,16},{32,24},{40,32},{48,40},{56,48},{64,5... | collective-permute-start | bytes 786440 | tf_op jit(solution)/shard_map/ppermute | solution.py:315
  62.6 21.2 %first.1 = (bf16[512,1024]{1,0:T(8,128)(2,1)}, f32[8,512,256]{2,1,0:T(8,128)}, f32[8,128]{1,0:T(8,128)}) custom-call(s32[4]{0:T(128)} %add_convert_fusion.refs_0_, bf16[384,1024]{1,0:T(8,128)(2,1)} %get-tuple-element.33.refs_1_, bf16[128,1024]{1,0:T(8,128)(2,1)} %get-tuple-element.34.refs_2_, bf16[384,1024]{1,0:T(8,128)(2,1)} %collective-permute-done.5.refs_3_, ...), custom_call_target="tpu_custom_call" | custom-call | flops 1 | bytes 1 | tf_op jit(solution)/shard_map/first/pallas_call | solution.py:253
  83.9 5.3 %collective-permute-start.15 = (bf16[128,1024]{1,0:T(8,128)(2,1)S(1)}, bf16[128,1024]{1,0:T(8,128)(2,1)S(1)}, u32[]{:S(2)}, u32[]{:S(2)}) collective-permute-start(bf16[128,1024]{1,0:T(8,128)(2,1)S(1)} %collective-permute-done.8.refs_2_), channel_id=1, source_target_pairs={{0,248},{8,0},{16,8},{24,16},{32,24},{40,32},{48,40},{56,48},{64,5... | collective-permute-start | bytes 786440 | tf_op jit(solution)/shard_map/ppermute | solution.py:315
  89.2 12.9 %step.2 = (f32[8,512,256]{2,1,0:T(8,128)}, f32[8,128]{1,0:T(8,128)}) custom-call(s32[4]{0:T(128)} %add_convert_fusion.refs_0_, bf16[384,1024]{1,0:T(8,128)(2,1)} %collective-permute-done.7.refs_1_, bf16[128,1024]{1,0:T(8,128)(2,1)} %copy-done.6, bf16[512,1024]{1,0:T(8,128)(2,1)} %stack.69.refs_5_.refs_13_.refs_21_.refs_3_.refs_11_.refs_4_.refs_12_.refs_20_, ...), custom_call_target="tpu_custom_call" | custom-call | flops 1 | bytes 1 | tf_op jit(solution)/shard_map/step/pallas_call | solution.py:275
  102.1 4.7 %collective-permute-done.14.refs_1_ = bf16[384,1024]{1,0:T(8,128)(2,1)S(1)} collective-permute-done((bf16[384,1024]{1,0:T(8,128)(2,1)}, bf16[384,1024]{1,0:T(8,128)(2,1)S(1)}, u32[]{:S(2)}, u32[]{:S(2)}) %collective-permute-start.14) | collective-permute-done | bytes 786464 | tf_op jit(solution)/shard_map/ppermute | solution.py:315
  106.9 5.3 %collective-permute-start.17 = (bf16[128,1024]{1,0:T(8,128)(2,1)S(1)}, bf16[128,1024]{1,0:T(8,128)(2,1)S(1)}, u32[]{:S(2)}, u32[]{:S(2)}) collective-permute-start(bf16[128,1024]{1,0:T(8,128)(2,1)S(1)} %collective-permute-done.15.refs_2_), channel_id=1, source_target_pairs={{0,248},{8,0},{16,8},{24,16},{32,24},{40,32},{48,40},{56,48},{64,5... | collective-permute-start | bytes 786440 | tf_op jit(solution)/shard_map/ppermute | solution.py:315
  112.2 12.8 %step.3 = (f32[8,512,256]{2,1,0:T(8,128)}, f32[8,128]{1,0:T(8,128)}) custom-call(s32[4]{0:T(128)} %add_convert_fusion.refs_0_, bf16[384,1024]{1,0:T(8,128)(2,1)} %copy-done.4, bf16[128,1024]{1,0:T(8,128)(2,1)} %copy-done.8, bf16[512,1024]{1,0:T(8,128)(2,1)} %stack.69.refs_5_.refs_13_.refs_21_.refs_3_.refs_11_.refs_4_.refs_12_.refs_20_, ...), custom_call_target="tpu_custom_call" | custom-call | flops 1 | bytes 1 | tf_op jit(solution)/shard_map/step/pallas_call | solution.py:275
  125.0 3.8 %collective-permute-done.16.refs_2_ = bf16[384,1024]{1,0:T(8,128)(2,1)S(1)} collective-permute-done((bf16[384,1024]{1,0:T(8,128)(2,1)S(1)}, bf16[384,1024]{1,0:T(8,128)(2,1)S(1)}, u32[]{:S(2)}, u32[]{:S(2)}) %collective-permute-start.16) | collective-permute-done | bytes 786464 | tf_op jit(solution)/shard_map/ppermute | solution.py:315
  128.8 0.9 copy-done.5
  129.7 13.7 %last.1 = bf16[512,1024]{1,0:T(8,128)(2,1)} custom-call(s32[4]{0:T(128)} %add_convert_fusion.refs_0_, s32[8]{0:T(128)} %stack.60.order_ref.refs_1_, bf16[384,1024]{1,0:T(8,128)(2,1)} %copy-done.5, bf16[128,1024]{1,0:T(8,128)(2,1)} %copy-done.7, bf16[512,1024]{1,0:T(8,128)(2,1)} %stack.69.refs_5_.refs_13_.refs_21_.refs_3_.refs_11_.refs_4_.refs_12_.refs_20_, ...), custom_call_target="tpu_custom_call" | custom-call | flops 1 | bytes 1 | tf_op jit(solution)/shard_map/last/pallas_call | solution.py:293
  (51 shorter events, 3.9 us)
Async XLA Ops:
  3.8 26.3 %collective-permute-start.3 = (bf16[512,1024]{1,0:T(8,128)(2,1)}, bf16[512,1024]{1,0:T(8,128)(2,1)S(1)}, u32[]{:S(2)}, u32[]{:S(2)}) collective-permute-start(bf16[512,1024]{1,0:T(8,128)(2,1)} %stack.69.refs_5_.refs_13_.refs_21_.refs_3_.refs_11_.refs_4_.refs_12_.refs_20_), channel_id=1, source_target_pairs={{0,6},{1,7},{2,0},{3,1},{4,2},{5,3},{6,4},{7,5},{8,14},{9,15},{10,... | collective-permute-start | bytes 3145736 | tf_op jit(solution)/shard_map/ppermute | solution.py:320
  4.6 25.7 %collective-permute-start.1 = (bf16[512,1024]{1,0:T(8,128)(2,1)}, bf16[512,1024]{1,0:T(8,128)(2,1)S(1)}, u32[]{:S(2)}, u32[]{:S(2)}) collective-permute-start(bf16[512,1024]{1,0:T(8,128)(2,1)} %stack.69.refs_5_.refs_13_.refs_21_.refs_3_.refs_11_.refs_4_.refs_12_.refs_20_), channel_id=1, source_target_pairs={{0,2},{1,3},{2,4},{3,5},{4,6},{5,7},{6,0},{7,1},{8,10},{9,11},{10,... | collective-permute-start | bytes 3145736 | tf_op jit(solution)/shard_map/ppermute | solution.py:320
  7.1 11.0 %collective-permute-start = (bf16[64,1024]{1,0:T(8,128)(2,1)S(1)}, bf16[64,1024]{1,0:T(8,128)(2,1)S(1)}, u32[]{:S(2)}, u32[]{:S(2)}) collective-permute-start(bf16[64,1024]{1,0:T(8,128)(2,1)S(1)} %slice_bitcast_fusion), channel_id=1, source_target_pairs={{0,8},{8,16},{16,24},{24,32},{32,40},{40,48},{48,56},{56,64},{64,7... | collective-permute-start | bytes 393224 | tf_op jit(solution)/shard_map/ppermute | solution.py:315
  22.2 32.7 %collective-permute-start.5 = (bf16[384,1024]{1,0:T(8,128)(2,1)}, bf16[384,1024]{1,0:T(8,128)(2,1)}, u32[]{:S(2)}, u32[]{:S(2)}) collective-permute-start(bf16[384,1024]{1,0:T(8,128)(2,1)} %get-tuple-element.33.refs_1_), channel_id=1, source_target_pairs={{0,8},{8,16},{16,24},{24,32},{32,40},{40,48},{48,56},{56,64},{64,7... | collective-permute-start | bytes 2359304 | tf_op jit(solution)/shard_map/ppermute | solution.py:315
  22.2 33.3 %collective-permute-start.9 = (bf16[512,1024]{1,0:T(8,128)(2,1)}, bf16[512,1024]{1,0:T(8,128)(2,1)S(1)}, u32[]{:S(2)}, u32[]{:S(2)}) collective-permute-start(bf16[512,1024]{1,0:T(8,128)(2,1)} %stack.69.refs_5_.refs_13_.refs_21_.refs_3_.refs_11_.refs_4_.refs_12_.refs_20_), channel_id=1, source_target_pairs={{0,1},{1,0},{2,3},{3,2},{4,5},{5,4},{6,7},{7,6},{8,9},{9,8},{10,11... | collective-permute-start | bytes 3145736 | tf_op jit(solution)/shard_map/ppermute | solution.py:320
  22.2 30.3 %collective-permute-start.6 = (bf16[128,1024]{1,0:T(8,128)(2,1)}, bf16[128,1024]{1,0:T(8,128)(2,1)}, u32[]{:S(2)}, u32[]{:S(2)}) collective-permute-start(bf16[128,1024]{1,0:T(8,128)(2,1)} %get-tuple-element.34.refs_2_), channel_id=1, source_target_pairs={{0,32},{8,40},{16,48},{24,56},{32,64},{40,72},{48,80},{56,88},{64,... | collective-permute-start | bytes 786440 | tf_op jit(solution)/shard_map/ppermute | solution.py:315
  30.2 32.4 %copy-start = (bf16[512,1024]{1,0:T(8,128)(2,1)}, bf16[512,1024]{1,0:T(8,128)(2,1)S(1)}, u32[]{:S(2)}) copy-start(bf16[512,1024]{1,0:T(8,128)(2,1)S(1)} %collective-permute-done.3.refs_9_.refs_17_.refs_25_.refs_7_.refs_15_.refs_8_.refs_16_.refs_24_) | copy-start | bytes 3145732
  30.2 24.8 %collective-permute-start.4 = (bf16[256,1024]{1,0:T(8,128)(2,1)S(1)}, bf16[256,1024]{1,0:T(8,128)(2,1)}, u32[]{:S(2)}, u32[]{:S(2)}) collective-permute-start(bf16[256,1024]{1,0:T(8,128)(2,1)S(1)} %slice.39), channel_id=1, source_target_pairs={{0,6},{1,7},{2,0},{3,1},{4,2},{5,3},{6,4},{7,5},{8,14},{9,15},{10,... | collective-permute-start | bytes 1572872 | tf_op jit(solution)/shard_map/ppermute | solution.py:320
  30.3 32.3 %copy-start.1 = (bf16[512,1024]{1,0:T(8,128)(2,1)}, bf16[512,1024]{1,0:T(8,128)(2,1)S(1)}, u32[]{:S(2)}) copy-start(bf16[512,1024]{1,0:T(8,128)(2,1)S(1)} %collective-permute-done.1.refs_7_.refs_15_.refs_23_.refs_5_.refs_13_.refs_6_.refs_14_.refs_22_) | copy-start | bytes 3145732
  30.4 24.6 %collective-permute-start.2 = (bf16[256,1024]{1,0:T(8,128)(2,1)S(1)}, bf16[256,1024]{1,0:T(8,128)(2,1)}, u32[]{:S(2)}, u32[]{:S(2)}) collective-permute-start(bf16[256,1024]{1,0:T(8,128)(2,1)S(1)} %slice.38), channel_id=1, source_target_pairs={{0,2},{1,3},{2,4},{3,5},{4,6},{5,7},{6,0},{7,1},{8,10},{9,11},{10,... | collective-permute-start | bytes 1572872 | tf_op jit(solution)/shard_map/ppermute | solution.py:320
  52.6 3.1 %collective-permute-start.11 = (bf16[512,1024]{1,0:T(8,128)(2,1)S(1)}, bf16[512,1024]{1,0:T(8,128)(2,1)S(1)}, u32[]{:S(2)}, u32[]{:S(2)}) collective-permute-start(bf16[512,1024]{1,0:T(8,128)(2,1)S(1)} %collective-permute-done.3.refs_9_.refs_17_.refs_25_.refs_7_.refs_15_.refs_8_.refs_16_.refs_24_), channel_id=1, source_target_pairs={{0,1},{1,0},{2,3},{3,2},{4,5},{5,4},{6,7},{7,6},{8,9},{9,8},{10,11... | collective-permute-start | bytes 3145736 | tf_op jit(solution)/shard_map/ppermute | solution.py:320
  54.9 7.6 %collective-permute-start.10 = (bf16[512,1024]{1,0:T(8,128)(2,1)S(1)}, bf16[512,1024]{1,0:T(8,128)(2,1)}, u32[]{:S(2)}, u32[]{:S(2)}) collective-permute-start(bf16[512,1024]{1,0:T(8,128)(2,1)S(1)} %collective-permute-done.1.refs_7_.refs_15_.refs_23_.refs_5_.refs_13_.refs_6_.refs_14_.refs_22_), channel_id=1, source_target_pairs={{0,1},{1,0},{2,3},{3,2},{4,5},{5,4},{6,7},{7,6},{8,9},{9,8},{10,11... | collective-permute-start | bytes 3145736 | tf_op jit(solution)/shard_map/ppermute | solution.py:320
  55.0 28.8 %collective-permute-start.7 = (bf16[384,1024]{1,0:T(8,128)(2,1)}, bf16[384,1024]{1,0:T(8,128)(2,1)}, u32[]{:S(2)}, u32[]{:S(2)}) collective-permute-start(bf16[384,1024]{1,0:T(8,128)(2,1)} %collective-permute-done.5.refs_3_), channel_id=1, source_target_pairs={{0,8},{8,16},{16,24},{24,32},{32,40},{40,48},{48,56},{56,64},{64,7... | collective-permute-start | bytes 2359304 | tf_op jit(solution)/shard_map/ppermute | solution.py:315
  55.1 7.5 %collective-permute-start.12 = (bf16[256,1024]{1,0:T(8,128)(2,1)}, bf16[256,1024]{1,0:T(8,128)(2,1)}, u32[]{:S(2)}, u32[]{:S(2)}) collective-permute-start(bf16[256,1024]{1,0:T(8,128)(2,1)} %collective-permute-done.2.refs_11_.refs_19_.refs_9_.refs_10_), channel_id=1, source_target_pairs={{0,1},{1,0},{2,3},{3,2},{4,5},{5,4},{6,7},{7,6},{8,9},{9,8},{10,11... | collective-permute-start | bytes 1572872 | tf_op jit(solution)/shard_map/ppermute | solution.py:320
  55.6 7.0 %copy-start.2 = (bf16[512,1024]{1,0:T(8,128)(2,1)}, bf16[512,1024]{1,0:T(8,128)(2,1)S(1)}, u32[]{:S(2)}) copy-start(bf16[512,1024]{1,0:T(8,128)(2,1)S(1)} %collective-permute-done.9.refs_6_.refs_14_.refs_22_.refs_4_.refs_12_.refs_5_.refs_13_.refs_21_) | copy-start | bytes 3145732
  55.6 7.0 %collective-permute-start.13 = (bf16[256,1024]{1,0:T(8,128)(2,1)}, bf16[256,1024]{1,0:T(8,128)(2,1)}, u32[]{:S(2)}, u32[]{:S(2)}) collective-permute-start(bf16[256,1024]{1,0:T(8,128)(2,1)} %collective-permute-done.4.refs_27_.refs_17_.refs_18_.refs_26_), channel_id=1, source_target_pairs={{0,1},{1,0},{2,3},{3,2},{4,5},{5,4},{6,7},{7,6},{8,9},{9,8},{10,11... | collective-permute-start | bytes 1572872 | tf_op jit(solution)/shard_map/ppermute | solution.py:320
  56.8 27.0 %collective-permute-start.8 = (bf16[128,1024]{1,0:T(8,128)(2,1)}, bf16[128,1024]{1,0:T(8,128)(2,1)S(1)}, u32[]{:S(2)}, u32[]{:S(2)}) collective-permute-start(bf16[128,1024]{1,0:T(8,128)(2,1)} %collective-permute-done.6.refs_4_), channel_id=1, source_target_pairs={{0,248},{8,0},{16,8},{24,16},{32,24},{40,32},{48,40},{56,48},{64,5... | collective-permute-start | bytes 786440 | tf_op jit(solution)/shard_map/ppermute | solution.py:315
  83.8 5.4 %copy-start.6 = (bf16[128,1024]{1,0:T(8,128)(2,1)}, bf16[128,1024]{1,0:T(8,128)(2,1)S(1)}, u32[]{:S(2)}) copy-start(bf16[128,1024]{1,0:T(8,128)(2,1)S(1)} %collective-permute-done.8.refs_2_) | copy-start | bytes 786436
  83.8 23.1 %collective-permute-start.14 = (bf16[384,1024]{1,0:T(8,128)(2,1)}, bf16[384,1024]{1,0:T(8,128)(2,1)S(1)}, u32[]{:S(2)}, u32[]{:S(2)}) collective-permute-start(bf16[384,1024]{1,0:T(8,128)(2,1)} %collective-permute-done.7.refs_1_), channel_id=1, source_target_pairs={{0,8},{8,16},{16,24},{24,32},{32,40},{40,48},{48,56},{56,64},{64,7... | collective-permute-start | bytes 2359304 | tf_op jit(solution)/shard_map/ppermute | solution.py:315
  83.9 18.2 %collective-permute-start.15 = (bf16[128,1024]{1,0:T(8,128)(2,1)S(1)}, bf16[128,1024]{1,0:T(8,128)(2,1)S(1)}, u32[]{:S(2)}, u32[]{:S(2)}) collective-permute-start(bf16[128,1024]{1,0:T(8,128)(2,1)S(1)} %collective-permute-done.8.refs_2_), channel_id=1, source_target_pairs={{0,248},{8,0},{16,8},{24,16},{32,24},{40,32},{48,40},{56,48},{64,5... | collective-permute-start | bytes 786440 | tf_op jit(solution)/shard_map/ppermute | solution.py:315
  102.1 10.1 %copy-start.8 = (bf16[128,1024]{1,0:T(8,128)(2,1)}, bf16[128,1024]{1,0:T(8,128)(2,1)S(1)}, u32[]{:S(2)}) copy-start(bf16[128,1024]{1,0:T(8,128)(2,1)S(1)} %collective-permute-done.15.refs_2_) | copy-start | bytes 786436
  106.9 5.4 %copy-start.4 = (bf16[384,1024]{1,0:T(8,128)(2,1)}, bf16[384,1024]{1,0:T(8,128)(2,1)S(1)}, u32[]{:S(2)}) copy-start(bf16[384,1024]{1,0:T(8,128)(2,1)S(1)} %collective-permute-done.14.refs_1_) | copy-start | bytes 2359300
  106.9 21.9 %collective-permute-start.16 = (bf16[384,1024]{1,0:T(8,128)(2,1)S(1)}, bf16[384,1024]{1,0:T(8,128)(2,1)S(1)}, u32[]{:S(2)}, u32[]{:S(2)}) collective-permute-start(bf16[384,1024]{1,0:T(8,128)(2,1)S(1)} %collective-permute-done.14.refs_1_), channel_id=1, source_target_pairs={{0,8},{8,16},{16,24},{24,32},{32,40},{40,48},{48,56},{56,64},{64,7... | collective-permute-start | bytes 2359304 | tf_op jit(solution)/shard_map/ppermute | solution.py:315
  106.9 18.1 %collective-permute-start.17 = (bf16[128,1024]{1,0:T(8,128)(2,1)S(1)}, bf16[128,1024]{1,0:T(8,128)(2,1)S(1)}, u32[]{:S(2)}, u32[]{:S(2)}) collective-permute-start(bf16[128,1024]{1,0:T(8,128)(2,1)S(1)} %collective-permute-done.15.refs_2_), channel_id=1, source_target_pairs={{0,248},{8,0},{16,8},{24,16},{32,24},{40,32},{48,40},{56,48},{64,5... | collective-permute-start | bytes 786440 | tf_op jit(solution)/shard_map/ppermute | solution.py:315
  (4 other events, 6.4 us)

commit v4 on v3

--- a/solution.py
+++ b/solution.py
@@ -23,7 +23,7 @@
 SMALL = pl.CostEstimate(flops=1, bytes_accessed=1, transcendentals=0)
 TOKEN = jax.ShapeDtypeStruct((8, 128), F32)
 NT = (((1,), (1,)), ((), ()))
-VMEM_LIMIT = 60 * 2**20
+VMEM_LIMIT = 63 * 2**20
 
 
 def params():
@@ -354,6 +354,7 @@
     gap = jnp.full((PAIR - TAIL,), never, jnp.int32)
     window = jnp.stack([jnp.concatenate([w[:TAIL], gap, w[TAIL:]]) for w in (begin, end)])
 
+    order, valid = together(order, valid)
     dechunked, upper, lower = prep(order, window, own_bytes, carried, own_groups)
 
     up, down = {1: along_seq(upper, 1)}, {4: along_seq(lower, 4)}

time: 144 us -> 143 us (level)
  waiting for transfers between devices: 42 us -> 39.4 us
  local copies, waits for them, and re-layouts: 5.27 us -> 6.99 us
    ppermute x9, waiting for transfers between devices: 36.5 us -> 33.8 us  [along_seq(): lax.ppermute(block, 'seq', [(i, (i + distance) % count) for i in range(co...]
    slice x2, local copies, waits for them, and re-layouts: 0.07 us -> 2.15 us  [local(): far = (over_fsdp(below[:half], 1, 0), over_fsdp(above[half:], -1, 0))]
  transfers between devices with their start and end apart: 18 -> 18, of which waited for: 6 -> 6; matrix products, arithmetic and copies ran while one was open for 2% -> 4% of each run, Pallas kernels for 35% -> 35%
where the time goes in v4:
time: 143 us; the launch traced here: 142 us
  Pallas kernels  66.2 us (46%)
  waiting for transfers between devices  39.4 us (28%)
  starting transfers between devices  27.5 us (19%)
  local copies, waits for them, and re-layouts  6.99 us (5%)
    ppermute x9, waiting for transfers between devices, along_seq(): lax.ppermute(block, 'seq', [(i, (i + distance) % count) for i in range(co...  33.8 us
    pallas_call x2, Pallas kernels, attend_step(): pl.pallas_call(functools.partial(step_kernel, plan, places), grid=(width...  25.6 us
    pallas_call x1, Pallas kernels, attend_first(): pl.pallas_call(first_kernel, grid=(width // QUAD,), in_specs=[SMEM_WHOLE]...  21.1 us
    ppermute x9, starting transfers between devices, along_seq(): lax.ppermute(block, 'seq', [(i, (i + distance) % count) for i in range(co...  19.8 us
    pallas_call x1, Pallas kernels, attend_last(): pl.pallas_call(functools.partial(last_kernel, plan, places), grid=(width...  13.7 us
    ppermute x9, starting transfers between devices, over_fsdp(): lax.ppermute(block, 'fsdp', [(i, (i // 2 * 2 + 2 * dy) % count + (i + oth...  7.7 us
    ppermute x9, waiting for transfers between devices, over_fsdp(): lax.ppermute(block, 'fsdp', [(i, (i // 2 * 2 + 2 * dy) % count + (i + oth...  5.62 us
    pallas_call x1, Pallas kernels, prep(): pl.pallas_call(prep_kernel, grid=(1,), in_specs=[SMEM_WHOLE] + [whole(x.s...  3.47 us
  transfers between devices with their start and end apart: 18, of which 6 were waited for; matrix products, arithmetic and copies ran while one was open for 4% of the time, Pallas kernels for 35%

profile of v4, /device:TPU:24, one launch (start us, length us, event | category | flops | bytes accessed | tf_op | source)
XLA Modules:
  0.0 142.5 jit_solution(4629993234837744731)
XLA Ops:
  0.6 0.9 slice_bitcast_fusion
  1.5 2.3 %stack.69.refs_5_.refs_13_.refs_21_.refs_3_.refs_11_.refs_4_.refs_12_.refs_20_ = bf16[512,1024]{1,0:T(8,128)(2,1)} custom-call(bf16[128,1024]{1,0:T(8,128)(2,1)} %refs_0_, bf16[128,1024]{1,0:T(8,128)(2,1)} %refs_1_, bf16[128,1024]{1,0:T(8,128)(2,1)} %refs_2_, bf16[128,1024]{1,0:T(8,128)(2,1)} %refs_3_), custom_call_target="tpu_custom_call" | custom-call | flops 1 | bytes 1 | tf_op jit(solution)/shard_map/stack/pallas_call | solution.py:85
  4.6 2.5 %collective-permute-start.1 = (bf16[512,1024]{1,0:T(8,128)(2,1)}, bf16[512,1024]{1,0:T(8,128)(2,1)}, u32[]{:S(2)}, u32[]{:S(2)}) collective-permute-start(bf16[512,1024]{1,0:T(8,128)(2,1)} %stack.69.refs_5_.refs_13_.refs_21_.refs_3_.refs_11_.refs_4_.refs_12_.refs_20_), channel_id=1, source_target_pairs={{0,2},{1,3},{2,4},{3,5},{4,6},{5,7},{6,0},{7,1},{8,10},{9,11},{10,... | collective-permute-start | bytes 3145736 | tf_op jit(solution)/shard_map/ppermute | solution.py:320
  7.1 1.9 %collective-permute-start = (bf16[64,1024]{1,0:T(8,128)(2,1)S(1)}, bf16[64,1024]{1,0:T(8,128)(2,1)S(1)}, u32[]{:S(2)}, u32[]{:S(2)}) collective-permute-start(bf16[64,1024]{1,0:T(8,128)(2,1)S(1)} %slice_bitcast_fusion), channel_id=1, source_target_pairs={{0,8},{8,16},{16,24},{24,32},{32,40},{40,48},{48,56},{56,64},{64,7... | collective-permute-start | bytes 393224 | tf_op jit(solution)/shard_map/ppermute | solution.py:315
  9.0 0.8 concatenate.9
  12.0 6.1 %collective-permute-done.carried_ref = bf16[64,1024]{1,0:T(8,128)(2,1)S(1)} collective-permute-done((bf16[64,1024]{1,0:T(8,128)(2,1)S(1)}, bf16[64,1024]{1,0:T(8,128)(2,1)S(1)}, u32[]{:S(2)}, u32[]{:S(2)}) %collective-permute-start) | collective-permute-done | bytes 131104 | tf_op jit(solution)/shard_map/ppermute | solution.py:315
  18.8 3.5 %prep.1 = (bf16[512,1024]{1,0:T(8,128)(2,1)}, bf16[384,1024]{1,0:T(8,128)(2,1)}, bf16[128,1024]{1,0:T(8,128)(2,1)}) custom-call(s32[8]{0:T(128)} %stack.60.order_ref.refs_1_, s32[2,256]{1,0:T(2,128)} %pad_add_fusion.win_ref, bf16[512,1024]{1,0:T(8,128)(2,1)} %bitcast.22, bf16[64,1024]{1,0:T(8,128)(2,1)} %copy-done.5, bf16[128,1024]{1,0:T(8,128)(2,1)} %bitcast.23), custom_call_target="tpu_custom_call" | custom-call | flops 1 | bytes 1 | tf_op jit(solution)/shard_map/prep/pallas_call | solution.py:62
  22.2 2.4 %collective-permute-start.6 = (bf16[128,1024]{1,0:T(8,128)(2,1)}, bf16[128,1024]{1,0:T(8,128)(2,1)}, u32[]{:S(2)}, u32[]{:S(2)}) collective-permute-start(bf16[128,1024]{1,0:T(8,128)(2,1)} %get-tuple-element.38.refs_2_), channel_id=1, source_target_pairs={{0,32},{8,40},{16,48},{24,56},{32,64},{40,72},{48,80},{56,88},{64,... | collective-permute-start | bytes 786440 | tf_op jit(solution)/shard_map/ppermute | solution.py:315
  24.7 5.6 %collective-permute-done.3.refs_9_.refs_17_.refs_25_.refs_7_.refs_15_.refs_8_.refs_16_.refs_24_ = bf16[512,1024]{1,0:T(8,128)(2,1)} collective-permute-done((bf16[512,1024]{1,0:T(8,128)(2,1)}, bf16[512,1024]{1,0:T(8,128)(2,1)}, u32[]{:S(2)}, u32[]{:S(2)}) %collective-permute-start.3) | collective-permute-done | bytes 1048608 | tf_op jit(solution)/shard_map/ppermute | solution.py:320
  30.3 1.1 slice.39
  31.5 1.1 slice.38
  32.5 3.3 %collective-permute-start.2 = (bf16[256,1024]{1,0:T(8,128)(2,1)S(1)}, bf16[256,1024]{1,0:T(8,128)(2,1)S(1)}, u32[]{:S(2)}, u32[]{:S(2)}) collective-permute-start(bf16[256,1024]{1,0:T(8,128)(2,1)S(1)} %slice.38), channel_id=1, source_target_pairs={{0,2},{1,3},{2,4},{3,5},{4,6},{5,7},{6,0},{7,1},{8,10},{9,11},{10,... | collective-permute-start | bytes 1572872 | tf_op jit(solution)/shard_map/ppermute | solution.py:320
  35.8 15.3 %collective-permute-done.6.refs_4_ = bf16[128,1024]{1,0:T(8,128)(2,1)} collective-permute-done((bf16[128,1024]{1,0:T(8,128)(2,1)}, bf16[128,1024]{1,0:T(8,128)(2,1)}, u32[]{:S(2)}, u32[]{:S(2)}) %collective-permute-start.6) | collective-permute-done | bytes 262176 | tf_op jit(solution)/shard_map/ppermute | solution.py:315
  51.2 3.8 %collective-permute-done.5.refs_3_ = bf16[384,1024]{1,0:T(8,128)(2,1)} collective-permute-done((bf16[384,1024]{1,0:T(8,128)(2,1)}, bf16[384,1024]{1,0:T(8,128)(2,1)}, u32[]{:S(2)}, u32[]{:S(2)}) %collective-permute-start.5) | collective-permute-done | bytes 786464 | tf_op jit(solution)/shard_map/ppermute | solution.py:315
  56.3 4.6 %collective-permute-start.8 = (bf16[128,1024]{1,0:T(8,128)(2,1)}, bf16[128,1024]{1,0:T(8,128)(2,1)S(1)}, u32[]{:S(2)}, u32[]{:S(2)}) collective-permute-start(bf16[128,1024]{1,0:T(8,128)(2,1)} %collective-permute-done.6.refs_4_), channel_id=1, source_target_pairs={{0,248},{8,0},{16,8},{24,16},{32,24},{40,32},{48,40},{56,48},{64,5... | collective-permute-start | bytes 786440 | tf_op jit(solution)/shard_map/ppermute | solution.py:315
  60.9 0.8 copy-done.2
  61.8 21.1 %first.1 = (bf16[512,1024]{1,0:T(8,128)(2,1)}, f32[8,512,256]{2,1,0:T(8,128)}, f32[8,128]{1,0:T(8,128)}) custom-call(s32[4]{0:T(128)} %add_convert_fusion.refs_0_, bf16[384,1024]{1,0:T(8,128)(2,1)} %get-tuple-element.37.refs_1_, bf16[128,1024]{1,0:T(8,128)(2,1)} %get-tuple-element.38.refs_2_, bf16[384,1024]{1,0:T(8,128)(2,1)} %collective-permute-done.5.refs_3_, ...), custom_call_target="tpu_custom_call" | custom-call | flops 1 | bytes 1 | tf_op jit(solution)/shard_map/first/pallas_call | solution.py:253
  83.6 5.3 %collective-permute-start.15 = (bf16[128,1024]{1,0:T(8,128)(2,1)}, bf16[128,1024]{1,0:T(8,128)(2,1)}, u32[]{:S(2)}, u32[]{:S(2)}) collective-permute-start(bf16[128,1024]{1,0:T(8,128)(2,1)} %copy-done.4), channel_id=1, source_target_pairs={{0,248},{8,0},{16,8},{24,16},{32,24},{40,32},{48,40},{56,48},{64,5... | collective-permute-start | bytes 786440 | tf_op jit(solution)/shard_map/ppermute | solution.py:315
  88.9 12.9 %step.2 = (f32[8,512,256]{2,1,0:T(8,128)}, f32[8,128]{1,0:T(8,128)}) custom-call(s32[4]{0:T(128)} %add_convert_fusion.refs_0_, bf16[384,1024]{1,0:T(8,128)(2,1)} %collective-permute-done.7.refs_1_, bf16[128,1024]{1,0:T(8,128)(2,1)} %copy-done.4, bf16[512,1024]{1,0:T(8,128)(2,1)} %stack.69.refs_5_.refs_13_.refs_21_.refs_3_.refs_11_.refs_4_.refs_12_.refs_20_, ...), custom_call_target="tpu_custom_call" | custom-call | flops 1 | bytes 1 | tf_op jit(solution)/shard_map/step/pallas_call | solution.py:275
  101.8 4.7 %collective-permute-done.14.refs_1_ = bf16[384,1024]{1,0:T(8,128)(2,1)S(1)} collective-permute-done((bf16[384,1024]{1,0:T(8,128)(2,1)}, bf16[384,1024]{1,0:T(8,128)(2,1)S(1)}, u32[]{:S(2)}, u32[]{:S(2)}) %collective-permute-start.14) | collective-permute-done | bytes 786464 | tf_op jit(solution)/shard_map/ppermute | solution.py:315
  106.6 5.3 %collective-permute-start.17 = (bf16[128,1024]{1,0:T(8,128)(2,1)}, bf16[128,1024]{1,0:T(8,128)(2,1)}, u32[]{:S(2)}, u32[]{:S(2)}) collective-permute-start(bf16[128,1024]{1,0:T(8,128)(2,1)} %collective-permute-done.15.refs_2_), channel_id=1, source_target_pairs={{0,248},{8,0},{16,8},{24,16},{32,24},{40,32},{48,40},{56,48},{64,5... | collective-permute-start | bytes 786440 | tf_op jit(solution)/shard_map/ppermute | solution.py:315
  111.9 12.8 %step.3 = (f32[8,512,256]{2,1,0:T(8,128)}, f32[8,128]{1,0:T(8,128)}) custom-call(s32[4]{0:T(128)} %add_convert_fusion.refs_0_, bf16[384,1024]{1,0:T(8,128)(2,1)} %copy-done.3, bf16[128,1024]{1,0:T(8,128)(2,1)} %collective-permute-done.15.refs_2_, bf16[512,1024]{1,0:T(8,128)(2,1)} %stack.69.refs_5_.refs_13_.refs_21_.refs_3_.refs_11_.refs_4_.refs_12_.refs_20_, ...), custom_call_target="tpu_custom_call" | custom-call | flops 1 | bytes 1 | tf_op jit(solution)/shard_map/step/pallas_call | solution.py:275
  124.7 3.9 %collective-permute-done.16.refs_2_ = bf16[384,1024]{1,0:T(8,128)(2,1)} collective-permute-done((bf16[384,1024]{1,0:T(8,128)(2,1)S(1)}, bf16[384,1024]{1,0:T(8,128)(2,1)}, u32[]{:S(2)}, u32[]{:S(2)}) %collective-permute-start.16) | collective-permute-done | bytes 786464 | tf_op jit(solution)/shard_map/ppermute | solution.py:315
  128.6 13.7 %last.1 = bf16[512,1024]{1,0:T(8,128)(2,1)} custom-call(s32[4]{0:T(128)} %add_convert_fusion.refs_0_, s32[8]{0:T(128)} %stack.60.order_ref.refs_1_, bf16[384,1024]{1,0:T(8,128)(2,1)} %collective-permute-done.16.refs_2_, bf16[128,1024]{1,0:T(8,128)(2,1)} %collective-permute-done.17.refs_3_, ...), custom_call_target="tpu_custom_call" | custom-call | flops 1 | bytes 1 | tf_op jit(solution)/shard_map/last/pallas_call | solution.py:293
  (43 shorter events, 5.7 us)
Async XLA Ops:
  3.9 26.4 %collective-permute-start.3 = (bf16[512,1024]{1,0:T(8,128)(2,1)}, bf16[512,1024]{1,0:T(8,128)(2,1)}, u32[]{:S(2)}, u32[]{:S(2)}) collective-permute-start(bf16[512,1024]{1,0:T(8,128)(2,1)} %stack.69.refs_5_.refs_13_.refs_21_.refs_3_.refs_11_.refs_4_.refs_12_.refs_20_), channel_id=1, source_target_pairs={{0,6},{1,7},{2,0},{3,1},{4,2},{5,3},{6,4},{7,5},{8,14},{9,15},{10,... | collective-permute-start | bytes 3145736 | tf_op jit(solution)/shard_map/ppermute | solution.py:320
  4.6 26.9 %collective-permute-start.1 = (bf16[512,1024]{1,0:T(8,128)(2,1)}, bf16[512,1024]{1,0:T(8,128)(2,1)}, u32[]{:S(2)}, u32[]{:S(2)}) collective-permute-start(bf16[512,1024]{1,0:T(8,128)(2,1)} %stack.69.refs_5_.refs_13_.refs_21_.refs_3_.refs_11_.refs_4_.refs_12_.refs_20_), channel_id=1, source_target_pairs={{0,2},{1,3},{2,4},{3,5},{4,6},{5,7},{6,0},{7,1},{8,10},{9,11},{10,... | collective-permute-start | bytes 3145736 | tf_op jit(solution)/shard_map/ppermute | solution.py:320
  7.1 11.0 %collective-permute-start = (bf16[64,1024]{1,0:T(8,128)(2,1)S(1)}, bf16[64,1024]{1,0:T(8,128)(2,1)S(1)}, u32[]{:S(2)}, u32[]{:S(2)}) collective-permute-start(bf16[64,1024]{1,0:T(8,128)(2,1)S(1)} %slice_bitcast_fusion), channel_id=1, source_target_pairs={{0,8},{8,16},{16,24},{24,32},{32,40},{40,48},{48,56},{56,64},{64,7... | collective-permute-start | bytes 393224 | tf_op jit(solution)/shard_map/ppermute | solution.py:315
  18.1 0.7 copy-start.5
  22.2 32.7 %collective-permute-start.5 = (bf16[384,1024]{1,0:T(8,128)(2,1)}, bf16[384,1024]{1,0:T(8,128)(2,1)}, u32[]{:S(2)}, u32[]{:S(2)}) collective-permute-start(bf16[384,1024]{1,0:T(8,128)(2,1)} %get-tuple-element.37.refs_1_), channel_id=1, source_target_pairs={{0,8},{8,16},{16,24},{24,32},{32,40},{40,48},{48,56},{56,64},{64,7... | collective-permute-start | bytes 2359304 | tf_op jit(solution)/shard_map/ppermute | solution.py:315
  22.2 33.6 %collective-permute-start.9 = (bf16[512,1024]{1,0:T(8,128)(2,1)}, bf16[512,1024]{1,0:T(8,128)(2,1)}, u32[]{:S(2)}, u32[]{:S(2)}) collective-permute-start(bf16[512,1024]{1,0:T(8,128)(2,1)} %stack.69.refs_5_.refs_13_.refs_21_.refs_3_.refs_11_.refs_4_.refs_12_.refs_20_), channel_id=1, source_target_pairs={{0,1},{1,0},{2,3},{3,2},{4,5},{5,4},{6,7},{7,6},{8,9},{9,8},{10,11... | collective-permute-start | bytes 3145736 | tf_op jit(solution)/shard_map/ppermute | solution.py:320
  22.2 28.9 %collective-permute-start.6 = (bf16[128,1024]{1,0:T(8,128)(2,1)}, bf16[128,1024]{1,0:T(8,128)(2,1)}, u32[]{:S(2)}, u32[]{:S(2)}) collective-permute-start(bf16[128,1024]{1,0:T(8,128)(2,1)} %get-tuple-element.38.refs_2_), channel_id=1, source_target_pairs={{0,32},{8,40},{16,48},{24,56},{32,64},{40,72},{48,80},{56,88},{64,... | collective-permute-start | bytes 786440 | tf_op jit(solution)/shard_map/ppermute | solution.py:315
  31.4 23.6 %collective-permute-start.4 = (bf16[256,1024]{1,0:T(8,128)(2,1)S(1)}, bf16[256,1024]{1,0:T(8,128)(2,1)S(1)}, u32[]{:S(2)}, u32[]{:S(2)}) collective-permute-start(bf16[256,1024]{1,0:T(8,128)(2,1)S(1)} %slice.39), channel_id=1, source_target_pairs={{0,6},{1,7},{2,0},{3,1},{4,2},{5,3},{6,4},{7,5},{8,14},{9,15},{10,... | collective-permute-start | bytes 1572872 | tf_op jit(solution)/shard_map/ppermute | solution.py:320
  32.5 22.4 %collective-permute-start.2 = (bf16[256,1024]{1,0:T(8,128)(2,1)S(1)}, bf16[256,1024]{1,0:T(8,128)(2,1)S(1)}, u32[]{:S(2)}, u32[]{:S(2)}) collective-permute-start(bf16[256,1024]{1,0:T(8,128)(2,1)S(1)} %slice.38), channel_id=1, source_target_pairs={{0,2},{1,3},{2,4},{3,5},{4,6},{5,7},{6,0},{7,1},{8,10},{9,11},{10,... | collective-permute-start | bytes 1572872 | tf_op jit(solution)/shard_map/ppermute | solution.py:320
  51.2 5.1 %collective-permute-start.11 = (bf16[512,1024]{1,0:T(8,128)(2,1)}, bf16[512,1024]{1,0:T(8,128)(2,1)}, u32[]{:S(2)}, u32[]{:S(2)}) collective-permute-start(bf16[512,1024]{1,0:T(8,128)(2,1)} %collective-permute-done.3.refs_9_.refs_17_.refs_25_.refs_7_.refs_15_.refs_8_.refs_16_.refs_24_), channel_id=1, source_target_pairs={{0,1},{1,0},{2,3},{3,2},{4,5},{5,4},{6,7},{7,6},{8,9},{9,8},{10,11... | collective-permute-start | bytes 3145736 | tf_op jit(solution)/shard_map/ppermute | solution.py:320
  54.9 6.0 %collective-permute-start.10 = (bf16[512,1024]{1,0:T(8,128)(2,1)}, bf16[512,1024]{1,0:T(8,128)(2,1)}, u32[]{:S(2)}, u32[]{:S(2)}) collective-permute-start(bf16[512,1024]{1,0:T(8,128)(2,1)} %collective-permute-done.1.refs_7_.refs_15_.refs_23_.refs_5_.refs_13_.refs_6_.refs_14_.refs_22_), channel_id=1, source_target_pairs={{0,1},{1,0},{2,3},{3,2},{4,5},{5,4},{6,7},{7,6},{8,9},{9,8},{10,11... | collective-permute-start | bytes 3145736 | tf_op jit(solution)/shard_map/ppermute | solution.py:320
  55.0 6.8 %copy-start = (bf16[256,1024]{1,0:T(8,128)(2,1)}, bf16[256,1024]{1,0:T(8,128)(2,1)S(1)}, u32[]{:S(2)}) copy-start(bf16[256,1024]{1,0:T(8,128)(2,1)S(1)} %collective-permute-done.4.refs_27_.refs_17_.refs_18_.refs_26_) | copy-start | bytes 1572868
  55.0 0.8 copy-start.1
  55.0 27.9 %collective-permute-start.7 = (bf16[384,1024]{1,0:T(8,128)(2,1)}, bf16[384,1024]{1,0:T(8,128)(2,1)}, u32[]{:S(2)}, u32[]{:S(2)}) collective-permute-start(bf16[384,1024]{1,0:T(8,128)(2,1)} %collective-permute-done.5.refs_3_), channel_id=1, source_target_pairs={{0,8},{8,16},{16,24},{24,32},{32,40},{40,48},{48,56},{56,64},{64,7... | collective-permute-start | bytes 2359304 | tf_op jit(solution)/shard_map/ppermute | solution.py:315
  55.1 5.9 %collective-permute-start.12 = (bf16[256,1024]{1,0:T(8,128)(2,1)S(1)}, bf16[256,1024]{1,0:T(8,128)(2,1)S(1)}, u32[]{:S(2)}, u32[]{:S(2)}) collective-permute-start(bf16[256,1024]{1,0:T(8,128)(2,1)S(1)} %collective-permute-done.2.refs_11_.refs_19_.refs_9_.refs_10_), channel_id=1, source_target_pairs={{0,1},{1,0},{2,3},{3,2},{4,5},{5,4},{6,7},{7,6},{8,9},{9,8},{10,11... | collective-permute-start | bytes 1572872 | tf_op jit(solution)/shard_map/ppermute | solution.py:320
  55.8 6.0 %collective-permute-start.13 = (bf16[256,1024]{1,0:T(8,128)(2,1)S(1)}, bf16[256,1024]{1,0:T(8,128)(2,1)}, u32[]{:S(2)}, u32[]{:S(2)}) collective-permute-start(bf16[256,1024]{1,0:T(8,128)(2,1)S(1)} %collective-permute-done.4.refs_27_.refs_17_.refs_18_.refs_26_), channel_id=1, source_target_pairs={{0,1},{1,0},{2,3},{3,2},{4,5},{5,4},{6,7},{7,6},{8,9},{9,8},{10,11... | collective-permute-start | bytes 1572872 | tf_op jit(solution)/shard_map/ppermute | solution.py:320
  56.3 26.6 %collective-permute-start.8 = (bf16[128,1024]{1,0:T(8,128)(2,1)}, bf16[128,1024]{1,0:T(8,128)(2,1)S(1)}, u32[]{:S(2)}, u32[]{:S(2)}) collective-permute-start(bf16[128,1024]{1,0:T(8,128)(2,1)} %collective-permute-done.6.refs_4_), channel_id=1, source_target_pairs={{0,248},{8,0},{16,8},{24,16},{32,24},{40,32},{48,40},{56,48},{64,5... | collective-permute-start | bytes 786440 | tf_op jit(solution)/shard_map/ppermute | solution.py:315
  60.9 0.8 copy-start.2
  82.9 0.7 copy-start.4
  83.6 23.0 %collective-permute-start.14 = (bf16[384,1024]{1,0:T(8,128)(2,1)}, bf16[384,1024]{1,0:T(8,128)(2,1)S(1)}, u32[]{:S(2)}, u32[]{:S(2)}) collective-permute-start(bf16[384,1024]{1,0:T(8,128)(2,1)} %collective-permute-done.7.refs_1_), channel_id=1, source_target_pairs={{0,8},{8,16},{16,24},{24,32},{32,40},{40,48},{48,56},{56,64},{64,7... | collective-permute-start | bytes 2359304 | tf_op jit(solution)/shard_map/ppermute | solution.py:315
  83.6 18.2 %collective-permute-start.15 = (bf16[128,1024]{1,0:T(8,128)(2,1)}, bf16[128,1024]{1,0:T(8,128)(2,1)}, u32[]{:S(2)}, u32[]{:S(2)}) collective-permute-start(bf16[128,1024]{1,0:T(8,128)(2,1)} %copy-done.4), channel_id=1, source_target_pairs={{0,248},{8,0},{16,8},{24,16},{32,24},{40,32},{48,40},{56,48},{64,5... | collective-permute-start | bytes 786440 | tf_op jit(solution)/shard_map/ppermute | solution.py:315
  106.6 5.4 %copy-start.3 = (bf16[384,1024]{1,0:T(8,128)(2,1)}, bf16[384,1024]{1,0:T(8,128)(2,1)S(1)}, u32[]{:S(2)}) copy-start(bf16[384,1024]{1,0:T(8,128)(2,1)S(1)} %collective-permute-done.14.refs_1_) | copy-start | bytes 2359300
  106.6 22.0 %collective-permute-start.16 = (bf16[384,1024]{1,0:T(8,128)(2,1)S(1)}, bf16[384,1024]{1,0:T(8,128)(2,1)}, u32[]{:S(2)}, u32[]{:S(2)}) collective-permute-start(bf16[384,1024]{1,0:T(8,128)(2,1)S(1)} %collective-permute-done.14.refs_1_), channel_id=1, source_target_pairs={{0,8},{8,16},{16,24},{24,32},{32,40},{40,48},{48,56},{56,64},{64,7... | collective-permute-start | bytes 2359304 | tf_op jit(solution)/shard_map/ppermute | solution.py:315
  106.6 18.1 %collective-permute-start.17 = (bf16[128,1024]{1,0:T(8,128)(2,1)}, bf16[128,1024]{1,0:T(8,128)(2,1)}, u32[]{:S(2)}, u32[]{:S(2)}) collective-permute-start(bf16[128,1024]{1,0:T(8,128)(2,1)} %collective-permute-done.15.refs_2_), channel_id=1, source_target_pairs={{0,248},{8,0},{16,8},{24,16},{32,24},{40,32},{48,40},{56,48},{64,5... | collective-permute-start | bytes 786440 | tf_op jit(solution)/shard_map/ppermute | solution.py:315

commit v5 on v4

--- a/solution.py
+++ b/solution.py
@@ -159,15 +159,16 @@
     return (j >= UPPER) | (j >= i)
 
 
-def first_lower_since(i, j):
-    return (j < BLOCK + UPPER) | (j - BLOCK >= i)
+def middle_since(i, j):
+    return (j < UPPER) | (j >= BLOCK) | (j >= i)
 
 
 FIRST_PLAN = (
-    ((0, HALF, until), (BLOCK, 2 * BLOCK, None)),
-    ((0, HALF, None), (HALF, BLOCK, until), (BLOCK, 2 * BLOCK, first_lower_since)),
+    ((0, HALF, until), (BLOCK, BLOCK + UPPER, None)),
+    ((0, HALF, None), (HALF, BLOCK, until), (BLOCK, BLOCK + UPPER, None)),
 )
-FIRST_PLACES = (None, None, 0, 3)
+FIRST_PLACES = (None, None, 0)
+SECOND_PLAN = (((0, 2 * BLOCK - UPPER, None),), ((0, 2 * BLOCK - UPPER, middle_since),))
 FULL_PLAN = (((0, BLOCK, None),),) * 2
 LAST_PLAN = (((0, BLOCK, upper_since),), ((HALF, BLOCK, upper_since),))
 
@@ -366,11 +367,12 @@
         parts.append(((a, 0), (a, 1), (b, 0), (b, 1)))
 
     up[2], down[3] = along_seq(up[1], 1), along_seq(down[4], -1)
-    query, total, token = attend_first(valid, (upper, lower, up[1], down[4]), parts)
+    query, total, token = attend_first(valid, (upper, lower, up[1]), parts)
 
     up[2], down[3], token = together(up[2], down[3], token)
     up[3], down[2] = along_seq(up[2], 1), along_seq(down[3], -1)
-    total, token = attend_step(FULL_PLAN, (1, 2), valid, (up[2], down[3]), parts, query, total, token)
+    rows = (up[2], down[4], down[3])
+    total, token = attend_step(SECOND_PLAN, (1, 3, 2), valid, rows, parts, query, total, token)
 
     up[3], down[2], token = together(up[3], down[2], token)
     up[4], down[1] = along_seq(up[3], 1), along_seq(down[2], -1)

time: 143 us -> 142 us (level)
  transfers between devices with their start and end apart: 18 -> 18, of which waited for: 6 -> 6; matrix products, arithmetic and copies ran while one was open for 4% -> 4% of each run, Pallas kernels for 35% -> 36%
where the time goes in v5:
time: 142 us
  Pallas kernels  66.9 us (47%)
  waiting for transfers between devices  38.7 us (27%)
  starting transfers between devices  27.5 us (19%)
  local copies, waits for them, and re-layouts  6.24 us (4%)
    ppermute x9, waiting for transfers between devices, along_seq(): lax.ppermute(block, 'seq', [(i, (i + distance) % count) for i in range(co...  33 us
    pallas_call x2, Pallas kernels, attend_step(): pl.pallas_call(functools.partial(step_kernel, plan, places), grid=(width...  26.5 us
    pallas_call x1, Pallas kernels, attend_first(): pl.pallas_call(first_kernel, grid=(width // QUAD,), in_specs=[SMEM_WHOLE]...  20.9 us
    ppermute x9, starting transfers between devices, along_seq(): lax.ppermute(block, 'seq', [(i, (i + distance) % count) for i in range(co...  19.8 us
    pallas_call x1, Pallas kernels, attend_last(): pl.pallas_call(functools.partial(last_kernel, plan, places), grid=(width...  13.7 us
    ppermute x9, starting transfers between devices, over_fsdp(): lax.ppermute(block, 'fsdp', [(i, (i // 2 * 2 + 2 * dy) % count + (i + oth...  7.7 us
    ppermute x9, waiting for transfers between devices, over_fsdp(): lax.ppermute(block, 'fsdp', [(i, (i // 2 * 2 + 2 * dy) % count + (i + oth...  5.62 us
    pallas_call x1, Pallas kernels, prep(): pl.pallas_call(prep_kernel, grid=(1,), in_specs=[SMEM_WHOLE] + [whole(x.s...  3.47 us
  transfers between devices with their start and end apart: 18, of which 6 were waited for; matrix products, arithmetic and copies ran while one was open for 4% of the time, Pallas kernels for 36%

profile of v5, /device:TPU:24, one launch (start us, length us, event | category | flops | bytes accessed | tf_op | source)
XLA Modules:
  0.0 141.6 jit_solution(7810240388840935196)
XLA Ops:
  0.6 0.9 slice_bitcast_fusion
  1.5 2.3 %stack.69.refs_4_.refs_12_.refs_20_.refs_3_.refs_11_ = bf16[512,1024]{1,0:T(8,128)(2,1)} custom-call(bf16[128,1024]{1,0:T(8,128)(2,1)} %refs_0_, bf16[128,1024]{1,0:T(8,128)(2,1)} %refs_1_, bf16[128,1024]{1,0:T(8,128)(2,1)} %refs_2_, bf16[128,1024]{1,0:T(8,128)(2,1)} %refs_3_), custom_call_target="tpu_custom_call" | custom-call | flops 1 | bytes 1 | tf_op jit(solution)/shard_map/stack/pallas_call | solution.py:85
  4.6 2.5 %collective-permute-start.1 = (bf16[512,1024]{1,0:T(8,128)(2,1)}, bf16[512,1024]{1,0:T(8,128)(2,1)}, u32[]{:S(2)}, u32[]{:S(2)}) collective-permute-start(bf16[512,1024]{1,0:T(8,128)(2,1)} %stack.69.refs_4_.refs_12_.refs_20_.refs_3_.refs_11_), channel_id=1, source_target_pairs={{0,2},{1,3},{2,4},{3,5},{4,6},{5,7},{6,0},{7,1},{8,10},{9,11},{10,... | collective-permute-start | bytes 3145736 | tf_op jit(solution)/shard_map/ppermute | solution.py:321
  7.1 1.9 %collective-permute-start = (bf16[64,1024]{1,0:T(8,128)(2,1)S(1)}, bf16[64,1024]{1,0:T(8,128)(2,1)S(1)}, u32[]{:S(2)}, u32[]{:S(2)}) collective-permute-start(bf16[64,1024]{1,0:T(8,128)(2,1)S(1)} %slice_bitcast_fusion), channel_id=1, source_target_pairs={{0,8},{8,16},{16,24},{24,32},{32,40},{40,48},{48,56},{56,64},{64,7... | collective-permute-start | bytes 393224 | tf_op jit(solution)/shard_map/ppermute | solution.py:316
  9.0 0.8 concatenate.9
  11.9 6.2 %collective-permute-done.carried_ref = bf16[64,1024]{1,0:T(8,128)(2,1)S(1)} collective-permute-done((bf16[64,1024]{1,0:T(8,128)(2,1)S(1)}, bf16[64,1024]{1,0:T(8,128)(2,1)S(1)}, u32[]{:S(2)}, u32[]{:S(2)}) %collective-permute-start) | collective-permute-done | bytes 131104 | tf_op jit(solution)/shard_map/ppermute | solution.py:316
  18.8 3.5 %prep.1 = (bf16[512,1024]{1,0:T(8,128)(2,1)}, bf16[384,1024]{1,0:T(8,128)(2,1)}, bf16[128,1024]{1,0:T(8,128)(2,1)}) custom-call(s32[8]{0:T(128)} %stack.60.order_ref.refs_1_, s32[2,256]{1,0:T(2,128)} %pad_add_fusion.win_ref, bf16[512,1024]{1,0:T(8,128)(2,1)} %bitcast.22, bf16[64,1024]{1,0:T(8,128)(2,1)} %copy-done.5, bf16[128,1024]{1,0:T(8,128)(2,1)} %bitcast.23), custom_call_target="tpu_custom_call" | custom-call | flops 1 | bytes 1 | tf_op jit(solution)/shard_map/prep/pallas_call | solution.py:62
  22.2 2.4 %collective-permute-start.6 = (bf16[128,1024]{1,0:T(8,128)(2,1)}, bf16[128,1024]{1,0:T(8,128)(2,1)S(1)}, u32[]{:S(2)}, u32[]{:S(2)}) collective-permute-start(bf16[128,1024]{1,0:T(8,128)(2,1)} %get-tuple-element.38.refs_2_), channel_id=1, source_target_pairs={{0,32},{8,40},{16,48},{24,56},{32,64},{40,72},{48,80},{56,88},{64,... | collective-permute-start | bytes 786440 | tf_op jit(solution)/shard_map/ppermute | solution.py:316
  24.7 5.6 %collective-permute-done.3.refs_8_.refs_16_.refs_24_.refs_7_.refs_15_ = bf16[512,1024]{1,0:T(8,128)(2,1)} collective-permute-done((bf16[512,1024]{1,0:T(8,128)(2,1)}, bf16[512,1024]{1,0:T(8,128)(2,1)}, u32[]{:S(2)}, u32[]{:S(2)}) %collective-permute-start.3) | collective-permute-done | bytes 1048608 | tf_op jit(solution)/shard_map/ppermute | solution.py:321
  30.3 1.1 slice.39
  31.5 1.1 slice.38
  32.5 3.3 %collective-permute-start.2 = (bf16[256,1024]{1,0:T(8,128)(2,1)S(1)}, bf16[256,1024]{1,0:T(8,128)(2,1)S(1)}, u32[]{:S(2)}, u32[]{:S(2)}) collective-permute-start(bf16[256,1024]{1,0:T(8,128)(2,1)S(1)} %slice.38), channel_id=1, source_target_pairs={{0,2},{1,3},{2,4},{3,5},{4,6},{5,7},{6,0},{7,1},{8,10},{9,11},{10,... | collective-permute-start | bytes 1572872 | tf_op jit(solution)/shard_map/ppermute | solution.py:321
  35.8 15.4 %collective-permute-done.6.refs_2_ = bf16[128,1024]{1,0:T(8,128)(2,1)S(1)} collective-permute-done((bf16[128,1024]{1,0:T(8,128)(2,1)}, bf16[128,1024]{1,0:T(8,128)(2,1)S(1)}, u32[]{:S(2)}, u32[]{:S(2)}) %collective-permute-start.6) | collective-permute-done | bytes 262176 | tf_op jit(solution)/shard_map/ppermute | solution.py:316
  51.3 3.7 %collective-permute-done.5.refs_3_ = bf16[384,1024]{1,0:T(8,128)(2,1)} collective-permute-done((bf16[384,1024]{1,0:T(8,128)(2,1)}, bf16[384,1024]{1,0:T(8,128)(2,1)}, u32[]{:S(2)}, u32[]{:S(2)}) %collective-permute-start.5) | collective-permute-done | bytes 786464 | tf_op jit(solution)/shard_map/ppermute | solution.py:316
  56.3 4.6 %collective-permute-start.8 = (bf16[128,1024]{1,0:T(8,128)(2,1)S(1)}, bf16[128,1024]{1,0:T(8,128)(2,1)}, u32[]{:S(2)}, u32[]{:S(2)}) collective-permute-start(bf16[128,1024]{1,0:T(8,128)(2,1)S(1)} %collective-permute-done.6.refs_2_), channel_id=1, source_target_pairs={{0,248},{8,0},{16,8},{24,16},{32,24},{40,32},{48,40},{56,48},{64,5... | collective-permute-start | bytes 786440 | tf_op jit(solution)/shard_map/ppermute | solution.py:316
  60.9 0.8 copy-done.2
  61.7 20.9 %first.1 = (bf16[512,1024]{1,0:T(8,128)(2,1)}, f32[8,512,256]{2,1,0:T(8,128)}, f32[8,128]{1,0:T(8,128)}) custom-call(s32[4]{0:T(128)} %add_convert_fusion.refs_0_, bf16[384,1024]{1,0:T(8,128)(2,1)} %get-tuple-element.37.refs_1_, bf16[128,1024]{1,0:T(8,128)(2,1)} %get-tuple-element.38.refs_2_, bf16[384,1024]{1,0:T(8,128)(2,1)} %collective-permute-done.5.refs_3_, ...), custom_call_target="tpu_custom_call" | custom-call | flops 1 | bytes 1 | tf_op jit(solution)/shard_map/first/pallas_call | solution.py:254
  82.8 5.3 %collective-permute-start.15 = (bf16[128,1024]{1,0:T(8,128)(2,1)}, bf16[128,1024]{1,0:T(8,128)(2,1)}, u32[]{:S(2)}, u32[]{:S(2)}) collective-permute-start(bf16[128,1024]{1,0:T(8,128)(2,1)} %collective-permute-done.8.refs_3_), channel_id=1, source_target_pairs={{0,248},{8,0},{16,8},{24,16},{32,24},{40,32},{48,40},{56,48},{64,5... | collective-permute-start | bytes 786440 | tf_op jit(solution)/shard_map/ppermute | solution.py:316
  88.1 13.8 %step.2 = (f32[8,512,256]{2,1,0:T(8,128)}, f32[8,128]{1,0:T(8,128)}) custom-call(s32[4]{0:T(128)} %add_convert_fusion.refs_0_, bf16[384,1024]{1,0:T(8,128)(2,1)} %collective-permute-done.7.refs_1_, bf16[128,1024]{1,0:T(8,128)(2,1)} %copy-done.4, bf16[128,1024]{1,0:T(8,128)(2,1)} %collective-permute-done.8.refs_3_, ...), custom_call_target="tpu_custom_call" | custom-call | flops 1 | bytes 1 | tf_op jit(solution)/shard_map/step/pallas_call | solution.py:276
  101.9 3.8 %collective-permute-done.14.refs_1_ = bf16[384,1024]{1,0:T(8,128)(2,1)S(1)} collective-permute-done((bf16[384,1024]{1,0:T(8,128)(2,1)}, bf16[384,1024]{1,0:T(8,128)(2,1)S(1)}, u32[]{:S(2)}, u32[]{:S(2)}) %collective-permute-start.14) | collective-permute-done | bytes 786464 | tf_op jit(solution)/shard_map/ppermute | solution.py:316
  105.7 5.3 %collective-permute-start.17 = (bf16[128,1024]{1,0:T(8,128)(2,1)}, bf16[128,1024]{1,0:T(8,128)(2,1)}, u32[]{:S(2)}, u32[]{:S(2)}) collective-permute-start(bf16[128,1024]{1,0:T(8,128)(2,1)} %collective-permute-done.15.refs_2_), channel_id=1, source_target_pairs={{0,248},{8,0},{16,8},{24,16},{32,24},{40,32},{48,40},{56,48},{64,5... | collective-permute-start | bytes 786440 | tf_op jit(solution)/shard_map/ppermute | solution.py:316
  111.1 12.8 %step.3 = (f32[8,512,256]{2,1,0:T(8,128)}, f32[8,128]{1,0:T(8,128)}) custom-call(s32[4]{0:T(128)} %add_convert_fusion.refs_0_, bf16[384,1024]{1,0:T(8,128)(2,1)} %copy-done.3, bf16[128,1024]{1,0:T(8,128)(2,1)} %collective-permute-done.15.refs_2_, bf16[512,1024]{1,0:T(8,128)(2,1)} %stack.69.refs_4_.refs_12_.refs_20_.refs_3_.refs_11_, ...), custom_call_target="tpu_custom_call" | custom-call | flops 1 | bytes 1 | tf_op jit(solution)/shard_map/step/pallas_call | solution.py:276
  123.9 3.9 %collective-permute-done.16.refs_2_ = bf16[384,1024]{1,0:T(8,128)(2,1)} collective-permute-done((bf16[384,1024]{1,0:T(8,128)(2,1)S(1)}, bf16[384,1024]{1,0:T(8,128)(2,1)}, u32[]{:S(2)}, u32[]{:S(2)}) %collective-permute-start.16) | collective-permute-done | bytes 786464 | tf_op jit(solution)/shard_map/ppermute | solution.py:316
  127.7 13.7 %last.1 = bf16[512,1024]{1,0:T(8,128)(2,1)} custom-call(s32[4]{0:T(128)} %add_convert_fusion.refs_0_, s32[8]{0:T(128)} %stack.60.order_ref.refs_1_, bf16[384,1024]{1,0:T(8,128)(2,1)} %collective-permute-done.16.refs_2_, bf16[128,1024]{1,0:T(8,128)(2,1)} %collective-permute-done.17.refs_3_, ...), custom_call_target="tpu_custom_call" | custom-call | flops 1 | bytes 1 | tf_op jit(solution)/shard_map/last/pallas_call | solution.py:294
  (43 shorter events, 5.0 us)
Async XLA Ops:
  3.9 26.4 %collective-permute-start.3 = (bf16[512,1024]{1,0:T(8,128)(2,1)}, bf16[512,1024]{1,0:T(8,128)(2,1)}, u32[]{:S(2)}, u32[]{:S(2)}) collective-permute-start(bf16[512,1024]{1,0:T(8,128)(2,1)} %stack.69.refs_4_.refs_12_.refs_20_.refs_3_.refs_11_), channel_id=1, source_target_pairs={{0,6},{1,7},{2,0},{3,1},{4,2},{5,3},{6,4},{7,5},{8,14},{9,15},{10,... | collective-permute-start | bytes 3145736 | tf_op jit(solution)/shard_map/ppermute | solution.py:321
  4.6 26.9 %collective-permute-start.1 = (bf16[512,1024]{1,0:T(8,128)(2,1)}, bf16[512,1024]{1,0:T(8,128)(2,1)}, u32[]{:S(2)}, u32[]{:S(2)}) collective-permute-start(bf16[512,1024]{1,0:T(8,128)(2,1)} %stack.69.refs_4_.refs_12_.refs_20_.refs_3_.refs_11_), channel_id=1, source_target_pairs={{0,2},{1,3},{2,4},{3,5},{4,6},{5,7},{6,0},{7,1},{8,10},{9,11},{10,... | collective-permute-start | bytes 3145736 | tf_op jit(solution)/shard_map/ppermute | solution.py:321
  7.1 11.0 %collective-permute-start = (bf16[64,1024]{1,0:T(8,128)(2,1)S(1)}, bf16[64,1024]{1,0:T(8,128)(2,1)S(1)}, u32[]{:S(2)}, u32[]{:S(2)}) collective-permute-start(bf16[64,1024]{1,0:T(8,128)(2,1)S(1)} %slice_bitcast_fusion), channel_id=1, source_target_pairs={{0,8},{8,16},{16,24},{24,32},{32,40},{40,48},{48,56},{56,64},{64,7... | collective-permute-start | bytes 393224 | tf_op jit(solution)/shard_map/ppermute | solution.py:316
  18.1 0.7 copy-start.5
  22.2 32.7 %collective-permute-start.5 = (bf16[384,1024]{1,0:T(8,128)(2,1)}, bf16[384,1024]{1,0:T(8,128)(2,1)}, u32[]{:S(2)}, u32[]{:S(2)}) collective-permute-start(bf16[384,1024]{1,0:T(8,128)(2,1)} %get-tuple-element.37.refs_1_), channel_id=1, source_target_pairs={{0,8},{8,16},{16,24},{24,32},{32,40},{40,48},{48,56},{56,64},{64,7... | collective-permute-start | bytes 2359304 | tf_op jit(solution)/shard_map/ppermute | solution.py:316
  22.2 33.6 %collective-permute-start.9 = (bf16[512,1024]{1,0:T(8,128)(2,1)}, bf16[512,1024]{1,0:T(8,128)(2,1)}, u32[]{:S(2)}, u32[]{:S(2)}) collective-permute-start(bf16[512,1024]{1,0:T(8,128)(2,1)} %stack.69.refs_4_.refs_12_.refs_20_.refs_3_.refs_11_), channel_id=1, source_target_pairs={{0,1},{1,0},{2,3},{3,2},{4,5},{5,4},{6,7},{7,6},{8,9},{9,8},{10,11... | collective-permute-start | bytes 3145736 | tf_op jit(solution)/shard_map/ppermute | solution.py:321
  22.2 29.0 %collective-permute-start.6 = (bf16[128,1024]{1,0:T(8,128)(2,1)}, bf16[128,1024]{1,0:T(8,128)(2,1)S(1)}, u32[]{:S(2)}, u32[]{:S(2)}) collective-permute-start(bf16[128,1024]{1,0:T(8,128)(2,1)} %get-tuple-element.38.refs_2_), channel_id=1, source_target_pairs={{0,32},{8,40},{16,48},{24,56},{32,64},{40,72},{48,80},{56,88},{64,... | collective-permute-start | bytes 786440 | tf_op jit(solution)/shard_map/ppermute | solution.py:316
  31.4 23.6 %collective-permute-start.4 = (bf16[256,1024]{1,0:T(8,128)(2,1)S(1)}, bf16[256,1024]{1,0:T(8,128)(2,1)S(1)}, u32[]{:S(2)}, u32[]{:S(2)}) collective-permute-start(bf16[256,1024]{1,0:T(8,128)(2,1)S(1)} %slice.39), channel_id=1, source_target_pairs={{0,6},{1,7},{2,0},{3,1},{4,2},{5,3},{6,4},{7,5},{8,14},{9,15},{10,... | collective-permute-start | bytes 1572872 | tf_op jit(solution)/shard_map/ppermute | solution.py:321
  32.5 22.4 %collective-permute-start.2 = (bf16[256,1024]{1,0:T(8,128)(2,1)S(1)}, bf16[256,1024]{1,0:T(8,128)(2,1)S(1)}, u32[]{:S(2)}, u32[]{:S(2)}) collective-permute-start(bf16[256,1024]{1,0:T(8,128)(2,1)S(1)} %slice.38), channel_id=1, source_target_pairs={{0,2},{1,3},{2,4},{3,5},{4,6},{5,7},{6,0},{7,1},{8,10},{9,11},{10,... | collective-permute-start | bytes 1572872 | tf_op jit(solution)/shard_map/ppermute | solution.py:321
  51.2 31.4 %copy-start.4 = (bf16[128,1024]{1,0:T(8,128)(2,1)}, bf16[128,1024]{1,0:T(8,128)(2,1)S(1)}, u32[]{:S(2)}) copy-start(bf16[128,1024]{1,0:T(8,128)(2,1)S(1)} %collective-permute-done.6.refs_2_) | copy-start | bytes 786436
  51.2 5.1 %collective-permute-start.11 = (bf16[512,1024]{1,0:T(8,128)(2,1)}, bf16[512,1024]{1,0:T(8,128)(2,1)}, u32[]{:S(2)}, u32[]{:S(2)}) collective-permute-start(bf16[512,1024]{1,0:T(8,128)(2,1)} %collective-permute-done.3.refs_8_.refs_16_.refs_24_.refs_7_.refs_15_), channel_id=1, source_target_pairs={{0,1},{1,0},{2,3},{3,2},{4,5},{5,4},{6,7},{7,6},{8,9},{9,8},{10,11... | collective-permute-start | bytes 3145736 | tf_op jit(solution)/shard_map/ppermute | solution.py:321
  54.9 6.0 %collective-permute-start.10 = (bf16[512,1024]{1,0:T(8,128)(2,1)}, bf16[512,1024]{1,0:T(8,128)(2,1)}, u32[]{:S(2)}, u32[]{:S(2)}) collective-permute-start(bf16[512,1024]{1,0:T(8,128)(2,1)} %collective-permute-done.1.refs_6_.refs_14_.refs_22_.refs_5_.refs_13_), channel_id=1, source_target_pairs={{0,1},{1,0},{2,3},{3,2},{4,5},{5,4},{6,7},{7,6},{8,9},{9,8},{10,11... | collective-permute-start | bytes 3145736 | tf_op jit(solution)/shard_map/ppermute | solution.py:321
  55.0 6.8 %copy-start = (bf16[256,1024]{1,0:T(8,128)(2,1)}, bf16[256,1024]{1,0:T(8,128)(2,1)S(1)}, u32[]{:S(2)}) copy-start(bf16[256,1024]{1,0:T(8,128)(2,1)S(1)} %collective-permute-done.4.refs_26_.refs_18_.refs_17_) | copy-start | bytes 1572868
  55.0 0.8 copy-start.1
  55.0 27.7 %collective-permute-start.7 = (bf16[384,1024]{1,0:T(8,128)(2,1)}, bf16[384,1024]{1,0:T(8,128)(2,1)}, u32[]{:S(2)}, u32[]{:S(2)}) collective-permute-start(bf16[384,1024]{1,0:T(8,128)(2,1)} %collective-permute-done.5.refs_3_), channel_id=1, source_target_pairs={{0,8},{8,16},{16,24},{24,32},{32,40},{40,48},{48,56},{56,64},{64,7... | collective-permute-start | bytes 2359304 | tf_op jit(solution)/shard_map/ppermute | solution.py:316
  55.1 5.9 %collective-permute-start.12 = (bf16[256,1024]{1,0:T(8,128)(2,1)S(1)}, bf16[256,1024]{1,0:T(8,128)(2,1)S(1)}, u32[]{:S(2)}, u32[]{:S(2)}) collective-permute-start(bf16[256,1024]{1,0:T(8,128)(2,1)S(1)} %collective-permute-done.2.refs_10_.refs_18_.refs_9_), channel_id=1, source_target_pairs={{0,1},{1,0},{2,3},{3,2},{4,5},{5,4},{6,7},{7,6},{8,9},{9,8},{10,11... | collective-permute-start | bytes 1572872 | tf_op jit(solution)/shard_map/ppermute | solution.py:321
  55.8 5.9 %collective-permute-start.13 = (bf16[256,1024]{1,0:T(8,128)(2,1)S(1)}, bf16[256,1024]{1,0:T(8,128)(2,1)}, u32[]{:S(2)}, u32[]{:S(2)}) collective-permute-start(bf16[256,1024]{1,0:T(8,128)(2,1)S(1)} %collective-permute-done.4.refs_26_.refs_18_.refs_17_), channel_id=1, source_target_pairs={{0,1},{1,0},{2,3},{3,2},{4,5},{5,4},{6,7},{7,6},{8,9},{9,8},{10,11... | collective-permute-start | bytes 1572872 | tf_op jit(solution)/shard_map/ppermute | solution.py:321
  56.3 26.4 %collective-permute-start.8 = (bf16[128,1024]{1,0:T(8,128)(2,1)S(1)}, bf16[128,1024]{1,0:T(8,128)(2,1)}, u32[]{:S(2)}, u32[]{:S(2)}) collective-permute-start(bf16[128,1024]{1,0:T(8,128)(2,1)S(1)} %collective-permute-done.6.refs_2_), channel_id=1, source_target_pairs={{0,248},{8,0},{16,8},{24,16},{32,24},{40,32},{48,40},{56,48},{64,5... | collective-permute-start | bytes 786440 | tf_op jit(solution)/shard_map/ppermute | solution.py:316
  60.9 0.8 copy-start.2
  82.7 23.0 %collective-permute-start.14 = (bf16[384,1024]{1,0:T(8,128)(2,1)}, bf16[384,1024]{1,0:T(8,128)(2,1)S(1)}, u32[]{:S(2)}, u32[]{:S(2)}) collective-permute-start(bf16[384,1024]{1,0:T(8,128)(2,1)} %collective-permute-done.7.refs_1_), channel_id=1, source_target_pairs={{0,8},{8,16},{16,24},{24,32},{32,40},{40,48},{48,56},{56,64},{64,7... | collective-permute-start | bytes 2359304 | tf_op jit(solution)/shard_map/ppermute | solution.py:316
  82.8 19.1 %collective-permute-start.15 = (bf16[128,1024]{1,0:T(8,128)(2,1)}, bf16[128,1024]{1,0:T(8,128)(2,1)}, u32[]{:S(2)}, u32[]{:S(2)}) collective-permute-start(bf16[128,1024]{1,0:T(8,128)(2,1)} %collective-permute-done.8.refs_3_), channel_id=1, source_target_pairs={{0,248},{8,0},{16,8},{24,16},{32,24},{40,32},{48,40},{56,48},{64,5... | collective-permute-start | bytes 786440 | tf_op jit(solution)/shard_map/ppermute | solution.py:316
  105.7 5.4 %copy-start.3 = (bf16[384,1024]{1,0:T(8,128)(2,1)}, bf16[384,1024]{1,0:T(8,128)(2,1)S(1)}, u32[]{:S(2)}) copy-start(bf16[384,1024]{1,0:T(8,128)(2,1)S(1)} %collective-permute-done.14.refs_1_) | copy-start | bytes 2359300
  105.7 22.0 %collective-permute-start.16 = (bf16[384,1024]{1,0:T(8,128)(2,1)S(1)}, bf16[384,1024]{1,0:T(8,128)(2,1)}, u32[]{:S(2)}, u32[]{:S(2)}) collective-permute-start(bf16[384,1024]{1,0:T(8,128)(2,1)S(1)} %collective-permute-done.14.refs_1_), channel_id=1, source_target_pairs={{0,8},{8,16},{16,24},{24,32},{32,40},{40,48},{48,56},{56,64},{64,7... | collective-permute-start | bytes 2359304 | tf_op jit(solution)/shard_map/ppermute | solution.py:316
  105.7 18.1 %collective-permute-start.17 = (bf16[128,1024]{1,0:T(8,128)(2,1)}, bf16[128,1024]{1,0:T(8,128)(2,1)}, u32[]{:S(2)}, u32[]{:S(2)}) collective-permute-start(bf16[128,1024]{1,0:T(8,128)(2,1)} %collective-permute-done.15.refs_2_), channel_id=1, source_target_pairs={{0,248},{8,0},{16,8},{24,16},{32,24},{40,32},{48,40},{56,48},{64,5... | collective-permute-start | bytes 786440 | tf_op jit(solution)/shard_map/ppermute | solution.py:316
